TPU v7x, 32 devices: a whole 2x2x4 slice. The times are simulated.
32 devices in a mesh: row: 16 (over z, y, x), col: 2 (over core).
Axes of the slice: x: 2, y: 2, z: 4, core: 2. Of those that a mesh axis runs over, the one named last changes fastest.
Arguments:
- orbitals: bfloat16 [4096, 2, 256], P(('row', 'col')), may hold values from -6 to 6
- kernel: bfloat16 [4096, 4096], P('row', 'col'), may hold values from -0.005859375 to 0.005859375
- basis: bfloat16 [4096, 2048], P('row'), may hold values from -0.09375 to 0.09375
Outputs:
- exchange: float32 [2048, 2, 256], P('row')
All inputs are finite; a program needn't handle non-finite values.
Results may differ from a plain program's by a relative error of at most 0.0041.
Values may be sent and summed in bfloat16 or wider, within the bound.
No kernel may reach another device: no remote copies, remote signals or barrier semaphores. Data moves between devices by JAX's collectives and lax.ppermute only.
A program may use at most 64 MiB of HBM per device.

v0:
```python
import jax
import jax.numpy as jnp
from jax import lax
from jax.sharding import PartitionSpec as P


def body(orbitals, kernel, basis):
    row_orbitals = lax.all_gather(orbitals, "col", axis=0, tiled=True)
    point_rows = row_orbitals.shape[0]
    occupied = orbitals.shape[2]
    column_orbitals = lax.all_gather(orbitals, "row", axis=0, tiled=True)
    density = jnp.einsum(
        "psi,qsi->spq", row_orbitals, column_orbitals, preferred_element_type=jnp.float32
    )
    weighted = (density * kernel[None].astype(jnp.float32)).astype(jnp.bfloat16)
    applied = jnp.einsum(
        "spq,qsi->psi", weighted, column_orbitals, preferred_element_type=jnp.float32
    )
    out_rows = basis.shape[1] // lax.axis_size("row")
    summed = lax.psum(applied, "col").astype(jnp.bfloat16)
    flattened = summed.reshape(point_rows, -1)
    result = lax.psum_scatter(
        lax.dot_general(
            basis, flattened, (((0,), (0,)), ((), ())), preferred_element_type=jnp.float32
        ),
        "row",
        scatter_dimension=0,
        tiled=True,
    )
    return result.reshape(out_rows, 2, occupied)


def solution(mesh):
    return jax.shard_map(
        body,
        mesh=mesh,
        in_specs=(P(("row", "col"), None, None), P("row", "col"), P("row", None)),
        out_specs=P("row", None, None),
        check_vma=False,
    )
```

profile of v0, /device:TPU:0, one launch (start us, length us, event | category | flops | bytes accessed | tf_op | source)
XLA Modules:
  0.0 188.7 jit_solution(7788071884037564255)
XLA Ops:
  6.5 0.0 copy-start
  6.5 0.0 copy-start.1
  6.5 0.0 all-gather.2.cloned.1.call-start
  6.5 1.7 copy.9
  8.2 0.0 all-gather.2.cloned.1.call-update
  8.2 0.0 reduce-scatter.2.cloned.1.call-start
  8.3 1.5 convert_element_type.10
  9.8 0.0 copy-done.1
  9.8 2.1 %all_gather.6 = bf16[256,2,256]{2,1,0:T(2,128)(2,1)S(1)} all-gather(bf16[128,2,256]{2,1,0:T(2,128)(2,1)S(1)} %copy-done.1), channel_id=1, replica_groups=mesh['row'=16,'col'=2] {'col'}, dimensions={0}, use_global_device_ids=true | all-gather | bytes 393216 | tf_op jit(solution)/shard_map/all_gather | solution.py:8
  11.8 61.7 %all-gather.2.cloned.1.call-done = bf16[2048,2,256]{2,0,1:T(8,128)(2,1)} async-done(((bf16[128,2,256]{2,0,1:T(8,128)(2,1)}), bf16[2048,2,256]{2,0,1:T(8,128)(2,1)}) %all-gather.2.cloned.1.call-update) | async-done | bytes 2097168 | tf_op jit(solution)/shard_map/all_gather | solution.py:11
  73.5 4.3 %fusion.1 = f32[256,2,256]{2,0,1:T(8,128)} fusion(bf16[2048,2,256]{2,0,1:T(8,128)(2,1)} %all-gather.2.cloned.1.call-done, f32[256,2048]{1,0:T(8,128)S(1)} %convert_element_type.10, bf16[256,2,256]{2,1,0:T(2,128)(2,1)S(1)} %all_gather.6), kind=kOutput, calls=%fused_computation.3 | convolution fusion | flops 1075838976 | bytes 4980736 | tf_op jit(solution)/shard_map/spq,qsi->psi/dot_general | solution.py:16
  77.8 5.6 %all-reduce.1 = bf16[256,2,256]{2,0,1:T(8,128)(2,1)S(1)} all-reduce(f32[256,2,256]{2,0,1:T(8,128)} %fusion.1), channel_id=1, replica_groups=mesh['row'=16,'col'=2] {'col'}, use_global_device_ids=true, to_apply=%region_0.0 | all-reduce | flops 131072 | bytes 786432 | tf_op jit(solution)/shard_map/psum | solution.py:20
  83.4 0.1 copy.11
  83.6 0.0 copy-done
  83.6 2.6 %convolution_bitcast_fusion = f32[2048,512]{0,1:T(8,128)} fusion(bf16[256,512]{0,1:T(8,128)(2,1)S(1)} %bitcast.10, bf16[256,2048]{1,0:T(8,128)(2,1)S(1)} %copy-done), kind=kOutput, calls=%fused_computation.1 | convolution fusion | flops 536870912 | bytes 5505024 | tf_op jit(solution)/shard_map/dot_general | solution.py:23
  86.2 0.0 reduce-scatter.2.cloned.1.call-update
  86.2 93.9 %reduce-scatter.2.cloned.1.call-done = f32[128,512]{0,1:T(8,128)} async-done(((f32[2048,512]{0,1:T(8,128)}), f32[128,512]{0,1:T(8,128)}) %reduce-scatter.2.cloned.1.call-update) | async-done | bytes 262160 | tf_op jit(solution)/shard_map/reduce_scatter | solution.py:22
  180.1 1.8 copy.12
Async XLA Ops:
  6.5 77.0 %copy-start = (bf16[256,2048]{1,0:T(8,128)(2,1)S(1)}, bf16[256,2048]{1,0:T(8,128)(2,1)}, u32[]{:S(2)}) copy-start(bf16[256,2048]{1,0:T(8,128)(2,1)} %param.5) | copy-start | bytes 3145732
  6.5 3.2 %copy-start.1 = (bf16[128,2,256]{2,1,0:T(2,128)(2,1)S(1)}, bf16[128,2,256]{2,1,0:T(2,128)(2,1)}, u32[]{:S(2)}) copy-start(bf16[128,2,256]{2,1,0:T(2,128)(2,1)} %param.3) | copy-start | bytes 393220
  6.5 67.0 %all-gather.2.cloned.1.call-start = ((), (), s32[]{:S(2)}) async-start(), calls=%async_computation.1 | async-start | bytes 2228224 | tf_op jit(solution)/shard_map/all_gather | solution.py:11
  8.2 171.9 %reduce-scatter.2.cloned.1.call-start = ((), (), s32[]{:S(2)}) async-start(), calls=%async_computation.2 | async-start | bytes 4456448 | tf_op jit(solution)/shard_map/reduce_scatter | solution.py:22
Sparse Core Ops, SparseCore 0:
  10.1 63.3 all-gather.1
  86.4 93.7 reduce-scatter.1
where the time goes:
time: 189 us
  waiting for transfers between devices  156 us (83%)
  between operations  13.4 us (7%)
  blocking collectives  7.67 us (4%)
  matrix products  6.95 us (4%)
  local copies, waits for them, and re-layouts  3.6 us (2%)
    reduce_scatter x1, waiting for transfers between devices, body(): lax.psum_scatter(lax.dot_general(basis, flattened, (((0,), (0,)), ((), ()...  93.9 us
    all_gather x1, waiting for transfers between devices, body(): column_orbitals = lax.all_gather(orbitals, 'row', axis=0, tiled=True)  61.7 us
    psum x1, blocking collectives, body(): summed = lax.psum(applied, 'col').astype(jnp.bfloat16)  5.58 us
    dot_general x1, matrix products, body(): jnp.einsum('spq,qsi->psi', weighted, column_orbitals, preferred_element_t...  4.3 us
  transfers between devices with their start and end apart: 2, of which 2 were waited for; matrix products, arithmetic and copies ran while one was open for 1% of the time, Pallas kernels for 0%

commit v1 on v0

v1 whole, which is shorter than its diff:
```python
import functools

import jax
import jax.numpy as jnp
from jax import lax
from jax.experimental import pallas as pl
from jax.experimental.pallas import tpu as pltpu
from jax.sharding import PartitionSpec as P

F32 = jnp.float32
BF16 = jnp.bfloat16
VMEM = pl.BlockSpec(memory_space=pltpu.VMEM)
SMEM = pl.BlockSpec(memory_space=pltpu.SMEM)
LIMIT = 40 * 1024 * 1024


def general_body(orbitals, kernel, basis):
    row_orbitals = lax.all_gather(orbitals, "col", axis=0, tiled=True)
    point_rows = row_orbitals.shape[0]
    occupied = orbitals.shape[2]
    column_orbitals = lax.all_gather(orbitals, "row", axis=0, tiled=True)
    density = jnp.einsum(
        "psi,qsi->spq", row_orbitals, column_orbitals, preferred_element_type=F32
    )
    weighted = (density * kernel[None].astype(F32)).astype(BF16)
    applied = jnp.einsum(
        "spq,qsi->psi", weighted, column_orbitals, preferred_element_type=F32
    )
    out_rows = basis.shape[1] // lax.axis_size("row")
    summed = lax.psum(applied, "col").astype(BF16)
    flattened = summed.reshape(point_rows, -1)
    result = lax.psum_scatter(
        lax.dot_general(basis, flattened, (((0,), (0,)), ((), ())), preferred_element_type=F32),
        "row",
        scatter_dimension=0,
        tiled=True,
    )
    return result.reshape(out_rows, 2, occupied)


def apply_kernel(n_parts, piece, accumulate, ids, rows, kernel_own, kernel_other, *refs):
    parts = refs[:n_parts]
    acc = refs[n_parts] if accumulate else None
    out = refs[-1]
    total = acc[...] if accumulate else None
    left = rows[...]
    block = 2 * piece
    index = 0
    for part in parts:
        for b in range(part.shape[0] // block):
            columns = part[b * block : (b + 1) * block, :]
            at = pl.ds(pl.multiple_of(ids[index] * piece, piece), piece)
            index += 1
            density = lax.dot_general(
                left, columns, (((1,), (1,)), ((), ())), preferred_element_type=F32
            )
            tile = jnp.concatenate([kernel_own[:, at], kernel_other[:, at]], axis=1)
            weighted = (density * tile.astype(F32)).astype(BF16)
            term = jnp.dot(weighted, columns, preferred_element_type=F32)
            total = term if total is None else total + term
    out[...] = total.astype(out.dtype)


def apply_blocks(ids, rows, kernel_own, kernel_other, parts, acc, dtype):
    args = [ids, rows, kernel_own, kernel_other, *parts]
    if acc is not None:
        args.append(acc)
    columns = sum(part.shape[0] for part in parts)
    n, i = rows.shape
    return pl.pallas_call(
        functools.partial(apply_kernel, len(parts), kernel_own.shape[1] // 16, acc is not None),
        out_shape=jax.ShapeDtypeStruct((n, i), dtype),
        in_specs=[SMEM] + [VMEM] * (len(args) - 1),
        out_specs=VMEM,
        compiler_params=pltpu.CompilerParams(vmem_limit_bytes=LIMIT),
        cost_estimate=pl.CostEstimate(
            flops=4 * n * i * columns, bytes_accessed=2 * columns * (n + i), transcendentals=0
        ),
    )(*args)


def project_kernel(width, ids, basis, applied, out):
    right = applied[...]
    for b in range(out.shape[0] // width):
        at = pl.ds(pl.multiple_of(ids[b] * width, width), width)
        out[b * width : (b + 1) * width, :] = lax.dot_general(
            basis[:, at], right, (((0,), (0,)), ((), ())), preferred_element_type=F32
        ).astype(out.dtype)


def project(ids, basis, applied, width, blocks, dtype):
    p, i = applied.shape
    return pl.pallas_call(
        functools.partial(project_kernel, width),
        out_shape=jax.ShapeDtypeStruct((blocks * width, i), dtype),
        in_specs=[SMEM, VMEM, VMEM],
        out_specs=VMEM,
        compiler_params=pltpu.CompilerParams(vmem_limit_bytes=LIMIT),
        cost_estimate=pl.CostEstimate(
            flops=2 * p * i * blocks * width, bytes_accessed=2 * blocks * width * (p + i), transcendentals=0
        ),
    )(ids, basis, applied)


def box_body(orbitals, kernel, basis):
    r = lax.axis_index("row")
    c = lax.axis_index("col")
    piece = orbitals.shape[0]

    def send(a, to):
        pairs = [(2 * q + k, 2 * to(q, k) + k) for q in range(16) for k in range(2)]
        return lax.ppermute(a, ("row", "col"), pairs)

    first = lambda a: send(a, lambda q, k: q ^ (1 + k))
    second = lambda a: send(a, lambda q, k: q ^ (2 - k))
    plane = lambda a, d: send(a, lambda q, k: (q + 4 * d) % 16)
    swap = lambda a: lax.ppermute(a, "col", [(0, 1), (1, 0)])
    join = lambda *a: jnp.concatenate(a, axis=0)

    own = lax.dynamic_index_in_dim(orbitals, c, 1, keepdims=False)
    other = swap(lax.dynamic_index_in_dim(orbitals, 1 - c, 1, keepdims=False))
    kernel_other = swap(kernel)
    block = join(own, other)
    rows = jnp.where(c == 0, block, join(other, own))

    near, far = 1 + c, 2 - c
    x0 = first(block)
    z1 = plane(block, 1)
    p0 = join(block, x0)
    y0 = second(p0)
    z2 = plane(z1, 1)
    zp = plane(join(p0, y0), -1)
    z12 = join(z1, z2)
    x12 = first(z12)
    y12 = second(join(z12, x12))

    up, down, twice = (r + 4) % 16, (r + 12) % 16, (r + 8) % 16
    ids = lambda *v: jnp.stack(v).astype(jnp.int32)
    acc = apply_blocks(
        ids(r, r ^ near, r ^ far, r ^ 3), rows, kernel, kernel_other, [block, x0, y0], None, F32
    )
    acc = apply_blocks(
        ids(up, up ^ near, up ^ far, up ^ 3, down, twice, down ^ near, twice ^ near),
        rows, kernel, kernel_other, [zp, z12, x12], acc, F32,
    )
    applied = apply_blocks(
        ids(down ^ far, twice ^ far, down ^ 3, twice ^ 3), rows, kernel, kernel_other, [y12], acc, BF16
    )

    width = basis.shape[1] // 16
    along = lambda base: [(base + 4 * k) % 16 for k in range(4)]
    send1 = project(ids(*along(r ^ far), *along(r ^ 3)), basis, applied, width, 8, BF16)
    keep1 = project(ids(*along(r), *along(r ^ near)), basis, applied, width, 8, F32)
    half = 4 * width
    got1 = second(send1)
    send2 = (keep1[half:] + got1[half:].astype(F32)).astype(BF16)
    keep2 = keep1[:half] + got1[:half].astype(F32)
    got2 = first(send2)
    sums = keep2 + got2.astype(F32)
    result = sums[:width]
    for k in (1, 2, 3):
        result = result + plane(sums[k * width : (k + 1) * width].astype(BF16), k).astype(F32)
    partner = swap(result)
    return jnp.where(
        c == 0, jnp.stack([result, partner], axis=1), jnp.stack([partner, result], axis=1)
    )


def solution(mesh):
    box = dict(mesh.shape) == {"row": 16, "col": 2}
    return jax.shard_map(
        box_body if box else general_body,
        mesh=mesh,
        in_specs=(P(("row", "col"), None, None), P("row", "col"), P("row", None)),
        out_specs=P("row", None, None),
        check_vma=False,
    )
```

time: 189 us -> 68.1 us (0.36)
  waiting for transfers between devices: 156 us -> 33.1 us
  starting transfers between devices: 0.04 us -> 23.4 us
  between operations: 13.4 us -> 0.13 us
  blocking collectives: 7.67 us -> 0 us
  matrix products: 6.95 us -> 0 us
  Pallas kernels: 0 us -> 6.7 us
    reduce_scatter x1 -> x0, waiting for transfers between devices: 93.9 us -> none  [body(): lax.psum_scatter(lax.dot_general(basis, flattened, (((0,), (0,)), ((), ()...]
    all_gather x1 -> x0, waiting for transfers between devices: 61.7 us -> none  [body(): column_orbitals = lax.all_gather(orbitals, 'row', axis=0, tiled=True)]
    ppermute x0 -> x15, waiting for transfers between devices: none -> 33.1 us  [the longest x12 30.8 us: send(): return lax.ppermute(a, ('row', 'col'), pairs)]
    ppermute x0 -> x15, starting transfers between devices: none -> 23.4 us  [the longest x12 22.8 us: send(): return lax.ppermute(a, ('row', 'col'), pairs)]
    dot_general x2 -> x0, matrix products: 6.95 us -> none  [the longest x1 4.3 us: body(): jnp.einsum('spq,qsi->psi', weighted, column_orbitals, preferred_element_t...]
    pallas_call x0 -> x5, Pallas kernels: none -> 6.7 us  [the longest x3 4.91 us: apply_blocks(): pl.pallas_call(functools.partial(apply_kernel, len(parts), kernel_own.sha...]
    psum x1 -> x0, blocking collectives: 5.58 us -> none  [body(): summed = lax.psum(applied, 'col').astype(jnp.bfloat16)]
    all_gather x1 -> x0, blocking collectives: 2.09 us -> none  [body(): row_orbitals = lax.all_gather(orbitals, 'col', axis=0, tiled=True)]
  transfers between devices with their start and end apart: 2 -> 15, of which waited for: 2 -> 11; matrix products, arithmetic and copies ran while one was open for 1% -> 3% of each run, Pallas kernels for 0% -> 6%
where the time goes in v1:
time: 68.1 us; the launch traced here: 67.9 us
  waiting for transfers between devices  33.1 us (49%)
  starting transfers between devices  23.4 us (34%)
  Pallas kernels  6.7 us (10%)
  local copies, waits for them, and re-layouts  2.55 us (4%)
  other arithmetic  2.11 us (3%)
    ppermute x12, waiting for transfers between devices, send(): return lax.ppermute(a, ('row', 'col'), pairs)  30.8 us
    ppermute x12, starting transfers between devices, send(): return lax.ppermute(a, ('row', 'col'), pairs)  22.8 us
    pallas_call x3, Pallas kernels, apply_blocks(): pl.pallas_call(functools.partial(apply_kernel, len(parts), kernel_own.sha...  4.91 us
    ppermute x3, waiting for transfers between devices, box_body(): swap = lambda a: lax.ppermute(a, 'col', [(0, 1), (1, 0)])  2.23 us
    pallas_call x2, Pallas kernels, project(): pl.pallas_call(functools.partial(project_kernel, width), out_shape=jax.Sh...  1.79 us
    concatenate x4, other arithmetic, box_body(): join = lambda *a: jnp.concatenate(a, axis=0)  1.73 us
  transfers between devices with their start and end apart: 15, of which 11 were waited for; matrix products, arithmetic and copies ran while one was open for 3% of the time, Pallas kernels for 6%

profile of v1, /device:TPU:0, one launch (start us, length us, event | category | flops | bytes accessed | tf_op | source)
XLA Modules:
  0.0 67.9 jit_solution(1349205457873294174)
XLA Ops:
  0.0 1.3 %constant_dynamic-slice_fusion = (bf16[128,1,256]{2,1,0:T(2,128)(2,1)S(1)}, bf16[128,1,256]{2,1,0:T(2,128)(2,1)S(1)}) fusion(bf16[128,2,256]{2,1,0:T(2,128)(2,1)} %param.3, s32[]{:T(128)S(6)} %select_n.107, s32[]{:T(128)S(6)} %select_n.106), kind=kLoop, calls=%fused_computation.19 | loop fusion | bytes 262152 | tf_op jit(solution)/shard_map/jit(dynamic_index_in_dim)/dynamic_slice | solution.py:121
  2.8 3.0 %collective-permute-start.2 = (bf16[256,256]{1,0:T(8,128)(2,1)S(1)}, bf16[256,256]{1,0:T(8,128)(2,1)S(1)}, u32[]{:S(2)}, u32[]{:S(2)}) collective-permute-start(bf16[256,256]{1,0:T(8,128)(2,1)S(1)} %get-tuple-element.10.refs_0_), channel_id=1, source_target_pairs={{0,8},{1,9},{2,10},{3,11},{4,12},{5,13},{6,14},{7,15},{8,16},{9,17... | collective-permute-start | bytes 393224 | tf_op jit(solution)/shard_map/ppermute | solution.py:112
  5.8 1.5 %collective-permute-start.6 = (bf16[256,256]{1,0:T(8,128)(2,1)S(1)}, bf16[256,256]{1,0:T(8,128)(2,1)S(1)}, u32[]{:S(2)}, u32[]{:S(2)}) collective-permute-start(bf16[256,256]{1,0:T(8,128)(2,1)S(1)} %get-tuple-element.10.refs_0_), channel_id=1, source_target_pairs={{0,2},{1,5},{2,0},{3,7},{4,6},{5,1},{6,4},{7,3},{8,10},{9,13},{10,... | collective-permute-start | bytes 393224 | tf_op jit(solution)/shard_map/ppermute | solution.py:112
  7.3 4.3 %collective-permute-done.2 = bf16[256,256]{1,0:T(8,128)(2,1)S(1)} collective-permute-done((bf16[256,256]{1,0:T(8,128)(2,1)S(1)}, bf16[256,256]{1,0:T(8,128)(2,1)S(1)}, u32[]{:S(2)}, u32[]{:S(2)}) %collective-permute-start.2) | collective-permute-done | bytes 131104 | tf_op jit(solution)/shard_map/ppermute | solution.py:112
  11.7 1.6 %collective-permute-start.7 = (bf16[512,256]{1,0:T(8,128)(2,1)S(1)}, bf16[512,256]{1,0:T(8,128)(2,1)S(1)}, u32[]{:S(2)}, u32[]{:S(2)}) collective-permute-start(bf16[512,256]{1,0:T(8,128)(2,1)S(1)} %pad_maximum_fusion.2), channel_id=1, source_target_pairs={{0,4},{1,3},{2,6},{3,1},{4,0},{5,7},{6,2},{7,5},{8,12},{9,11},{10,... | collective-permute-start | bytes 786440 | tf_op jit(solution)/shard_map/ppermute | solution.py:112
  13.3 5.2 %collective-permute-done.3 = bf16[256,256]{1,0:T(8,128)(2,1)S(1)} collective-permute-done((bf16[256,256]{1,0:T(8,128)(2,1)S(1)}, bf16[256,256]{1,0:T(8,128)(2,1)S(1)}, u32[]{:S(2)}, u32[]{:S(2)}) %collective-permute-start.3) | collective-permute-done | bytes 131104 | tf_op jit(solution)/shard_map/ppermute | solution.py:112
  18.5 1.5 %collective-permute-start.4 = (bf16[512,256]{1,0:T(8,128)(2,1)S(1)}, bf16[512,256]{1,0:T(8,128)(2,1)S(1)}, u32[]{:S(2)}, u32[]{:S(2)}) collective-permute-start(bf16[512,256]{1,0:T(8,128)(2,1)S(1)} %constant_dynamic-update-slice_fusion.refs_1_), channel_id=1, source_target_pairs={{0,2},{1,5},{2,0},{3,7},{4,6},{5,1},{6,4},{7,3},{8,10},{9,13},{10,... | collective-permute-start | bytes 786440 | tf_op jit(solution)/shard_map/ppermute | solution.py:112
  20.8 4.4 %collective-permute-start.8 = (bf16[1024,256]{1,0:T(8,128)(2,1)}, bf16[1024,256]{1,0:T(8,128)(2,1)}, u32[]{:S(2)}, u32[]{:S(2)}) collective-permute-start(bf16[1024,256]{1,0:T(8,128)(2,1)} %pad_maximum_fusion.1), channel_id=1, source_target_pairs={{0,24},{1,25},{2,26},{3,27},{4,28},{5,29},{6,30},{7,31},{8,0},{9,1... | collective-permute-start | bytes 1572872 | tf_op jit(solution)/shard_map/ppermute | solution.py:112
  26.1 1.8 %collective-permute-start.5 = (bf16[1024,256]{1,0:T(8,128)(2,1)}, bf16[1024,256]{1,0:T(8,128)(2,1)}, u32[]{:S(2)}, u32[]{:S(2)}) collective-permute-start(bf16[1024,256]{1,0:T(8,128)(2,1)} %pad_maximum_fusion), channel_id=1, source_target_pairs={{0,4},{1,3},{2,6},{3,1},{4,0},{5,7},{6,2},{7,5},{8,12},{9,11},{10,... | collective-permute-start | bytes 1572872 | tf_op jit(solution)/shard_map/ppermute | solution.py:112
  28.2 1.2 %shard_map.37.refs_3_ = f32[256,256]{1,0:T(8,128)S(1)} custom-call(s32[4]{0:T(128)S(1)} %pad_add_fusion.1.ids, bf16[256,256]{1,0:T(8,128)(2,1)S(1)} %get-tuple-element.11.rows, bf16[256,2048]{1,0:T(8,128)(2,1)S(1)} %copy-done, bf16[256,2048]{1,0:T(8,128)(2,1)S(1)} %collective-permute-done.1.kernel_other, bf16[256,256]{1,0:T(8,128)(2,1)S(1)} %get-tuple-element.10.refs_0_, ...), custom_call_target="tpu_custom_call" | custom-call | flops 268435456 | bytes 1048576 | tf_op jit(solution)/shard_map/pallas_call | solution.py:70
  29.4 3.6 %collective-permute-done.8.refs_0_ = bf16[1024,256]{1,0:T(8,128)(2,1)} collective-permute-done((bf16[1024,256]{1,0:T(8,128)(2,1)}, bf16[1024,256]{1,0:T(8,128)(2,1)}, u32[]{:S(2)}, u32[]{:S(2)}) %collective-permute-start.8) | collective-permute-done | bytes 524320 | tf_op jit(solution)/shard_map/ppermute | solution.py:112
  33.0 2.0 %shard_map.38.refs_1_ = f32[256,256]{1,0:T(8,128)S(1)} custom-call(s32[8]{0:T(128)S(1)} %stack.138.ids, bf16[256,256]{1,0:T(8,128)(2,1)S(1)} %get-tuple-element.11.rows, bf16[256,2048]{1,0:T(8,128)(2,1)S(1)} %copy-done, bf16[256,2048]{1,0:T(8,128)(2,1)S(1)} %collective-permute-done.1.kernel_other, bf16[1024,256]{1,0:T(8,128)(2,1)} %collective-permute-done.8.refs_0_, ...), custom_call_target="tpu_custom_call" | custom-call | flops 536870912 | bytes 2097152 | tf_op jit(solution)/shard_map/pallas_call | solution.py:70
  35.6 1.7 %shard_map.39.applied = bf16[256,256]{1,0:T(8,128)(2,1)S(1)} custom-call(s32[4]{0:T(128)S(1)} %pad_add_fusion.ids, bf16[256,256]{1,0:T(8,128)(2,1)S(1)} %get-tuple-element.11.rows, bf16[256,2048]{1,0:T(8,128)(2,1)S(1)} %copy-done, bf16[256,2048]{1,0:T(8,128)(2,1)S(1)} %collective-permute-done.1.kernel_other, ...), custom_call_target="tpu_custom_call" | custom-call | flops 268435456 | bytes 1048576 | tf_op jit(solution)/shard_map/pallas_call | solution.py:70
  38.2 1.8 %collective-permute-start.9 = (bf16[1024,256]{1,0:T(8,128)(2,1)S(1)}, bf16[1024,256]{1,0:T(8,128)(2,1)S(1)}, u32[]{:S(2)}, u32[]{:S(2)}) collective-permute-start(bf16[1024,256]{1,0:T(8,128)(2,1)S(1)} %shard_map.41), channel_id=1, source_target_pairs={{0,4},{1,3},{2,6},{3,1},{4,0},{5,7},{6,2},{7,5},{8,12},{9,11},{10,... | collective-permute-start | bytes 1572872 | tf_op jit(solution)/shard_map/ppermute | solution.py:112
  40.1 0.9 %shard_map.40 = f32[1024,256]{1,0:T(8,128)S(1)} custom-call(s32[8]{0:T(128)S(1)} %stack.127.ids, bf16[256,2048]{1,0:T(8,128)(2,1)S(1)} %copy-done.1, bf16[256,256]{1,0:T(8,128)(2,1)S(1)} %shard_map.39.applied), custom_call_target="tpu_custom_call" | custom-call | flops 134217728 | bytes 1048576 | tf_op jit(solution)/shard_map/pallas_call | solution.py:93
  41.0 7.9 %collective-permute-done.9 = bf16[1024,256]{1,0:T(8,128)(2,1)S(1)} collective-permute-done((bf16[1024,256]{1,0:T(8,128)(2,1)S(1)}, bf16[1024,256]{1,0:T(8,128)(2,1)S(1)}, u32[]{:S(2)}, u32[]{:S(2)}) %collective-permute-start.9) | collective-permute-done | bytes 524320 | tf_op jit(solution)/shard_map/ppermute | solution.py:112
  49.0 1.5 %collective-permute-start.10 = (bf16[512,256]{1,0:T(8,128)(2,1)S(1)}, bf16[512,256]{1,0:T(8,128)(2,1)S(1)}, u32[]{:S(2)}, u32[]{:S(2)}) collective-permute-start(bf16[512,256]{1,0:T(8,128)(2,1)S(1)} %fusion), channel_id=1, source_target_pairs={{0,2},{1,5},{2,0},{3,7},{4,6},{5,1},{6,4},{7,3},{8,10},{9,13},{10,... | collective-permute-start | bytes 786440 | tf_op jit(solution)/shard_map/ppermute | solution.py:112
  50.4 5.0 %collective-permute-done.10 = bf16[512,256]{1,0:T(8,128)(2,1)S(1)} collective-permute-done((bf16[512,256]{1,0:T(8,128)(2,1)S(1)}, bf16[512,256]{1,0:T(8,128)(2,1)S(1)}, u32[]{:S(2)}, u32[]{:S(2)}) %collective-permute-start.10) | collective-permute-done | bytes 262176 | tf_op jit(solution)/shard_map/ppermute | solution.py:112
  55.6 5.7 %collective-permute-start.12 = (bf16[128,256]{1,0:T(8,128)(2,1)S(1)}, bf16[128,256]{1,0:T(8,128)(2,1)S(1)}, u32[]{:S(2)}, u32[]{:S(2)}) collective-permute-start(bf16[128,256]{1,0:T(8,128)(2,1)S(1)} %get-tuple-element.9), channel_id=1, source_target_pairs={{0,16},{1,17},{2,18},{3,19},{4,20},{5,21},{6,22},{7,23},{8,24},{9,... | collective-permute-start | bytes 196616 | tf_op jit(solution)/shard_map/ppermute | solution.py:112
  61.3 1.7 %collective-permute-done.11 = bf16[128,256]{1,0:T(8,128)(2,1)S(1)} collective-permute-done((bf16[128,256]{1,0:T(8,128)(2,1)S(1)}, bf16[128,256]{1,0:T(8,128)(2,1)S(1)}, u32[]{:S(2)}, u32[]{:S(2)}) %collective-permute-start.11) | collective-permute-done | bytes 65568 | tf_op jit(solution)/shard_map/ppermute | solution.py:112
  63.0 1.4 %collective-permute-done.12 = bf16[128,256]{1,0:T(8,128)(2,1)S(1)} collective-permute-done((bf16[128,256]{1,0:T(8,128)(2,1)S(1)}, bf16[128,256]{1,0:T(8,128)(2,1)S(1)}, u32[]{:S(2)}, u32[]{:S(2)}) %collective-permute-start.12) | collective-permute-done | bytes 65568 | tf_op jit(solution)/shard_map/ppermute | solution.py:112
  64.4 1.2 %collective-permute-done.13 = bf16[128,256]{1,0:T(8,128)(2,1)S(1)} collective-permute-done((bf16[128,256]{1,0:T(8,128)(2,1)S(1)}, bf16[128,256]{1,0:T(8,128)(2,1)S(1)}, u32[]{:S(2)}, u32[]{:S(2)}) %collective-permute-start.13) | collective-permute-done | bytes 65568 | tf_op jit(solution)/shard_map/ppermute | solution.py:112
  65.7 1.3 %collective-permute-done.14 = f32[128,256]{1,0:T(8,128)S(1)} collective-permute-done((f32[128,256]{1,0:T(8,128)S(1)}, f32[128,256]{1,0:T(8,128)S(1)}, u32[]{:S(2)}, u32[]{:S(2)}) %collective-permute-start.14) | collective-permute-done | bytes 131104 | tf_op jit(solution)/shard_map/ppermute | solution.py:117
  67.0 0.9 %copy.7 = f32[128,2,256]{2,1,0:T(2,128)} copy(f32[128,2,256]{2,0,1:T(8,128)S(1)} %maximum_select_fusion) | data formatting | bytes 524288 | tf_op jit(solution)/shard_map/jit(_where)/select_n | solution.py:164
  (35 shorter events, 5.5 us)
Async XLA Ops:
  0.0 7.3 %copy-start = (bf16[256,2048]{1,0:T(8,128)(2,1)S(1)}, bf16[256,2048]{1,0:T(8,128)(2,1)}, u32[]{:S(2)}) copy-start(bf16[256,2048]{1,0:T(8,128)(2,1)} %kernel_own.5) | copy-start | bytes 3145732
  1.4 1.4 %collective-permute-start = (bf16[128,256]{1,0:T(8,128)(2,1)S(1)}, bf16[128,256]{1,0:T(8,128)(2,1)S(1)}, u32[]{:S(2)}, u32[]{:S(2)}) collective-permute-start(bf16[128,256]{1,0:T(8,128)(2,1)S(1)} %bitcast.42), channel_id=1, source_target_pairs={{0,1},{1,0},{2,3},{3,2},{4,5},{5,4},{6,7},{7,6},{8,9},{9,8},{10,11... | collective-permute-start | bytes 196616 | tf_op jit(solution)/shard_map/ppermute | solution.py:117
  2.8 8.8 %collective-permute-start.2 = (bf16[256,256]{1,0:T(8,128)(2,1)S(1)}, bf16[256,256]{1,0:T(8,128)(2,1)S(1)}, u32[]{:S(2)}, u32[]{:S(2)}) collective-permute-start(bf16[256,256]{1,0:T(8,128)(2,1)S(1)} %get-tuple-element.10.refs_0_), channel_id=1, source_target_pairs={{0,8},{1,9},{2,10},{3,11},{4,12},{5,13},{6,14},{7,15},{8,16},{9,17... | collective-permute-start | bytes 393224 | tf_op jit(solution)/shard_map/ppermute | solution.py:112
  5.8 5.9 %collective-permute-start.6 = (bf16[256,256]{1,0:T(8,128)(2,1)S(1)}, bf16[256,256]{1,0:T(8,128)(2,1)S(1)}, u32[]{:S(2)}, u32[]{:S(2)}) collective-permute-start(bf16[256,256]{1,0:T(8,128)(2,1)S(1)} %get-tuple-element.10.refs_0_), channel_id=1, source_target_pairs={{0,2},{1,5},{2,0},{3,7},{4,6},{5,1},{6,4},{7,3},{8,10},{9,13},{10,... | collective-permute-start | bytes 393224 | tf_op jit(solution)/shard_map/ppermute | solution.py:112
  7.3 20.9 %collective-permute-start.1 = (bf16[256,2048]{1,0:T(8,128)(2,1)S(1)}, bf16[256,2048]{1,0:T(8,128)(2,1)S(1)}, u32[]{:S(2)}, u32[]{:S(2)}) collective-permute-start(bf16[256,2048]{1,0:T(8,128)(2,1)S(1)} %copy-done), channel_id=1, source_target_pairs={{0,1},{1,0},{2,3},{3,2},{4,5},{5,4},{6,7},{7,6},{8,9},{9,8},{10,11... | collective-permute-start | bytes 3145736 | tf_op jit(solution)/shard_map/ppermute | solution.py:117
  11.6 6.8 %collective-permute-start.3 = (bf16[256,256]{1,0:T(8,128)(2,1)S(1)}, bf16[256,256]{1,0:T(8,128)(2,1)S(1)}, u32[]{:S(2)}, u32[]{:S(2)}) collective-permute-start(bf16[256,256]{1,0:T(8,128)(2,1)S(1)} %collective-permute-done.2), channel_id=1, source_target_pairs={{0,8},{1,9},{2,10},{3,11},{4,12},{5,13},{6,14},{7,15},{8,16},{9,17... | collective-permute-start | bytes 393224 | tf_op jit(solution)/shard_map/ppermute | solution.py:112
  11.7 8.3 %collective-permute-start.7 = (bf16[512,256]{1,0:T(8,128)(2,1)S(1)}, bf16[512,256]{1,0:T(8,128)(2,1)S(1)}, u32[]{:S(2)}, u32[]{:S(2)}) collective-permute-start(bf16[512,256]{1,0:T(8,128)(2,1)S(1)} %pad_maximum_fusion.2), channel_id=1, source_target_pairs={{0,4},{1,3},{2,6},{3,1},{4,0},{5,7},{6,2},{7,5},{8,12},{9,11},{10,... | collective-permute-start | bytes 786440 | tf_op jit(solution)/shard_map/ppermute | solution.py:112
  18.5 6.8 %collective-permute-start.4 = (bf16[512,256]{1,0:T(8,128)(2,1)S(1)}, bf16[512,256]{1,0:T(8,128)(2,1)S(1)}, u32[]{:S(2)}, u32[]{:S(2)}) collective-permute-start(bf16[512,256]{1,0:T(8,128)(2,1)S(1)} %constant_dynamic-update-slice_fusion.refs_1_), channel_id=1, source_target_pairs={{0,2},{1,5},{2,0},{3,7},{4,6},{5,1},{6,4},{7,3},{8,10},{9,13},{10,... | collective-permute-start | bytes 786440 | tf_op jit(solution)/shard_map/ppermute | solution.py:112
  20.8 12.1 %collective-permute-start.8 = (bf16[1024,256]{1,0:T(8,128)(2,1)}, bf16[1024,256]{1,0:T(8,128)(2,1)}, u32[]{:S(2)}, u32[]{:S(2)}) collective-permute-start(bf16[1024,256]{1,0:T(8,128)(2,1)} %pad_maximum_fusion.1), channel_id=1, source_target_pairs={{0,24},{1,25},{2,26},{3,27},{4,28},{5,29},{6,30},{7,31},{8,0},{9,1... | collective-permute-start | bytes 1572872 | tf_op jit(solution)/shard_map/ppermute | solution.py:112
  26.1 9.5 %collective-permute-start.5 = (bf16[1024,256]{1,0:T(8,128)(2,1)}, bf16[1024,256]{1,0:T(8,128)(2,1)}, u32[]{:S(2)}, u32[]{:S(2)}) collective-permute-start(bf16[1024,256]{1,0:T(8,128)(2,1)} %pad_maximum_fusion), channel_id=1, source_target_pairs={{0,4},{1,3},{2,6},{3,1},{4,0},{5,7},{6,2},{7,5},{8,12},{9,11},{10,... | collective-permute-start | bytes 1572872 | tf_op jit(solution)/shard_map/ppermute | solution.py:112
  35.0 2.3 %copy-start.1 = (bf16[256,2048]{1,0:T(8,128)(2,1)S(1)}, bf16[256,2048]{1,0:T(8,128)(2,1)}, u32[]{:S(2)}) copy-start(bf16[256,2048]{1,0:T(8,128)(2,1)} %basis.3) | copy-start | bytes 3145732
  38.2 10.7 %collective-permute-start.9 = (bf16[1024,256]{1,0:T(8,128)(2,1)S(1)}, bf16[1024,256]{1,0:T(8,128)(2,1)S(1)}, u32[]{:S(2)}, u32[]{:S(2)}) collective-permute-start(bf16[1024,256]{1,0:T(8,128)(2,1)S(1)} %shard_map.41), channel_id=1, source_target_pairs={{0,4},{1,3},{2,6},{3,1},{4,0},{5,7},{6,2},{7,5},{8,12},{9,11},{10,... | collective-permute-start | bytes 1572872 | tf_op jit(solution)/shard_map/ppermute | solution.py:112
  49.0 6.4 %collective-permute-start.10 = (bf16[512,256]{1,0:T(8,128)(2,1)S(1)}, bf16[512,256]{1,0:T(8,128)(2,1)S(1)}, u32[]{:S(2)}, u32[]{:S(2)}) collective-permute-start(bf16[512,256]{1,0:T(8,128)(2,1)S(1)} %fusion), channel_id=1, source_target_pairs={{0,2},{1,5},{2,0},{3,7},{4,6},{5,1},{6,4},{7,3},{8,10},{9,13},{10,... | collective-permute-start | bytes 786440 | tf_op jit(solution)/shard_map/ppermute | solution.py:112
  55.5 7.5 %collective-permute-start.11 = (bf16[128,256]{1,0:T(8,128)(2,1)S(1)}, bf16[128,256]{1,0:T(8,128)(2,1)S(1)}, u32[]{:S(2)}, u32[]{:S(2)}) collective-permute-start(bf16[128,256]{1,0:T(8,128)(2,1)S(1)} %get-tuple-element.7), channel_id=1, source_target_pairs={{0,8},{1,9},{2,10},{3,11},{4,12},{5,13},{6,14},{7,15},{8,16},{9,17... | collective-permute-start | bytes 196616 | tf_op jit(solution)/shard_map/ppermute | solution.py:112
  55.6 8.8 %collective-permute-start.12 = (bf16[128,256]{1,0:T(8,128)(2,1)S(1)}, bf16[128,256]{1,0:T(8,128)(2,1)S(1)}, u32[]{:S(2)}, u32[]{:S(2)}) collective-permute-start(bf16[128,256]{1,0:T(8,128)(2,1)S(1)} %get-tuple-element.9), channel_id=1, source_target_pairs={{0,16},{1,17},{2,18},{3,19},{4,20},{5,21},{6,22},{7,23},{8,24},{9,... | collective-permute-start | bytes 196616 | tf_op jit(solution)/shard_map/ppermute | solution.py:112
  61.3 4.3 %collective-permute-start.13 = (bf16[128,256]{1,0:T(8,128)(2,1)S(1)}, bf16[128,256]{1,0:T(8,128)(2,1)S(1)}, u32[]{:S(2)}, u32[]{:S(2)}) collective-permute-start(bf16[128,256]{1,0:T(8,128)(2,1)S(1)} %get-tuple-element.8), channel_id=1, source_target_pairs={{0,24},{1,25},{2,26},{3,27},{4,28},{5,29},{6,30},{7,31},{8,0},{9,1... | collective-permute-start | bytes 196616 | tf_op jit(solution)/shard_map/ppermute | solution.py:112
  65.6 1.4 %collective-permute-start.14 = (f32[128,256]{1,0:T(8,128)S(1)}, f32[128,256]{1,0:T(8,128)S(1)}, u32[]{:S(2)}, u32[]{:S(2)}) collective-permute-start(f32[128,256]{1,0:T(8,128)S(1)} %fusion.3), channel_id=1, source_target_pairs={{0,1},{1,0},{2,3},{3,2},{4,5},{5,4},{6,7},{7,6},{8,9},{9,8},{10,11... | collective-permute-start | bytes 393224 | tf_op jit(solution)/shard_map/ppermute | solution.py:117

commit v2 on v1

v2 whole, which is shorter than its diff:
```python
import functools

import jax
import jax.numpy as jnp
from jax import lax
from jax.experimental import pallas as pl
from jax.experimental.pallas import tpu as pltpu
from jax.sharding import PartitionSpec as P

F32 = jnp.float32
BF16 = jnp.bfloat16
VMEM = pl.BlockSpec(memory_space=pltpu.VMEM)
SMEM = pl.BlockSpec(memory_space=pltpu.SMEM)
LIMIT = 40 * 1024 * 1024


def general_body(orbitals, kernel, basis):
    row_orbitals = lax.all_gather(orbitals, "col", axis=0, tiled=True)
    point_rows = row_orbitals.shape[0]
    occupied = orbitals.shape[2]
    column_orbitals = lax.all_gather(orbitals, "row", axis=0, tiled=True)
    density = jnp.einsum(
        "psi,qsi->spq", row_orbitals, column_orbitals, preferred_element_type=F32
    )
    weighted = (density * kernel[None].astype(F32)).astype(BF16)
    applied = jnp.einsum(
        "spq,qsi->psi", weighted, column_orbitals, preferred_element_type=F32
    )
    out_rows = basis.shape[1] // lax.axis_size("row")
    summed = lax.psum(applied, "col").astype(BF16)
    flattened = summed.reshape(point_rows, -1)
    result = lax.psum_scatter(
        lax.dot_general(basis, flattened, (((0,), (0,)), ((), ())), preferred_element_type=F32),
        "row",
        scatter_dimension=0,
        tiled=True,
    )
    return result.reshape(out_rows, 2, occupied)


PARAMS = pltpu.CompilerParams(vmem_limit_bytes=LIMIT)


def tile_at(index, width):
    return pl.ds(pl.multiple_of(index * width, width), width)


def split_kernel(core, orbitals, own, other):
    first_core = core[0] == 0
    zero, one = orbitals[:, 0, :], orbitals[:, 1, :]
    own[...] = jnp.where(first_core, zero, one)
    other[...] = jnp.where(first_core, one, zero)


def split_spins(core, orbitals):
    p, _, i = orbitals.shape
    return pl.pallas_call(
        split_kernel,
        out_shape=[jax.ShapeDtypeStruct((p, i), orbitals.dtype)] * 2,
        in_specs=[SMEM, VMEM],
        out_specs=[VMEM] * 2,
        compiler_params=PARAMS,
    )(core, orbitals)


def join_kernel(*refs):
    out = refs[-1]
    start = 0
    for ref in refs[:-1]:
        out[start : start + ref.shape[0], :] = ref[...]
        start += ref.shape[0]


def join_blocks(*blocks):
    rows = sum(block.shape[0] for block in blocks)
    return pl.pallas_call(
        join_kernel,
        out_shape=jax.ShapeDtypeStruct((rows, blocks[0].shape[1]), blocks[0].dtype),
        in_specs=[VMEM] * len(blocks),
        out_specs=VMEM,
        compiler_params=PARAMS,
        cost_estimate=pl.CostEstimate(flops=2 * 10**10, bytes_accessed=10**6, transcendentals=0),
    )(*blocks)


def turn_kernel(width, ids, basis, out):
    for b in range(out.shape[0] // width):
        out[b * width : (b + 1) * width, :] = basis[:, tile_at(ids[b], width)].T


def turn_tiles(ids, basis, width):
    return pl.pallas_call(
        functools.partial(turn_kernel, width),
        out_shape=jax.ShapeDtypeStruct((ids.shape[0] * width, basis.shape[0]), basis.dtype),
        in_specs=[SMEM, VMEM],
        out_specs=VMEM,
        compiler_params=PARAMS,
    )(ids, basis)


def apply_kernel(n_parts, piece, accumulate, ids, rows, kernel_own, kernel_other, *refs):
    parts = refs[:n_parts]
    acc = refs[n_parts] if accumulate else None
    out = refs[-1]
    total = acc[...] if accumulate else None
    left = rows[...]
    block = 2 * piece
    index = 0
    for part in parts:
        for b in range(part.shape[0] // block):
            columns = part[b * block : (b + 1) * block, :]
            at = pl.ds(pl.multiple_of(ids[index] * piece, piece), piece)
            index += 1
            density = lax.dot_general(
                left, columns, (((1,), (1,)), ((), ())), preferred_element_type=F32
            )
            tile = jnp.concatenate([kernel_own[:, at], kernel_other[:, at]], axis=1)
            weighted = (density * tile.astype(F32)).astype(BF16)
            term = jnp.dot(weighted, columns, preferred_element_type=F32)
            total = term if total is None else total + term
    out[...] = total.astype(out.dtype)


def apply_blocks(ids, rows, kernel_own, kernel_other, parts, acc, dtype, weight):
    args = [ids, rows, kernel_own, kernel_other, *parts]
    if acc is not None:
        args.append(acc)
    columns = sum(part.shape[0] for part in parts)
    n, i = rows.shape
    return pl.pallas_call(
        functools.partial(apply_kernel, len(parts), kernel_own.shape[1] // 16, acc is not None),
        out_shape=jax.ShapeDtypeStruct((n, i), dtype),
        in_specs=[SMEM] + [VMEM] * (len(args) - 1),
        out_specs=VMEM,
        compiler_params=PARAMS,
        cost_estimate=pl.CostEstimate(
            flops=weight * 4 * n * i * columns, bytes_accessed=weight * 2 * columns * (n + i), transcendentals=0
        ),
    )(*args)


def project_kernel(start, tiles, applied, *outs):
    for out in outs:
        n = out.shape[0]
        total = jnp.dot(tiles[start : start + n, :], applied[...], preferred_element_type=F32)
        out[...] = total.astype(out.dtype)
        start += n


def project(start, tiles, applied, shapes):
    p, i = applied.shape
    rows = sum(n for n, _ in shapes)
    return pl.pallas_call(
        functools.partial(project_kernel, start),
        out_shape=[jax.ShapeDtypeStruct((n, i), t) for n, t in shapes],
        in_specs=[VMEM, VMEM],
        out_specs=[VMEM] * len(shapes),
        compiler_params=PARAMS,
        cost_estimate=pl.CostEstimate(flops=2 * rows * p * i, bytes_accessed=4 * rows * p, transcendentals=0),
    )(tiles, applied)


def box_body(orbitals, kernel, basis):
    r = lax.axis_index("row")
    c = lax.axis_index("col")
    piece = orbitals.shape[0]
    width = basis.shape[1] // 16

    def send(a, to):
        pairs = [(2 * q + k, 2 * to(q, k) + k) for q in range(16) for k in range(2)]
        return lax.ppermute(a, ("row", "col"), pairs)

    first = lambda a: send(a, lambda q, k: q ^ (1 + k))
    second = lambda a: send(a, lambda q, k: q ^ (2 - k))
    plane = lambda a, d: send(a, lambda q, k: q ^ (4 * d))
    swap = lambda a: lax.ppermute(a, "col", [(0, 1), (1, 0)])
    join = lambda *a: jnp.concatenate(a, axis=0)
    ids = lambda *v: jnp.stack(v).astype(jnp.int32)

    def after(a, *others):
        return lax.optimization_barrier((a, *others))[0]

    near, far = 1 + c, 2 - c

    own, other = split_spins(ids(c), orbitals)
    other = swap(other)
    block = join(own, other)
    rows = jnp.where(c == 0, block, join(other, own))
    block, rows = lax.optimization_barrier((block, rows))
    x0 = first(block)
    z8 = plane(block, 2)
    p0 = join_blocks(block, x0)
    y0 = second(p0)
    z12 = plane(z8, 1)
    x8 = first(z8)
    zp = plane(join_blocks(p0, y0), 1)
    x12 = first(z12)
    p8 = join_blocks(z8, x8)
    y8 = second(p8)
    p12 = join_blocks(z12, x12)
    y12 = second(p12)
    kernel_other = swap(after(kernel, x8))
    tiles = turn_tiles(
        ids(*[r ^ (near * a) ^ (far * b) ^ (4 * k) for a in (1, 0) for b in (1, 0) for k in range(4)]),
        after(basis, x12), width,
    )

    around = lambda base: [base ^ d for d in (0, near, far, 3)]
    halves = (rows, kernel, kernel_other)
    acc = apply_blocks(ids(*around(r), *around(r ^ 8)), *halves, [p0, y0, p8, y8], None, F32, 20)
    applied = apply_blocks(ids(*around(r ^ 4), *around(r ^ 12)), *halves, [zp, p12, y12], acc, BF16, 1)

    n = 4 * width
    (send_a,) = project(0, tiles, applied, [(n, BF16)])
    send_b, keep_a, keep_b = project(n, tiles, applied, [(n, BF16), (n, F32), (n, F32)])
    got_a, got_b = first(send_a), first(send_b)
    rest = second((keep_a + got_a.astype(F32)).astype(BF16)).astype(F32) + (keep_b + got_b.astype(F32))
    result = rest[:width]
    for k in (1, 2, 3):
        result = result + plane(rest[k * width : (k + 1) * width].astype(BF16), k).astype(F32)
    partner = swap(result)
    return jnp.where(
        c == 0, jnp.stack([result, partner], axis=1), jnp.stack([partner, result], axis=1)
    )


def solution(mesh):
    box = dict(mesh.shape) == {"row": 16, "col": 2}
    return jax.shard_map(
        box_body if box else general_body,
        mesh=mesh,
        in_specs=(P(("row", "col"), None, None), P("row", "col"), P("row", None)),
        out_specs=P("row", None, None),
        check_vma=False,
    )
```

time: 68.1 us -> 63.3 us (0.930)
  other arithmetic: 2.11 us -> 0.22 us
  Pallas kernels: 6.7 us -> 4.92 us
  starting transfers between devices: 23.4 us -> 22.5 us
    pallas_call x3 -> x2, Pallas kernels: 4.91 us -> 2.99 us  [apply_blocks(): pl.pallas_call(functools.partial(apply_kernel, len(parts), kernel_own.sha...]
    concatenate x4 -> x0, other arithmetic: 1.73 us -> none  [box_body(): join = lambda *a: jnp.concatenate(a, axis=0)]
    dynamic_slice x1 -> x0, local copies, waits for them, and re-layouts: 1.33 us -> none  [box_body(): other = swap(lax.dynamic_index_in_dim(orbitals, 1 - c, 1, keepdims=False))]
    unnamed x7, local copies, waits for them, and re-layouts: 0.04 us -> 0.92 us
    ppermute x12 -> x15, starting transfers between devices: 22.8 us -> 21.9 us  [send(): return lax.ppermute(a, ('row', 'col'), pairs)]
    ppermute x12 -> x15, waiting for transfers between devices: 30.8 us -> 31.1 us  [send(): return lax.ppermute(a, ('row', 'col'), pairs)]
    pallas_call x2 -> x8, Pallas kernels: 1.79 us -> 1.93 us  [the longest x1 0.87 us: turn_tiles(): pl.pallas_call(functools.partial(turn_kernel, width), out_shape=jax.Shape...]
  transfers between devices with their start and end apart: 15 -> 18, of which waited for: 11 -> 14; matrix products, arithmetic and copies ran while one was open for 3% -> 1% of each run, Pallas kernels for 6% -> 4%
where the time goes in v2:
time: 63.3 us; the launch traced here: 63.2 us
  waiting for transfers between devices  33.3 us (53%)
  starting transfers between devices  22.5 us (36%)
  Pallas kernels  4.92 us (8%)
  local copies, waits for them, and re-layouts  2.11 us (3%)
    ppermute x15, waiting for transfers between devices, send(): return lax.ppermute(a, ('row', 'col'), pairs)  31.1 us
    ppermute x15, starting transfers between devices, send(): return lax.ppermute(a, ('row', 'col'), pairs)  21.9 us
    pallas_call x2, Pallas kernels, apply_blocks(): pl.pallas_call(functools.partial(apply_kernel, len(parts), kernel_own.sha...  2.99 us
    ppermute x3, waiting for transfers between devices, box_body(): swap = lambda a: lax.ppermute(a, 'col', [(0, 1), (1, 0)])  2.23 us
  transfers between devices with their start and end apart: 18, of which 14 were waited for; matrix products, arithmetic and copies ran while one was open for 1% of the time, Pallas kernels for 4%

profile of v2, /device:TPU:0, one launch (start us, length us, event | category | flops | bytes accessed | tf_op | source)
XLA Modules:
  0.0 63.2 jit_solution(5352851706292005452)
XLA Ops:
  0.0 0.9 %copy-done.2 = bf16[128,2,256]{2,1,0:T(2,128)(2,1)S(1)} copy-done((bf16[128,2,256]{2,1,0:T(2,128)(2,1)S(1)}, bf16[128,2,256]{2,1,0:T(2,128)(2,1)}, u32[]{:S(2)}) %copy-start.2) | copy-done | bytes 131096
  2.8 4.0 %collective-permute-start.1 = (bf16[256,256]{1,0:T(8,128)(2,1)S(1)}, bf16[256,256]{1,0:T(8,128)(2,1)S(1)}, u32[]{:S(2)}, u32[]{:S(2)}) collective-permute-start(bf16[256,256]{1,0:T(8,128)(2,1)S(1)} %constant_dynamic-update-slice_fusion.refs_0_), channel_id=1, source_target_pairs={{0,16},{1,17},{2,18},{3,19},{4,20},{5,21},{6,22},{7,23},{8,24},{9,... | collective-permute-start | bytes 393224 | tf_op jit(solution)/shard_map/ppermute | solution.py:171
  6.8 1.5 %collective-permute-start.6 = (bf16[256,256]{1,0:T(8,128)(2,1)S(1)}, bf16[256,256]{1,0:T(8,128)(2,1)S(1)}, u32[]{:S(2)}, u32[]{:S(2)}) collective-permute-start(bf16[256,256]{1,0:T(8,128)(2,1)S(1)} %constant_dynamic-update-slice_fusion.refs_0_), channel_id=1, source_target_pairs={{0,2},{1,5},{2,0},{3,7},{4,6},{5,1},{6,4},{7,3},{8,10},{9,13},{10,... | collective-permute-start | bytes 393224 | tf_op jit(solution)/shard_map/ppermute | solution.py:171
  8.5 4.9 %collective-permute-done.1.refs_0_ = bf16[256,256]{1,0:T(8,128)(2,1)S(1)} collective-permute-done((bf16[256,256]{1,0:T(8,128)(2,1)S(1)}, bf16[256,256]{1,0:T(8,128)(2,1)S(1)}, u32[]{:S(2)}, u32[]{:S(2)}) %collective-permute-start.1) | collective-permute-done | bytes 131104 | tf_op jit(solution)/shard_map/ppermute | solution.py:171
  13.4 1.5 %collective-permute-start.4 = (bf16[256,256]{1,0:T(8,128)(2,1)S(1)}, bf16[256,256]{1,0:T(8,128)(2,1)S(1)}, u32[]{:S(2)}, u32[]{:S(2)}) collective-permute-start(bf16[256,256]{1,0:T(8,128)(2,1)S(1)} %collective-permute-done.1.refs_0_), channel_id=1, source_target_pairs={{0,2},{1,5},{2,0},{3,7},{4,6},{5,1},{6,4},{7,3},{8,10},{9,13},{10,... | collective-permute-start | bytes 393224 | tf_op jit(solution)/shard_map/ppermute | solution.py:171
  15.0 1.6 %collective-permute-start.7 = (bf16[512,256]{1,0:T(8,128)(2,1)S(1)}, bf16[512,256]{1,0:T(8,128)(2,1)S(1)}, u32[]{:S(2)}, u32[]{:S(2)}) collective-permute-start(bf16[512,256]{1,0:T(8,128)(2,1)S(1)} %shard_map.39.refs_0_), channel_id=1, source_target_pairs={{0,4},{1,3},{2,6},{3,1},{4,0},{5,7},{6,2},{7,5},{8,12},{9,11},{10,... | collective-permute-start | bytes 786440 | tf_op jit(solution)/shard_map/ppermute | solution.py:171
  17.2 2.5 %collective-permute-done.4.refs_1_ = bf16[256,256]{1,0:T(8,128)(2,1)S(1)} collective-permute-done((bf16[256,256]{1,0:T(8,128)(2,1)S(1)}, bf16[256,256]{1,0:T(8,128)(2,1)S(1)}, u32[]{:S(2)}, u32[]{:S(2)}) %collective-permute-start.4) | collective-permute-done | bytes 131104 | tf_op jit(solution)/shard_map/ppermute | solution.py:171
  19.8 1.6 %collective-permute-start.10 = (bf16[512,256]{1,0:T(8,128)(2,1)S(1)}, bf16[512,256]{1,0:T(8,128)(2,1)S(1)}, u32[]{:S(2)}, u32[]{:S(2)}) collective-permute-start(bf16[512,256]{1,0:T(8,128)(2,1)S(1)} %shard_map.42.refs_2_), channel_id=1, source_target_pairs={{0,4},{1,3},{2,6},{3,1},{4,0},{5,7},{6,2},{7,5},{8,12},{9,11},{10,... | collective-permute-start | bytes 786440 | tf_op jit(solution)/shard_map/ppermute | solution.py:171
  21.5 1.5 %collective-permute-start.3 = (bf16[256,256]{1,0:T(8,128)(2,1)S(1)}, bf16[256,256]{1,0:T(8,128)(2,1)S(1)}, u32[]{:S(2)}, u32[]{:S(2)}) collective-permute-start(bf16[256,256]{1,0:T(8,128)(2,1)S(1)} %collective-permute-done.2.refs_0_), channel_id=1, source_target_pairs={{0,2},{1,5},{2,0},{3,7},{4,6},{5,1},{6,4},{7,3},{8,10},{9,13},{10,... | collective-permute-start | bytes 393224 | tf_op jit(solution)/shard_map/ppermute | solution.py:171
  23.7 2.8 %collective-permute-done.3.refs_1_ = bf16[256,256]{1,0:T(8,128)(2,1)S(1)} collective-permute-done((bf16[256,256]{1,0:T(8,128)(2,1)S(1)}, bf16[256,256]{1,0:T(8,128)(2,1)S(1)}, u32[]{:S(2)}, u32[]{:S(2)}) %collective-permute-start.3) | collective-permute-done | bytes 131104 | tf_op jit(solution)/shard_map/ppermute | solution.py:171
  28.0 1.5 %shard_map.43.refs_3_ = f32[256,256]{1,0:T(8,128)S(1)} custom-call(s32[8]{0:T(128)S(1)} %stack.139.ids, bf16[256,256]{1,0:T(8,128)(2,1)S(1)} %maximum_select_fusion.1.rows, bf16[256,2048]{1,0:T(8,128)(2,1)S(1)} %copy-done.1, bf16[256,2048]{1,0:T(8,128)(2,1)S(1)} %collective-permute-done.5.kernel_other, bf16[512,256]{1,0:T(8,128)(2,1)S(1)} %shard_map.39.refs_0_, ...), custom_call_target="tpu_custom_call" | custom-call | flops 10737418240 | bytes 41943040 | tf_op jit(solution)/shard_map/pallas_call | solution.py:130
  29.5 3.5 %collective-permute-done.9.refs_2_ = bf16[512,256]{1,0:T(8,128)(2,1)S(1)} collective-permute-done((bf16[512,256]{1,0:T(8,128)(2,1)S(1)}, bf16[512,256]{1,0:T(8,128)(2,1)S(1)}, u32[]{:S(2)}, u32[]{:S(2)}) %collective-permute-start.9) | collective-permute-done | bytes 262176 | tf_op jit(solution)/shard_map/ppermute | solution.py:171
  32.9 3.1 %collective-permute-done.8.refs_0_ = bf16[1024,256]{1,0:T(8,128)(2,1)S(1)} collective-permute-done((bf16[1024,256]{1,0:T(8,128)(2,1)S(1)}, bf16[1024,256]{1,0:T(8,128)(2,1)S(1)}, u32[]{:S(2)}, u32[]{:S(2)}) %collective-permute-start.8) | collective-permute-done | bytes 524320 | tf_op jit(solution)/shard_map/ppermute | solution.py:171
  36.0 1.5 %shard_map.44.applied = bf16[256,256]{1,0:T(8,128)(2,1)S(1)} custom-call(s32[8]{0:T(128)S(1)} %stack.134.ids, bf16[256,256]{1,0:T(8,128)(2,1)S(1)} %maximum_select_fusion.1.rows, bf16[256,2048]{1,0:T(8,128)(2,1)S(1)} %copy-done.1, bf16[256,2048]{1,0:T(8,128)(2,1)S(1)} %collective-permute-done.5.kernel_other, ...), custom_call_target="tpu_custom_call" | custom-call | flops 536870912 | bytes 2097152 | tf_op jit(solution)/shard_map/pallas_call | solution.py:130
  37.8 1.6 %collective-permute-start.11 = (bf16[512,256]{1,0:T(8,128)(2,1)S(1)}, bf16[512,256]{1,0:T(8,128)(2,1)S(1)}, u32[]{:S(2)}, u32[]{:S(2)}) collective-permute-start(bf16[512,256]{1,0:T(8,128)(2,1)S(1)} %shard_map.46), channel_id=1, source_target_pairs={{0,2},{1,5},{2,0},{3,7},{4,6},{5,1},{6,4},{7,3},{8,10},{9,13},{10,... | collective-permute-start | bytes 786440 | tf_op jit(solution)/shard_map/ppermute | solution.py:171
  40.3 3.9 %collective-permute-done.11 = bf16[512,256]{1,0:T(8,128)(2,1)S(1)} collective-permute-done((bf16[512,256]{1,0:T(8,128)(2,1)S(1)}, bf16[512,256]{1,0:T(8,128)(2,1)S(1)}, u32[]{:S(2)}, u32[]{:S(2)}) %collective-permute-start.11) | collective-permute-done | bytes 262176 | tf_op jit(solution)/shard_map/ppermute | solution.py:171
  44.3 1.6 %collective-permute-start.12 = (bf16[512,256]{1,0:T(8,128)(2,1)S(1)}, bf16[512,256]{1,0:T(8,128)(2,1)S(1)}, u32[]{:S(2)}, u32[]{:S(2)}) collective-permute-start(bf16[512,256]{1,0:T(8,128)(2,1)S(1)} %add_convert_fusion), channel_id=1, source_target_pairs={{0,4},{1,3},{2,6},{3,1},{4,0},{5,7},{6,2},{7,5},{8,12},{9,11},{10,... | collective-permute-start | bytes 786440 | tf_op jit(solution)/shard_map/ppermute | solution.py:171
  45.9 2.6 %collective-permute-done.13 = bf16[512,256]{1,0:T(8,128)(2,1)S(1)} collective-permute-done((bf16[512,256]{1,0:T(8,128)(2,1)S(1)}, bf16[512,256]{1,0:T(8,128)(2,1)S(1)}, u32[]{:S(2)}, u32[]{:S(2)}) %collective-permute-start.13) | collective-permute-done | bytes 262176 | tf_op jit(solution)/shard_map/ppermute | solution.py:171
  48.6 2.2 %collective-permute-done.12 = bf16[512,256]{1,0:T(8,128)(2,1)S(1)} collective-permute-done((bf16[512,256]{1,0:T(8,128)(2,1)S(1)}, bf16[512,256]{1,0:T(8,128)(2,1)S(1)}, u32[]{:S(2)}, u32[]{:S(2)}) %collective-permute-start.12) | collective-permute-done | bytes 262176 | tf_op jit(solution)/shard_map/ppermute | solution.py:171
  51.4 3.4 %collective-permute-start.15 = (bf16[128,256]{1,0:T(8,128)(2,1)S(1)}, bf16[128,256]{1,0:T(8,128)(2,1)S(1)}, u32[]{:S(2)}, u32[]{:S(2)}) collective-permute-start(bf16[128,256]{1,0:T(8,128)(2,1)S(1)} %get-tuple-element.27), channel_id=1, source_target_pairs={{0,16},{1,17},{2,18},{3,19},{4,20},{5,21},{6,22},{7,23},{8,24},{9,... | collective-permute-start | bytes 196616 | tf_op jit(solution)/shard_map/ppermute | solution.py:171
  55.7 3.1 %collective-permute-done.15 = bf16[128,256]{1,0:T(8,128)(2,1)S(1)} collective-permute-done((bf16[128,256]{1,0:T(8,128)(2,1)S(1)}, bf16[128,256]{1,0:T(8,128)(2,1)S(1)}, u32[]{:S(2)}, u32[]{:S(2)}) %collective-permute-start.15) | collective-permute-done | bytes 65568 | tf_op jit(solution)/shard_map/ppermute | solution.py:171
  58.8 2.0 %collective-permute-done.16 = bf16[128,256]{1,0:T(8,128)(2,1)S(1)} collective-permute-done((bf16[128,256]{1,0:T(8,128)(2,1)S(1)}, bf16[128,256]{1,0:T(8,128)(2,1)S(1)}, u32[]{:S(2)}, u32[]{:S(2)}) %collective-permute-start.16) | collective-permute-done | bytes 65568 | tf_op jit(solution)/shard_map/ppermute | solution.py:171
  60.9 1.3 %collective-permute-done.17 = f32[128,256]{1,0:T(8,128)S(1)} collective-permute-done((f32[128,256]{1,0:T(8,128)S(1)}, f32[128,256]{1,0:T(8,128)S(1)}, u32[]{:S(2)}, u32[]{:S(2)}) %collective-permute-start.17) | collective-permute-done | bytes 131104 | tf_op jit(solution)/shard_map/ppermute | solution.py:176
  62.3 0.9 %copy.4 = f32[128,2,256]{2,1,0:T(2,128)} copy(f32[128,2,256]{2,0,1:T(8,128)S(1)} %maximum_select_fusion) | data formatting | bytes 524288 | tf_op jit(solution)/shard_map/jit(_where)/select_n | solution.py:222
  (40 shorter events, 8.0 us)
Async XLA Ops:
  0.0 0.9 %copy-start.2 = (bf16[128,2,256]{2,1,0:T(2,128)(2,1)S(1)}, bf16[128,2,256]{2,1,0:T(2,128)(2,1)}, u32[]{:S(2)}) copy-start(bf16[128,2,256]{2,1,0:T(2,128)(2,1)} %orbitals.1) | copy-start | bytes 393220
  1.3 1.4 %collective-permute-start = (bf16[128,256]{1,0:T(8,128)(2,1)S(1)}, bf16[128,256]{1,0:T(8,128)(2,1)S(1)}, u32[]{:S(2)}, u32[]{:S(2)}) collective-permute-start(bf16[128,256]{1,0:T(8,128)(2,1)S(1)} %get-tuple-element.15), channel_id=1, source_target_pairs={{0,1},{1,0},{2,3},{3,2},{4,5},{5,4},{6,7},{7,6},{8,9},{9,8},{10,11... | collective-permute-start | bytes 196616 | tf_op jit(solution)/shard_map/ppermute | solution.py:176
  2.8 10.6 %collective-permute-start.1 = (bf16[256,256]{1,0:T(8,128)(2,1)S(1)}, bf16[256,256]{1,0:T(8,128)(2,1)S(1)}, u32[]{:S(2)}, u32[]{:S(2)}) collective-permute-start(bf16[256,256]{1,0:T(8,128)(2,1)S(1)} %constant_dynamic-update-slice_fusion.refs_0_), channel_id=1, source_target_pairs={{0,16},{1,17},{2,18},{3,19},{4,20},{5,21},{6,22},{7,23},{8,24},{9,... | collective-permute-start | bytes 393224 | tf_op jit(solution)/shard_map/ppermute | solution.py:171
  6.8 8.2 %collective-permute-start.6 = (bf16[256,256]{1,0:T(8,128)(2,1)S(1)}, bf16[256,256]{1,0:T(8,128)(2,1)S(1)}, u32[]{:S(2)}, u32[]{:S(2)}) collective-permute-start(bf16[256,256]{1,0:T(8,128)(2,1)S(1)} %constant_dynamic-update-slice_fusion.refs_0_), channel_id=1, source_target_pairs={{0,2},{1,5},{2,0},{3,7},{4,6},{5,1},{6,4},{7,3},{8,10},{9,13},{10,... | collective-permute-start | bytes 393224 | tf_op jit(solution)/shard_map/ppermute | solution.py:171
  13.4 6.4 %collective-permute-start.4 = (bf16[256,256]{1,0:T(8,128)(2,1)S(1)}, bf16[256,256]{1,0:T(8,128)(2,1)S(1)}, u32[]{:S(2)}, u32[]{:S(2)}) collective-permute-start(bf16[256,256]{1,0:T(8,128)(2,1)S(1)} %collective-permute-done.1.refs_0_), channel_id=1, source_target_pairs={{0,2},{1,5},{2,0},{3,7},{4,6},{5,1},{6,4},{7,3},{8,10},{9,13},{10,... | collective-permute-start | bytes 393224 | tf_op jit(solution)/shard_map/ppermute | solution.py:171
  14.9 6.5 %copy-start.1 = (bf16[256,2048]{1,0:T(8,128)(2,1)S(1)}, bf16[256,2048]{1,0:T(8,128)(2,1)}, u32[]{:S(2)}) copy-start(bf16[256,2048]{1,0:T(8,128)(2,1)} %kernel_own.3) | copy-start | bytes 3145732
  15.0 8.1 %collective-permute-start.7 = (bf16[512,256]{1,0:T(8,128)(2,1)S(1)}, bf16[512,256]{1,0:T(8,128)(2,1)S(1)}, u32[]{:S(2)}, u32[]{:S(2)}) collective-permute-start(bf16[512,256]{1,0:T(8,128)(2,1)S(1)} %shard_map.39.refs_0_), channel_id=1, source_target_pairs={{0,4},{1,3},{2,6},{3,1},{4,0},{5,7},{6,2},{7,5},{8,12},{9,11},{10,... | collective-permute-start | bytes 786440 | tf_op jit(solution)/shard_map/ppermute | solution.py:171
  16.5 5.0 %collective-permute-start.2 = (bf16[256,256]{1,0:T(8,128)(2,1)S(1)}, bf16[256,256]{1,0:T(8,128)(2,1)S(1)}, u32[]{:S(2)}, u32[]{:S(2)}) collective-permute-start(bf16[256,256]{1,0:T(8,128)(2,1)S(1)} %collective-permute-done.1.refs_0_), channel_id=1, source_target_pairs={{0,8},{1,9},{2,10},{3,11},{4,12},{5,13},{6,14},{7,15},{8,0},{9,1},... | collective-permute-start | bytes 393224 | tf_op jit(solution)/shard_map/ppermute | solution.py:171
  19.8 8.2 %collective-permute-start.10 = (bf16[512,256]{1,0:T(8,128)(2,1)S(1)}, bf16[512,256]{1,0:T(8,128)(2,1)S(1)}, u32[]{:S(2)}, u32[]{:S(2)}) collective-permute-start(bf16[512,256]{1,0:T(8,128)(2,1)S(1)} %shard_map.42.refs_2_), channel_id=1, source_target_pairs={{0,4},{1,3},{2,6},{3,1},{4,0},{5,7},{6,2},{7,5},{8,12},{9,11},{10,... | collective-permute-start | bytes 786440 | tf_op jit(solution)/shard_map/ppermute | solution.py:171
  21.4 6.6 %collective-permute-start.5 = (bf16[256,2048]{1,0:T(8,128)(2,1)S(1)}, bf16[256,2048]{1,0:T(8,128)(2,1)S(1)}, u32[]{:S(2)}, u32[]{:S(2)}) collective-permute-start(bf16[256,2048]{1,0:T(8,128)(2,1)S(1)} %copy-done.1), channel_id=1, source_target_pairs={{0,1},{1,0},{2,3},{3,2},{4,5},{5,4},{6,7},{7,6},{8,9},{9,8},{10,11... | collective-permute-start | bytes 3145736 | tf_op jit(solution)/shard_map/ppermute | solution.py:176
  21.5 5.0 %collective-permute-start.3 = (bf16[256,256]{1,0:T(8,128)(2,1)S(1)}, bf16[256,256]{1,0:T(8,128)(2,1)S(1)}, u32[]{:S(2)}, u32[]{:S(2)}) collective-permute-start(bf16[256,256]{1,0:T(8,128)(2,1)S(1)} %collective-permute-done.2.refs_0_), channel_id=1, source_target_pairs={{0,2},{1,5},{2,0},{3,7},{4,6},{5,1},{6,4},{7,3},{8,10},{9,13},{10,... | collective-permute-start | bytes 393224 | tf_op jit(solution)/shard_map/ppermute | solution.py:171
  23.1 4.0 %copy-start = (bf16[256,2048]{1,0:T(8,128)(2,1)S(1)}, bf16[256,2048]{1,0:T(8,128)(2,1)}, u32[]{:S(2)}) copy-start(bf16[256,2048]{1,0:T(8,128)(2,1)} %basis) | copy-start | bytes 3145732
  23.1 13.0 %collective-permute-start.8 = (bf16[1024,256]{1,0:T(8,128)(2,1)S(1)}, bf16[1024,256]{1,0:T(8,128)(2,1)S(1)}, u32[]{:S(2)}, u32[]{:S(2)}) collective-permute-start(bf16[1024,256]{1,0:T(8,128)(2,1)S(1)} %shard_map.40), channel_id=1, source_target_pairs={{0,8},{1,9},{2,10},{3,11},{4,12},{5,13},{6,14},{7,15},{8,0},{9,1},... | collective-permute-start | bytes 1572872 | tf_op jit(solution)/shard_map/ppermute | solution.py:171
  26.5 6.4 %collective-permute-start.9 = (bf16[512,256]{1,0:T(8,128)(2,1)S(1)}, bf16[512,256]{1,0:T(8,128)(2,1)S(1)}, u32[]{:S(2)}, u32[]{:S(2)}) collective-permute-start(bf16[512,256]{1,0:T(8,128)(2,1)S(1)} %shard_map.41.refs_1_), channel_id=1, source_target_pairs={{0,4},{1,3},{2,6},{3,1},{4,0},{5,7},{6,2},{7,5},{8,12},{9,11},{10,... | collective-permute-start | bytes 786440 | tf_op jit(solution)/shard_map/ppermute | solution.py:171
  37.8 6.4 %collective-permute-start.11 = (bf16[512,256]{1,0:T(8,128)(2,1)S(1)}, bf16[512,256]{1,0:T(8,128)(2,1)S(1)}, u32[]{:S(2)}, u32[]{:S(2)}) collective-permute-start(bf16[512,256]{1,0:T(8,128)(2,1)S(1)} %shard_map.46), channel_id=1, source_target_pairs={{0,2},{1,5},{2,0},{3,7},{4,6},{5,1},{6,4},{7,3},{8,10},{9,13},{10,... | collective-permute-start | bytes 786440 | tf_op jit(solution)/shard_map/ppermute | solution.py:171
  39.8 8.8 %collective-permute-start.13 = (bf16[512,256]{1,0:T(8,128)(2,1)S(1)}, bf16[512,256]{1,0:T(8,128)(2,1)S(1)}, u32[]{:S(2)}, u32[]{:S(2)}) collective-permute-start(bf16[512,256]{1,0:T(8,128)(2,1)S(1)} %get-tuple-element.22), channel_id=1, source_target_pairs={{0,2},{1,5},{2,0},{3,7},{4,6},{5,1},{6,4},{7,3},{8,10},{9,13},{10,... | collective-permute-start | bytes 786440 | tf_op jit(solution)/shard_map/ppermute | solution.py:171
  44.3 6.4 %collective-permute-start.12 = (bf16[512,256]{1,0:T(8,128)(2,1)S(1)}, bf16[512,256]{1,0:T(8,128)(2,1)S(1)}, u32[]{:S(2)}, u32[]{:S(2)}) collective-permute-start(bf16[512,256]{1,0:T(8,128)(2,1)S(1)} %add_convert_fusion), channel_id=1, source_target_pairs={{0,4},{1,3},{2,6},{3,1},{4,0},{5,7},{6,2},{7,5},{8,12},{9,11},{10,... | collective-permute-start | bytes 786440 | tf_op jit(solution)/shard_map/ppermute | solution.py:171
  50.8 4.9 %collective-permute-start.14 = (bf16[128,256]{1,0:T(8,128)(2,1)S(1)}, bf16[128,256]{1,0:T(8,128)(2,1)S(1)}, u32[]{:S(2)}, u32[]{:S(2)}) collective-permute-start(bf16[128,256]{1,0:T(8,128)(2,1)S(1)} %get-tuple-element.25), channel_id=1, source_target_pairs={{0,8},{1,9},{2,10},{3,11},{4,12},{5,13},{6,14},{7,15},{8,0},{9,1},... | collective-permute-start | bytes 196616 | tf_op jit(solution)/shard_map/ppermute | solution.py:171
  51.4 7.4 %collective-permute-start.15 = (bf16[128,256]{1,0:T(8,128)(2,1)S(1)}, bf16[128,256]{1,0:T(8,128)(2,1)S(1)}, u32[]{:S(2)}, u32[]{:S(2)}) collective-permute-start(bf16[128,256]{1,0:T(8,128)(2,1)S(1)} %get-tuple-element.27), channel_id=1, source_target_pairs={{0,16},{1,17},{2,18},{3,19},{4,20},{5,21},{6,22},{7,23},{8,24},{9,... | collective-permute-start | bytes 196616 | tf_op jit(solution)/shard_map/ppermute | solution.py:171
  54.8 6.1 %collective-permute-start.16 = (bf16[128,256]{1,0:T(8,128)(2,1)S(1)}, bf16[128,256]{1,0:T(8,128)(2,1)S(1)}, u32[]{:S(2)}, u32[]{:S(2)}) collective-permute-start(bf16[128,256]{1,0:T(8,128)(2,1)S(1)} %get-tuple-element.26), channel_id=1, source_target_pairs={{0,24},{1,25},{2,26},{3,27},{4,28},{5,29},{6,30},{7,31},{8,16},{9,... | collective-permute-start | bytes 196616 | tf_op jit(solution)/shard_map/ppermute | solution.py:171
  60.9 1.4 %collective-permute-start.17 = (f32[128,256]{1,0:T(8,128)S(1)}, f32[128,256]{1,0:T(8,128)S(1)}, u32[]{:S(2)}, u32[]{:S(2)}) collective-permute-start(f32[128,256]{1,0:T(8,128)S(1)} %fusion.1), channel_id=1, source_target_pairs={{0,1},{1,0},{2,3},{3,2},{4,5},{5,4},{6,7},{7,6},{8,9},{9,8},{10,11... | collective-permute-start | bytes 393224 | tf_op jit(solution)/shard_map/ppermute | solution.py:176

commit v3 on v2

--- a/solution.py
+++ b/solution.py
@@ -11,6 +11,7 @@
 BF16 = jnp.bfloat16
 VMEM = pl.BlockSpec(memory_space=pltpu.VMEM)
 SMEM = pl.BlockSpec(memory_space=pltpu.SMEM)
+ANY = pl.BlockSpec(memory_space=pl.ANY)
 LIMIT = 40 * 1024 * 1024
 
 
@@ -41,6 +42,10 @@
 PARAMS = pltpu.CompilerParams(vmem_limit_bytes=LIMIT)
 
 
+def pin(weight):
+    return pl.CostEstimate(flops=weight * 10**9, bytes_accessed=10**6, transcendentals=0)
+
+
 def tile_at(index, width):
     return pl.ds(pl.multiple_of(index * width, width), width)
 
@@ -71,7 +76,7 @@
         start += ref.shape[0]
 
 
-def join_blocks(*blocks):
+def join_blocks(*blocks, weight=20):
     rows = sum(block.shape[0] for block in blocks)
     return pl.pallas_call(
         join_kernel,
@@ -79,7 +84,7 @@
         in_specs=[VMEM] * len(blocks),
         out_specs=VMEM,
         compiler_params=PARAMS,
-        cost_estimate=pl.CostEstimate(flops=2 * 10**10, bytes_accessed=10**6, transcendentals=0),
+        cost_estimate=pin(weight),
     )(*blocks)
 
 
@@ -98,45 +103,81 @@
     )(ids, basis)
 
 
-def apply_kernel(n_parts, piece, accumulate, ids, rows, kernel_own, kernel_other, *refs):
-    parts = refs[:n_parts]
-    acc = refs[n_parts] if accumulate else None
-    out = refs[-1]
-    total = acc[...] if accumulate else None
-    left = rows[...]
-    block = 2 * piece
-    index = 0
+def apply_parts(rows, parts, tile, total):
+    for t, ref in enumerate(parts):
+        columns = ref[...]
+        density = lax.dot_general(
+            rows, columns, (((1,), (1,)), ((), ())), preferred_element_type=F32
+        )
+        weighted = (density * tile(t).astype(F32)).astype(BF16)
+        term = jnp.dot(weighted, columns, preferred_element_type=F32)
+        total = term if total is None else total + term
+    return total
+
+
+def early_kernel(slots, later, piece, ids, rows, kernel, kernel_other, *refs):
+    *parts, out, packed, held, sems = refs
+    copies = {}
+    for k in range(4):
+        at = tile_at(ids[k], 4 * piece)
+        copies[k] = [
+            pltpu.make_async_copy(ref.at[:, at], held.at[k, h], sems.at[2 * k + h])
+            for h, ref in enumerate((kernel, kernel_other))
+        ]
+        for copy in copies[k]:
+            copy.start()
+
+    def halves(k, j):
+        for copy in copies.pop(k, ()):
+            copy.wait()
+        at = tile_at(ids[4 + j], piece)
+        return [held[k, h, :, at] for h in range(2)]
+
+    out[...] = apply_parts(
+        rows[...], parts, lambda t: jnp.concatenate([half for kj in slots[t] for half in halves(*kj)], axis=1), None
+    )
+    for t, kj in enumerate(later):
+        for h, half in enumerate(halves(*kj)):
+            packed[:, (2 * t + h) * piece : (2 * t + h + 1) * piece] = half
+
+
+def late_kernel(rows, packed, acc, tiles, *refs):
+    *parts, out, send = refs
+    ends = [0]
     for part in parts:
-        for b in range(part.shape[0] // block):
-            columns = part[b * block : (b + 1) * block, :]
-            at = pl.ds(pl.multiple_of(ids[index] * piece, piece), piece)
-            index += 1
-            density = lax.dot_general(
-                left, columns, (((1,), (1,)), ((), ())), preferred_element_type=F32
-            )
-            tile = jnp.concatenate([kernel_own[:, at], kernel_other[:, at]], axis=1)
-            weighted = (density * tile.astype(F32)).astype(BF16)
-            term = jnp.dot(weighted, columns, preferred_element_type=F32)
-            total = term if total is None else total + term
-    out[...] = total.astype(out.dtype)
-
-
-def apply_blocks(ids, rows, kernel_own, kernel_other, parts, acc, dtype, weight):
-    args = [ids, rows, kernel_own, kernel_other, *parts]
-    if acc is not None:
-        args.append(acc)
-    columns = sum(part.shape[0] for part in parts)
+        ends.append(ends[-1] + part.shape[0])
+    total = apply_parts(rows[...], parts, lambda t: packed[:, ends[t] : ends[t + 1]], acc[...])
+    result = total.astype(out.dtype)
+    out[...] = result
+    n = send.shape[0]
+    send[...] = jnp.dot(tiles[:n, :], result, preferred_element_type=F32).astype(send.dtype)
+
+
+def apply_early(ids, rows, kernel, kernel_other, parts, later):
     n, i = rows.shape
-    return pl.pallas_call(
-        functools.partial(apply_kernel, len(parts), kernel_own.shape[1] // 16, acc is not None),
-        out_shape=jax.ShapeDtypeStruct((n, i), dtype),
-        in_specs=[SMEM] + [VMEM] * (len(args) - 1),
-        out_specs=VMEM,
-        compiler_params=PARAMS,
-        cost_estimate=pl.CostEstimate(
-            flops=weight * 4 * n * i * columns, bytes_accessed=weight * 2 * columns * (n + i), transcendentals=0
-        ),
-    )(*args)
+    slots = tuple(tuple(part) for _, part in parts)
+    return pl.pallas_call(
+        functools.partial(early_kernel, slots, tuple(later), n // 2),
+        out_shape=[jax.ShapeDtypeStruct((n, i), F32), jax.ShapeDtypeStruct((n, n * len(later)), BF16)],
+        in_specs=[SMEM, VMEM, ANY, ANY] + [VMEM] * len(parts),
+        out_specs=[VMEM] * 2,
+        scratch_shapes=[pltpu.VMEM((4, 2, n, 2 * n), BF16), pltpu.SemaphoreType.DMA((8,))],
+        compiler_params=PARAMS,
+        cost_estimate=pin(60),
+    )(ids, rows, kernel, kernel_other, *[array for array, _ in parts])
+
+
+def apply_late(rows, packed, acc, tiles, parts):
+    n, i = rows.shape
+    m = tiles.shape[0] // 4
+    return pl.pallas_call(
+        late_kernel,
+        out_shape=[jax.ShapeDtypeStruct((n, i), BF16), jax.ShapeDtypeStruct((m, i), BF16)],
+        in_specs=[VMEM] * (4 + len(parts)),
+        out_specs=[VMEM] * 2,
+        compiler_params=PARAMS,
+        cost_estimate=pin(1),
+    )(rows, packed, acc, tiles, *parts)
 
 
 def project_kernel(start, tiles, applied, *outs):
@@ -158,6 +199,60 @@
         compiler_params=PARAMS,
         cost_estimate=pl.CostEstimate(flops=2 * rows * p * i, bytes_accessed=4 * rows * p, transcendentals=0),
     )(tiles, applied)
+
+
+def halve_kernel(keep, got, *outs):
+    start = 0
+    for out in outs:
+        m = slice(start, start + out.shape[0])
+        start = m.stop
+        out[...] = (keep[m, :] + got[m, :].astype(F32)).astype(out.dtype)
+
+
+def halve(keep, got, shapes):
+    return pl.pallas_call(
+        halve_kernel,
+        out_shape=[jax.ShapeDtypeStruct((n, keep.shape[1]), t) for n, t in shapes],
+        in_specs=[VMEM] * 2,
+        out_specs=[VMEM] * len(shapes),
+        compiler_params=PARAMS,
+        cost_estimate=pin(20),
+    )(keep, got)
+
+
+def collect_kernel(start, keep, got, more, *outs):
+    at = 0
+    for out in outs:
+        m, here = slice(start + at, start + at + out.shape[0]), slice(at, at + out.shape[0])
+        at = here.stop
+        out[...] = (keep[m, :] + got[m, :].astype(F32) + more[here, :].astype(F32)).astype(out.dtype)
+
+
+def collect(start, keep, got, more, shapes):
+    return pl.pallas_call(
+        functools.partial(collect_kernel, start),
+        out_shape=[jax.ShapeDtypeStruct((n, keep.shape[1]), t) for n, t in shapes],
+        in_specs=[VMEM] * 3,
+        out_specs=[VMEM] * len(shapes),
+        compiler_params=PARAMS,
+        cost_estimate=pin(20),
+    )(keep, got, more)
+
+
+def spins_kernel(core, result, partner, out):
+    out[:, pl.ds(core[0], 1), :] = result[...][:, None, :]
+    out[:, pl.ds(1 - core[0], 1), :] = partner[...][:, None, :]
+
+
+def both_spins(core, result, partner):
+    n, i = result.shape
+    return pl.pallas_call(
+        spins_kernel,
+        out_shape=jax.ShapeDtypeStruct((n, 2, i), F32),
+        in_specs=[SMEM, VMEM, VMEM],
+        out_specs=VMEM,
+        compiler_params=PARAMS,
+    )(core, result, partner)
 
 
 def box_body(orbitals, kernel, basis):
@@ -191,37 +286,41 @@
     z8 = plane(block, 2)
     p0 = join_blocks(block, x0)
     y0 = second(p0)
+    whole = join_blocks(p0, y0)
+    z4 = plane(whole, 1)
     z12 = plane(z8, 1)
     x8 = first(z8)
-    zp = plane(join_blocks(p0, y0), 1)
     x12 = first(z12)
-    p8 = join_blocks(z8, x8)
+    p8 = join_blocks(after(z8, whole), x8, weight=6)
     y8 = second(p8)
     p12 = join_blocks(z12, x12)
     y12 = second(p12)
-    kernel_other = swap(after(kernel, x8))
+
+    kernel_other = swap(after(kernel, x12))
+    order = (1, 2, 0, 3)
     tiles = turn_tiles(
-        ids(*[r ^ (near * a) ^ (far * b) ^ (4 * k) for a in (1, 0) for b in (1, 0) for k in range(4)]),
+        ids(*[r ^ (near * a) ^ (far * b) ^ (4 * k) for a in (1, 0) for b in (1, 0) for k in order]),
         after(basis, x12), width,
     )
-
-    around = lambda base: [base ^ d for d in (0, near, far, 3)]
-    halves = (rows, kernel, kernel_other)
-    acc = apply_blocks(ids(*around(r), *around(r ^ 8)), *halves, [p0, y0, p8, y8], None, F32, 20)
-    applied = apply_blocks(ids(*around(r ^ 4), *around(r ^ 12)), *halves, [zp, p12, y12], acc, BF16, 1)
-
-    n = 4 * width
-    (send_a,) = project(0, tiles, applied, [(n, BF16)])
+    places = ids(*[(r // 4) ^ k for k in range(4)], *[(r & 3) ^ d for d in (0, near, far, 3)])
+    at = lambda k, *js: [(k, j) for j in js]
+    acc, packed = apply_early(
+        places, rows, kernel, kernel_other,
+        [(p0, at(0, 0, 1)), (y0, at(0, 2, 3)), (p8, at(2, 0, 1)), (y8, at(2, 2, 3)), (p12, at(3, 0, 1))],
+        at(3, 2, 3) + at(1, 0, 1, 2, 3),
+    )
+    applied, send_a = apply_late(rows, packed, acc, tiles, [y12, z4])
+
+    n, pair = 4 * width, 2 * width
     send_b, keep_a, keep_b = project(n, tiles, applied, [(n, BF16), (n, F32), (n, F32)])
     got_a, got_b = first(send_a), first(send_b)
-    rest = second((keep_a + got_a.astype(F32)).astype(BF16)).astype(F32) + (keep_b + got_b.astype(F32))
-    result = rest[:width]
-    for k in (1, 2, 3):
-        result = result + plane(rest[k * width : (k + 1) * width].astype(BF16), k).astype(F32)
-    partner = swap(result)
-    return jnp.where(
-        c == 0, jnp.stack([result, partner], axis=1), jnp.stack([partner, result], axis=1)
-    )
+    high, low = halve(keep_a, got_a, [(pair, BF16)] * 2)
+    got_high, got_low = second(high), second(low)
+    to_0, to_1 = collect(0, keep_b, got_b, got_high, [(width, BF16)] * 2)
+    from_0, from_1 = plane(to_0, order[0]), plane(to_1, order[1])
+    rest, to_3 = collect(pair, keep_b, got_b, got_low, [(width, F32), (width, BF16)])
+    result = rest + plane(to_3, order[3]).astype(F32) + from_0.astype(F32) + from_1.astype(F32)
+    return both_spins(ids(c), result, swap(result))
 
 
 def solution(mesh):

time: 63.3 us -> 57.3 us (0.905)
  waiting for transfers between devices: 33.3 us -> 25.2 us
  starting transfers between devices: 22.5 us -> 24.6 us
  Pallas kernels: 4.92 us -> 6.09 us
  local copies, waits for them, and re-layouts: 2.11 us -> 1.1 us
    ppermute x15 -> x16, waiting for transfers between devices: 31.1 us -> 22.9 us  [send(): return lax.ppermute(a, ('row', 'col'), pairs)]
    ppermute x15 -> x16, starting transfers between devices: 21.9 us -> 24 us  [send(): return lax.ppermute(a, ('row', 'col'), pairs)]
    pallas_call x2 -> x6, Pallas kernels: 2.99 us -> 4.38 us  [the longest x1 2.44 us: apply_early(): pl.pallas_call(functools.partial(early_kernel, slots, tuple(later), n //...]
    select_n x1 -> x0, local copies, waits for them, and re-layouts: 0.91 us -> none  [box_body(): jnp.where(c == 0, jnp.stack([result, partner], axis=1), jnp.stack([partne...]
  transfers between devices with their start and end apart: 18 -> 19, of which waited for: 14 -> 14; matrix products, arithmetic and copies ran while one was open for 1% -> 0% of each run, Pallas kernels for 4% -> 7%
where the time goes in v3:
time: 57.3 us; the launch traced here: 57.1 us
  waiting for transfers between devices  25.2 us (44%)
  starting transfers between devices  24.6 us (43%)
  Pallas kernels  6.09 us (11%)
  local copies, waits for them, and re-layouts  1.1 us (2%)
    ppermute x16, starting transfers between devices, send(): return lax.ppermute(a, ('row', 'col'), pairs)  24 us
    ppermute x16, waiting for transfers between devices, send(): return lax.ppermute(a, ('row', 'col'), pairs)  22.9 us
    pallas_call x1, Pallas kernels, apply_early(): pl.pallas_call(functools.partial(early_kernel, slots, tuple(later), n //...  2.44 us
    ppermute x3, waiting for transfers between devices, box_body(): swap = lambda a: lax.ppermute(a, 'col', [(0, 1), (1, 0)])  2.23 us
  transfers between devices with their start and end apart: 19, of which 14 were waited for; matrix products, arithmetic and copies ran while one was open for 0% of the time, Pallas kernels for 7%

profile of v3, /device:TPU:0, one launch (start us, length us, event | category | flops | bytes accessed | tf_op | source)
XLA Modules:
  0.0 57.1 jit_solution(8102058935531276096)
XLA Ops:
  0.0 0.9 %copy-done.1 = bf16[128,2,256]{2,1,0:T(2,128)(2,1)S(1)} copy-done((bf16[128,2,256]{2,1,0:T(2,128)(2,1)S(1)}, bf16[128,2,256]{2,1,0:T(2,128)(2,1)}, u32[]{:S(2)}) %copy-start.1) | copy-done | bytes 131096
  2.8 2.9 %collective-permute-start.5 = (bf16[256,256]{1,0:T(8,128)(2,1)S(1)}, bf16[256,256]{1,0:T(8,128)(2,1)S(1)}, u32[]{:S(2)}, u32[]{:S(2)}) collective-permute-start(bf16[256,256]{1,0:T(8,128)(2,1)S(1)} %constant_dynamic-update-slice_fusion.refs_0_), channel_id=1, source_target_pairs={{0,2},{1,5},{2,0},{3,7},{4,6},{5,1},{6,4},{7,3},{8,10},{9,13},{10,... | collective-permute-start | bytes 393224 | tf_op jit(solution)/shard_map/ppermute | solution.py:266
  5.7 2.6 %collective-permute-start.1 = (bf16[256,256]{1,0:T(8,128)(2,1)S(1)}, bf16[256,256]{1,0:T(8,128)(2,1)S(1)}, u32[]{:S(2)}, u32[]{:S(2)}) collective-permute-start(bf16[256,256]{1,0:T(8,128)(2,1)S(1)} %constant_dynamic-update-slice_fusion.refs_0_), channel_id=1, source_target_pairs={{0,16},{1,17},{2,18},{3,19},{4,20},{5,21},{6,22},{7,23},{8,24},{9,... | collective-permute-start | bytes 393224 | tf_op jit(solution)/shard_map/ppermute | solution.py:266
  8.6 2.1 %collective-permute-start.6 = (bf16[512,256]{1,0:T(8,128)(2,1)S(1)}, bf16[512,256]{1,0:T(8,128)(2,1)S(1)}, u32[]{:S(2)}, u32[]{:S(2)}) collective-permute-start(bf16[512,256]{1,0:T(8,128)(2,1)S(1)} %shard_map.39.refs_0_), channel_id=1, source_target_pairs={{0,4},{1,3},{2,6},{3,1},{4,0},{5,7},{6,2},{7,5},{8,12},{9,11},{10,... | collective-permute-start | bytes 786440 | tf_op jit(solution)/shard_map/ppermute | solution.py:266
  10.7 3.9 %collective-permute-done.1.refs_0_ = bf16[256,256]{1,0:T(8,128)(2,1)S(1)} collective-permute-done((bf16[256,256]{1,0:T(8,128)(2,1)S(1)}, bf16[256,256]{1,0:T(8,128)(2,1)S(1)}, u32[]{:S(2)}, u32[]{:S(2)}) %collective-permute-start.1) | collective-permute-done | bytes 131104 | tf_op jit(solution)/shard_map/ppermute | solution.py:266
  15.5 1.6 %collective-permute-start.7 = (bf16[256,256]{1,0:T(8,128)(2,1)S(1)}, bf16[256,256]{1,0:T(8,128)(2,1)S(1)}, u32[]{:S(2)}, u32[]{:S(2)}) collective-permute-start(bf16[256,256]{1,0:T(8,128)(2,1)S(1)} %collective-permute-done.1.refs_0_), channel_id=1, source_target_pairs={{0,2},{1,5},{2,0},{3,7},{4,6},{5,1},{6,4},{7,3},{8,10},{9,13},{10,... | collective-permute-start | bytes 393224 | tf_op jit(solution)/shard_map/ppermute | solution.py:266
  17.1 2.6 %collective-permute-done.2.refs_0_ = bf16[256,256]{1,0:T(8,128)(2,1)S(1)} collective-permute-done((bf16[256,256]{1,0:T(8,128)(2,1)S(1)}, bf16[256,256]{1,0:T(8,128)(2,1)S(1)}, u32[]{:S(2)}, u32[]{:S(2)}) %collective-permute-start.2) | collective-permute-done | bytes 131104 | tf_op jit(solution)/shard_map/ppermute | solution.py:266
  19.6 1.6 %collective-permute-start.3 = (bf16[256,256]{1,0:T(8,128)(2,1)S(1)}, bf16[256,256]{1,0:T(8,128)(2,1)S(1)}, u32[]{:S(2)}, u32[]{:S(2)}) collective-permute-start(bf16[256,256]{1,0:T(8,128)(2,1)S(1)} %collective-permute-done.2.refs_0_), channel_id=1, source_target_pairs={{0,2},{1,5},{2,0},{3,7},{4,6},{5,1},{6,4},{7,3},{8,10},{9,13},{10,... | collective-permute-start | bytes 393224 | tf_op jit(solution)/shard_map/ppermute | solution.py:266
  21.3 1.2 %collective-permute-start.10 = (bf16[1024,256]{1,0:T(8,128)(2,1)S(1)}, bf16[1024,256]{1,0:T(8,128)(2,1)S(1)}, u32[]{:S(2)}, u32[]{:S(2)}) collective-permute-start(bf16[1024,256]{1,0:T(8,128)(2,1)S(1)} %shard_map.40), channel_id=1, source_target_pairs={{0,8},{1,9},{2,10},{3,11},{4,12},{5,13},{6,14},{7,15},{8,0},{9,1},... | collective-permute-start | bytes 1572872 | tf_op jit(solution)/shard_map/ppermute | solution.py:266
  23.0 3.0 %collective-permute-done.3.refs_1_ = bf16[256,256]{1,0:T(8,128)(2,1)S(1)} collective-permute-done((bf16[256,256]{1,0:T(8,128)(2,1)S(1)}, bf16[256,256]{1,0:T(8,128)(2,1)S(1)}, u32[]{:S(2)}, u32[]{:S(2)}) %collective-permute-start.3) | collective-permute-done | bytes 131104 | tf_op jit(solution)/shard_map/ppermute | solution.py:266
  27.0 2.0 %collective-permute-done.8.refs_3_ = bf16[512,256]{1,0:T(8,128)(2,1)S(1)} collective-permute-done((bf16[512,256]{1,0:T(8,128)(2,1)S(1)}, bf16[512,256]{1,0:T(8,128)(2,1)S(1)}, u32[]{:S(2)}, u32[]{:S(2)}) %collective-permute-start.8) | collective-permute-done | bytes 262176 | tf_op jit(solution)/shard_map/ppermute | solution.py:266
  28.9 2.4 %shard_map.43 = (f32[256,256]{1,0:T(8,128)S(1)}, bf16[256,1536]{1,0:T(8,128)(2,1)S(1)}) custom-call(s32[8]{0:T(128)S(1)} %stack.108.ids, bf16[256,256]{1,0:T(8,128)(2,1)S(1)} %maximum_select_fusion.rows, bf16[256,2048]{1,0:T(8,128)(2,1)S(1)} %copy-done.2, bf16[256,2048]{1,0:T(8,128)(2,1)S(1)} %collective-permute-done.4.kernel_other, ...), custom_call_target="tpu_custom_call" | custom-call | flops 60000002048 | bytes 1000000 | tf_op jit(solution)/shard_map/pallas_call | solution.py:159
  31.4 1.0 %collective-permute-done.9.refs_0_ = bf16[512,256]{1,0:T(8,128)(2,1)S(1)} collective-permute-done((bf16[512,256]{1,0:T(8,128)(2,1)S(1)}, bf16[512,256]{1,0:T(8,128)(2,1)S(1)}, u32[]{:S(2)}, u32[]{:S(2)}) %collective-permute-start.9) | collective-permute-done | bytes 262176 | tf_op jit(solution)/shard_map/ppermute | solution.py:266
  32.4 1.0 %shard_map.44 = (bf16[256,256]{1,0:T(8,128)(2,1)S(1)}, bf16[512,256]{1,0:T(8,128)(2,1)S(1)}) custom-call(bf16[256,256]{1,0:T(8,128)(2,1)S(1)} %maximum_select_fusion.rows, bf16[256,1536]{1,0:T(8,128)(2,1)S(1)} %get-tuple-element.32.packed, f32[256,256]{1,0:T(8,128)S(1)} %get-tuple-element.33.acc, bf16[2048,256]{1,0:T(8,128)(2,1)S(1)} %shard_map.38.tiles, ...), custom_call_target="tpu_custom_call" | custom-call | flops 1000000000 | bytes 1000000 | tf_op jit(solution)/shard_map/pallas_call | solution.py:173
  33.5 2.1 %collective-permute-start.12 = (bf16[512,256]{1,0:T(8,128)(2,1)S(1)}, bf16[512,256]{1,0:T(8,128)(2,1)S(1)}, u32[]{:S(2)}, u32[]{:S(2)}) collective-permute-start(bf16[512,256]{1,0:T(8,128)(2,1)S(1)} %get-tuple-element.38), channel_id=1, source_target_pairs={{0,2},{1,5},{2,0},{3,7},{4,6},{5,1},{6,4},{7,3},{8,10},{9,13},{10,... | collective-permute-start | bytes 786440 | tf_op jit(solution)/shard_map/ppermute | solution.py:266
  36.0 3.9 %collective-permute-done.12.got = bf16[512,256]{1,0:T(8,128)(2,1)S(1)} collective-permute-done((bf16[512,256]{1,0:T(8,128)(2,1)S(1)}, bf16[512,256]{1,0:T(8,128)(2,1)S(1)}, u32[]{:S(2)}, u32[]{:S(2)}) %collective-permute-start.12) | collective-permute-done | bytes 262176 | tf_op jit(solution)/shard_map/ppermute | solution.py:266
  40.0 1.8 %collective-permute-start.13 = (bf16[256,256]{1,0:T(8,128)(2,1)S(1)}, bf16[256,256]{1,0:T(8,128)(2,1)S(1)}, u32[]{:S(2)}, u32[]{:S(2)}) collective-permute-start(bf16[256,256]{1,0:T(8,128)(2,1)S(1)} %get-tuple-element.39), channel_id=1, source_target_pairs={{0,4},{1,3},{2,6},{3,1},{4,0},{5,7},{6,2},{7,5},{8,12},{9,11},{10,... | collective-permute-start | bytes 393224 | tf_op jit(solution)/shard_map/ppermute | solution.py:266
  42.0 1.9 %collective-permute-done.11.got = bf16[512,256]{1,0:T(8,128)(2,1)S(1)} collective-permute-done((bf16[512,256]{1,0:T(8,128)(2,1)S(1)}, bf16[512,256]{1,0:T(8,128)(2,1)S(1)}, u32[]{:S(2)}, u32[]{:S(2)}) %collective-permute-start.11) | collective-permute-done | bytes 262176 | tf_op jit(solution)/shard_map/ppermute | solution.py:266
  43.9 1.0 %collective-permute-done.13.more = bf16[256,256]{1,0:T(8,128)(2,1)S(1)} collective-permute-done((bf16[256,256]{1,0:T(8,128)(2,1)S(1)}, bf16[256,256]{1,0:T(8,128)(2,1)S(1)}, u32[]{:S(2)}, u32[]{:S(2)}) %collective-permute-start.13) | collective-permute-done | bytes 131104 | tf_op jit(solution)/shard_map/ppermute | solution.py:266
  45.0 4.3 %collective-permute-start.14 = (bf16[128,256]{1,0:T(8,128)(2,1)S(1)}, bf16[128,256]{1,0:T(8,128)(2,1)S(1)}, u32[]{:S(2)}, u32[]{:S(2)}) collective-permute-start(bf16[128,256]{1,0:T(8,128)(2,1)S(1)} %get-tuple-element.41), channel_id=1, source_target_pairs={{0,24},{1,25},{2,26},{3,27},{4,28},{5,29},{6,30},{7,31},{8,16},{9,... | collective-permute-start | bytes 196616 | tf_op jit(solution)/shard_map/ppermute | solution.py:266
  49.5 2.2 %collective-permute-start.17 = (bf16[128,256]{1,0:T(8,128)(2,1)S(1)}, bf16[128,256]{1,0:T(8,128)(2,1)S(1)}, u32[]{:S(2)}, u32[]{:S(2)}) collective-permute-start(bf16[128,256]{1,0:T(8,128)(2,1)S(1)} %get-tuple-element.44), channel_id=1, source_target_pairs={{0,16},{1,17},{2,18},{3,19},{4,20},{5,21},{6,22},{7,23},{8,24},{9,... | collective-permute-start | bytes 196616 | tf_op jit(solution)/shard_map/ppermute | solution.py:266
  52.0 1.7 %collective-permute-done.16 = bf16[128,256]{1,0:T(8,128)(2,1)S(1)} collective-permute-done((bf16[128,256]{1,0:T(8,128)(2,1)S(1)}, bf16[128,256]{1,0:T(8,128)(2,1)S(1)}, u32[]{:S(2)}, u32[]{:S(2)}) %collective-permute-start.16) | collective-permute-done | bytes 65568 | tf_op jit(solution)/shard_map/ppermute | solution.py:266
  53.7 1.2 %collective-permute-done.17 = bf16[128,256]{1,0:T(8,128)(2,1)S(1)} collective-permute-done((bf16[128,256]{1,0:T(8,128)(2,1)S(1)}, bf16[128,256]{1,0:T(8,128)(2,1)S(1)}, u32[]{:S(2)}, u32[]{:S(2)}) %collective-permute-start.17) | collective-permute-done | bytes 65568 | tf_op jit(solution)/shard_map/ppermute | solution.py:266
  55.0 1.3 %collective-permute-done.18.partner = f32[128,256]{1,0:T(8,128)S(1)} collective-permute-done((f32[128,256]{1,0:T(8,128)S(1)}, f32[128,256]{1,0:T(8,128)S(1)}, u32[]{:S(2)}, u32[]{:S(2)}) %collective-permute-start.18) | collective-permute-done | bytes 131104 | tf_op jit(solution)/shard_map/ppermute | solution.py:271
  (39 shorter events, 6.8 us)
Async XLA Ops:
  0.0 0.9 %copy-start.1 = (bf16[128,2,256]{2,1,0:T(2,128)(2,1)S(1)}, bf16[128,2,256]{2,1,0:T(2,128)(2,1)}, u32[]{:S(2)}) copy-start(bf16[128,2,256]{2,1,0:T(2,128)(2,1)} %orbitals.1) | copy-start | bytes 393220
  1.3 1.4 %collective-permute-start = (bf16[128,256]{1,0:T(8,128)(2,1)S(1)}, bf16[128,256]{1,0:T(8,128)(2,1)S(1)}, u32[]{:S(2)}, u32[]{:S(2)}) collective-permute-start(bf16[128,256]{1,0:T(8,128)(2,1)S(1)} %get-tuple-element.26), channel_id=1, source_target_pairs={{0,1},{1,0},{2,3},{3,2},{4,5},{5,4},{6,7},{7,6},{8,9},{9,8},{10,11... | collective-permute-start | bytes 196616 | tf_op jit(solution)/shard_map/ppermute | solution.py:271
  2.8 5.9 %collective-permute-start.5 = (bf16[256,256]{1,0:T(8,128)(2,1)S(1)}, bf16[256,256]{1,0:T(8,128)(2,1)S(1)}, u32[]{:S(2)}, u32[]{:S(2)}) collective-permute-start(bf16[256,256]{1,0:T(8,128)(2,1)S(1)} %constant_dynamic-update-slice_fusion.refs_0_), channel_id=1, source_target_pairs={{0,2},{1,5},{2,0},{3,7},{4,6},{5,1},{6,4},{7,3},{8,10},{9,13},{10,... | collective-permute-start | bytes 393224 | tf_op jit(solution)/shard_map/ppermute | solution.py:266
  5.7 9.0 %collective-permute-start.1 = (bf16[256,256]{1,0:T(8,128)(2,1)S(1)}, bf16[256,256]{1,0:T(8,128)(2,1)S(1)}, u32[]{:S(2)}, u32[]{:S(2)}) collective-permute-start(bf16[256,256]{1,0:T(8,128)(2,1)S(1)} %constant_dynamic-update-slice_fusion.refs_0_), channel_id=1, source_target_pairs={{0,16},{1,17},{2,18},{3,19},{4,20},{5,21},{6,22},{7,23},{8,24},{9,... | collective-permute-start | bytes 393224 | tf_op jit(solution)/shard_map/ppermute | solution.py:266
  8.6 12.6 %collective-permute-start.6 = (bf16[512,256]{1,0:T(8,128)(2,1)S(1)}, bf16[512,256]{1,0:T(8,128)(2,1)S(1)}, u32[]{:S(2)}, u32[]{:S(2)}) collective-permute-start(bf16[512,256]{1,0:T(8,128)(2,1)S(1)} %shard_map.39.refs_0_), channel_id=1, source_target_pairs={{0,4},{1,3},{2,6},{3,1},{4,0},{5,7},{6,2},{7,5},{8,12},{9,11},{10,... | collective-permute-start | bytes 786440 | tf_op jit(solution)/shard_map/ppermute | solution.py:266
  14.7 5.0 %collective-permute-start.2 = (bf16[256,256]{1,0:T(8,128)(2,1)S(1)}, bf16[256,256]{1,0:T(8,128)(2,1)S(1)}, u32[]{:S(2)}, u32[]{:S(2)}) collective-permute-start(bf16[256,256]{1,0:T(8,128)(2,1)S(1)} %collective-permute-done.1.refs_0_), channel_id=1, source_target_pairs={{0,8},{1,9},{2,10},{3,11},{4,12},{5,13},{6,14},{7,15},{8,0},{9,1},... | collective-permute-start | bytes 393224 | tf_op jit(solution)/shard_map/ppermute | solution.py:266
  15.5 6.9 %collective-permute-start.7 = (bf16[256,256]{1,0:T(8,128)(2,1)S(1)}, bf16[256,256]{1,0:T(8,128)(2,1)S(1)}, u32[]{:S(2)}, u32[]{:S(2)}) collective-permute-start(bf16[256,256]{1,0:T(8,128)(2,1)S(1)} %collective-permute-done.1.refs_0_), channel_id=1, source_target_pairs={{0,2},{1,5},{2,0},{3,7},{4,6},{5,1},{6,4},{7,3},{8,10},{9,13},{10,... | collective-permute-start | bytes 393224 | tf_op jit(solution)/shard_map/ppermute | solution.py:266
  19.6 6.3 %collective-permute-start.3 = (bf16[256,256]{1,0:T(8,128)(2,1)S(1)}, bf16[256,256]{1,0:T(8,128)(2,1)S(1)}, u32[]{:S(2)}, u32[]{:S(2)}) collective-permute-start(bf16[256,256]{1,0:T(8,128)(2,1)S(1)} %collective-permute-done.2.refs_0_), channel_id=1, source_target_pairs={{0,2},{1,5},{2,0},{3,7},{4,6},{5,1},{6,4},{7,3},{8,10},{9,13},{10,... | collective-permute-start | bytes 393224 | tf_op jit(solution)/shard_map/ppermute | solution.py:266
  21.3 4.7 %copy-start.2 = (bf16[256,2048]{1,0:T(8,128)(2,1)S(1)}, bf16[256,2048]{1,0:T(8,128)(2,1)}, u32[]{:S(2)}) copy-start(bf16[256,2048]{1,0:T(8,128)(2,1)} %kernel.1) | copy-start | bytes 3145732
  21.3 11.1 %collective-permute-start.10 = (bf16[1024,256]{1,0:T(8,128)(2,1)S(1)}, bf16[1024,256]{1,0:T(8,128)(2,1)S(1)}, u32[]{:S(2)}, u32[]{:S(2)}) collective-permute-start(bf16[1024,256]{1,0:T(8,128)(2,1)S(1)} %shard_map.40), channel_id=1, source_target_pairs={{0,8},{1,9},{2,10},{3,11},{4,12},{5,13},{6,14},{7,15},{8,0},{9,1},... | collective-permute-start | bytes 1572872 | tf_op jit(solution)/shard_map/ppermute | solution.py:266
  22.5 3.6 %copy-start = (bf16[256,2048]{1,0:T(8,128)(2,1)S(1)}, bf16[256,2048]{1,0:T(8,128)(2,1)}, u32[]{:S(2)}) copy-start(bf16[256,2048]{1,0:T(8,128)(2,1)} %basis) | copy-start | bytes 3145732
  22.5 6.4 %collective-permute-start.8 = (bf16[512,256]{1,0:T(8,128)(2,1)S(1)}, bf16[512,256]{1,0:T(8,128)(2,1)S(1)}, u32[]{:S(2)}, u32[]{:S(2)}) collective-permute-start(bf16[512,256]{1,0:T(8,128)(2,1)S(1)} %shard_map.41.refs_2_), channel_id=1, source_target_pairs={{0,4},{1,3},{2,6},{3,1},{4,0},{5,7},{6,2},{7,5},{8,12},{9,11},{10,... | collective-permute-start | bytes 786440 | tf_op jit(solution)/shard_map/ppermute | solution.py:266
  26.0 3.0 %collective-permute-start.4 = (bf16[256,2048]{1,0:T(8,128)(2,1)S(1)}, bf16[256,2048]{1,0:T(8,128)(2,1)S(1)}, u32[]{:S(2)}, u32[]{:S(2)}) collective-permute-start(bf16[256,2048]{1,0:T(8,128)(2,1)S(1)} %copy-done.2), channel_id=1, source_target_pairs={{0,1},{1,0},{2,3},{3,2},{4,5},{5,4},{6,7},{7,6},{8,9},{9,8},{10,11... | collective-permute-start | bytes 3145736 | tf_op jit(solution)/shard_map/ppermute | solution.py:271
  26.0 6.4 %collective-permute-start.9 = (bf16[512,256]{1,0:T(8,128)(2,1)S(1)}, bf16[512,256]{1,0:T(8,128)(2,1)S(1)}, u32[]{:S(2)}, u32[]{:S(2)}) collective-permute-start(bf16[512,256]{1,0:T(8,128)(2,1)S(1)} %shard_map.42.refs_4_), channel_id=1, source_target_pairs={{0,4},{1,3},{2,6},{3,1},{4,0},{5,7},{6,2},{7,5},{8,12},{9,11},{10,... | collective-permute-start | bytes 786440 | tf_op jit(solution)/shard_map/ppermute | solution.py:266
  33.5 6.4 %collective-permute-start.12 = (bf16[512,256]{1,0:T(8,128)(2,1)S(1)}, bf16[512,256]{1,0:T(8,128)(2,1)S(1)}, u32[]{:S(2)}, u32[]{:S(2)}) collective-permute-start(bf16[512,256]{1,0:T(8,128)(2,1)S(1)} %get-tuple-element.38), channel_id=1, source_target_pairs={{0,2},{1,5},{2,0},{3,7},{4,6},{5,1},{6,4},{7,3},{8,10},{9,13},{10,... | collective-permute-start | bytes 786440 | tf_op jit(solution)/shard_map/ppermute | solution.py:266
  35.9 8.0 %collective-permute-start.11 = (bf16[512,256]{1,0:T(8,128)(2,1)S(1)}, bf16[512,256]{1,0:T(8,128)(2,1)S(1)}, u32[]{:S(2)}, u32[]{:S(2)}) collective-permute-start(bf16[512,256]{1,0:T(8,128)(2,1)S(1)} %get-tuple-element.36), channel_id=1, source_target_pairs={{0,2},{1,5},{2,0},{3,7},{4,6},{5,1},{6,4},{7,3},{8,10},{9,13},{10,... | collective-permute-start | bytes 786440 | tf_op jit(solution)/shard_map/ppermute | solution.py:266
  40.0 5.0 %collective-permute-start.13 = (bf16[256,256]{1,0:T(8,128)(2,1)S(1)}, bf16[256,256]{1,0:T(8,128)(2,1)S(1)}, u32[]{:S(2)}, u32[]{:S(2)}) collective-permute-start(bf16[256,256]{1,0:T(8,128)(2,1)S(1)} %get-tuple-element.39), channel_id=1, source_target_pairs={{0,4},{1,3},{2,6},{3,1},{4,0},{5,7},{6,2},{7,5},{8,12},{9,11},{10,... | collective-permute-start | bytes 393224 | tf_op jit(solution)/shard_map/ppermute | solution.py:266
  41.8 7.6 %collective-permute-start.15 = (bf16[256,256]{1,0:T(8,128)(2,1)S(1)}, bf16[256,256]{1,0:T(8,128)(2,1)S(1)}, u32[]{:S(2)}, u32[]{:S(2)}) collective-permute-start(bf16[256,256]{1,0:T(8,128)(2,1)S(1)} %get-tuple-element.42), channel_id=1, source_target_pairs={{0,4},{1,3},{2,6},{3,1},{4,0},{5,7},{6,2},{7,5},{8,12},{9,11},{10,... | collective-permute-start | bytes 393224 | tf_op jit(solution)/shard_map/ppermute | solution.py:266
  45.0 7.0 %collective-permute-start.14 = (bf16[128,256]{1,0:T(8,128)(2,1)S(1)}, bf16[128,256]{1,0:T(8,128)(2,1)S(1)}, u32[]{:S(2)}, u32[]{:S(2)}) collective-permute-start(bf16[128,256]{1,0:T(8,128)(2,1)S(1)} %get-tuple-element.41), channel_id=1, source_target_pairs={{0,24},{1,25},{2,26},{3,27},{4,28},{5,29},{6,30},{7,31},{8,16},{9,... | collective-permute-start | bytes 196616 | tf_op jit(solution)/shard_map/ppermute | solution.py:266
  49.4 4.3 %collective-permute-start.16 = (bf16[128,256]{1,0:T(8,128)(2,1)S(1)}, bf16[128,256]{1,0:T(8,128)(2,1)S(1)}, u32[]{:S(2)}, u32[]{:S(2)}) collective-permute-start(bf16[128,256]{1,0:T(8,128)(2,1)S(1)} %get-tuple-element.43), channel_id=1, source_target_pairs={{0,8},{1,9},{2,10},{3,11},{4,12},{5,13},{6,14},{7,15},{8,0},{9,1},... | collective-permute-start | bytes 196616 | tf_op jit(solution)/shard_map/ppermute | solution.py:266
  49.5 5.4 %collective-permute-start.17 = (bf16[128,256]{1,0:T(8,128)(2,1)S(1)}, bf16[128,256]{1,0:T(8,128)(2,1)S(1)}, u32[]{:S(2)}, u32[]{:S(2)}) collective-permute-start(bf16[128,256]{1,0:T(8,128)(2,1)S(1)} %get-tuple-element.44), channel_id=1, source_target_pairs={{0,16},{1,17},{2,18},{3,19},{4,20},{5,21},{6,22},{7,23},{8,24},{9,... | collective-permute-start | bytes 196616 | tf_op jit(solution)/shard_map/ppermute | solution.py:266
  54.9 1.4 %collective-permute-start.18 = (f32[128,256]{1,0:T(8,128)S(1)}, f32[128,256]{1,0:T(8,128)S(1)}, u32[]{:S(2)}, u32[]{:S(2)}) collective-permute-start(f32[128,256]{1,0:T(8,128)S(1)} %convert_add_fusion.result), channel_id=1, source_target_pairs={{0,1},{1,0},{2,3},{3,2},{4,5},{5,4},{6,7},{7,6},{8,9},{9,8},{10,11... | collective-permute-start | bytes 393224 | tf_op jit(solution)/shard_map/ppermute | solution.py:271

commit v4 on v3

--- a/solution.py
+++ b/solution.py
@@ -57,7 +57,7 @@
     other[...] = jnp.where(first_core, one, zero)
 
 
-def split_spins(core, orbitals):
+def split_spins(core, orbitals, weight):
     p, _, i = orbitals.shape
     return pl.pallas_call(
         split_kernel,
@@ -65,6 +65,7 @@
         in_specs=[SMEM, VMEM],
         out_specs=[VMEM] * 2,
         compiler_params=PARAMS,
+        cost_estimate=pin(weight),
     )(core, orbitals)
 
 
@@ -277,23 +278,29 @@
 
     near, far = 1 + c, 2 - c
 
-    own, other = split_spins(ids(c), orbitals)
+    core = ids(c)
+    raw8 = plane(orbitals, 2)
+    own, other = split_spins(core, orbitals, 0)
     other = swap(other)
     block = join(own, other)
     rows = jnp.where(c == 0, block, join(other, own))
     block, rows = lax.optimization_barrier((block, rows))
+
+    own8, other8 = split_spins(core, raw8, 20)
     x0 = first(block)
-    z8 = plane(block, 2)
-    p0 = join_blocks(block, x0)
+    p0 = join_blocks(after(block, own8), x0, weight=6)
     y0 = second(p0)
     whole = join_blocks(p0, y0)
+    raw12 = plane(after(raw8, p0), 1)
+    z8 = join_blocks(own8, swap(other8), weight=2)
+    own12, other12 = split_spins(core, raw12, 6)
+    z12 = join_blocks(own12, swap(other12), weight=6)
+    x8 = first(z8)
     z4 = plane(whole, 1)
-    z12 = plane(z8, 1)
-    x8 = first(z8)
-    x12 = first(z12)
+    x12 = first(after(z12, whole))
     p8 = join_blocks(after(z8, whole), x8, weight=6)
+    p12 = join_blocks(z12, x12)
     y8 = second(p8)
-    p12 = join_blocks(z12, x12)
     y12 = second(p12)
 
     kernel_other = swap(after(kernel, x12))
@@ -312,7 +319,8 @@
     applied, send_a = apply_late(rows, packed, acc, tiles, [y12, z4])
 
     n, pair = 4 * width, 2 * width
-    send_b, keep_a, keep_b = project(n, tiles, applied, [(n, BF16), (n, F32), (n, F32)])
+    (send_b,) = project(n, tiles, applied, [(n, BF16)])
+    keep_a, keep_b = project(2 * n, tiles, applied, [(n, F32), (n, F32)])
     got_a, got_b = first(send_a), first(send_b)
     high, low = halve(keep_a, got_a, [(pair, BF16)] * 2)
     got_high, got_low = second(high), second(low)
@@ -320,7 +328,7 @@
     from_0, from_1 = plane(to_0, order[0]), plane(to_1, order[1])
     rest, to_3 = collect(pair, keep_b, got_b, got_low, [(width, F32), (width, BF16)])
     result = rest + plane(to_3, order[3]).astype(F32) + from_0.astype(F32) + from_1.astype(F32)
-    return both_spins(ids(c), result, swap(result))
+    return both_spins(core, result, swap(result))
 
 
 def solution(mesh):

time: 57.3 us -> 56.9 us (level)
  waiting for transfers between devices: 25.2 us -> 23.7 us
  Pallas kernels: 6.09 us -> 7.03 us
    ppermute x16, waiting for transfers between devices: 22.9 us -> 20.9 us  [send(): return lax.ppermute(a, ('row', 'col'), pairs)]
    pallas_call x1 -> x3, Pallas kernels: 0.38 us -> 1.15 us  [split_spins(): pl.pallas_call(split_kernel, out_shape=[jax.ShapeDtypeStruct((p, i), orbi...]
    ppermute x3 -> x5, waiting for transfers between devices: 2.23 us -> 2.72 us  [box_body(): swap = lambda a: lax.ppermute(a, 'col', [(0, 1), (1, 0)])]
  transfers between devices with their start and end apart: 19 -> 21, of which waited for: 14 -> 17; matrix products, arithmetic and copies ran while one was open for 0% -> 0% of each run, Pallas kernels for 7% -> 9%
where the time goes in v4:
time: 56.9 us; the launch traced here: 56.8 us
  starting transfers between devices  24.7 us (43%)
  waiting for transfers between devices  23.7 us (42%)
  Pallas kernels  7.03 us (12%)
  local copies, waits for them, and re-layouts  1.14 us (2%)
    ppermute x16, starting transfers between devices, send(): return lax.ppermute(a, ('row', 'col'), pairs)  24.4 us
    ppermute x16, waiting for transfers between devices, send(): return lax.ppermute(a, ('row', 'col'), pairs)  20.9 us
    ppermute x5, waiting for transfers between devices, box_body(): swap = lambda a: lax.ppermute(a, 'col', [(0, 1), (1, 0)])  2.72 us
    pallas_call x1, Pallas kernels, apply_early(): pl.pallas_call(functools.partial(early_kernel, slots, tuple(later), n //...  2.44 us
    pallas_call x3, Pallas kernels, split_spins(): pl.pallas_call(split_kernel, out_shape=[jax.ShapeDtypeStruct((p, i), orbi...  1.15 us
  transfers between devices with their start and end apart: 21, of which 17 were waited for; matrix products, arithmetic and copies ran while one was open for 0% of the time, Pallas kernels for 9%

profile of v4, /device:TPU:0, one launch (start us, length us, event | category | flops | bytes accessed | tf_op | source)
XLA Modules:
  0.0 56.8 jit_solution(17914114930018402116)
XLA Ops:
  0.0 4.0 %collective-permute-start = (bf16[128,2,256]{2,1,0:T(2,128)(2,1)}, bf16[128,2,256]{2,1,0:T(2,128)(2,1)S(1)}, u32[]{:S(2)}, u32[]{:S(2)}) collective-permute-start(bf16[128,2,256]{2,1,0:T(2,128)(2,1)} %orbitals.1), channel_id=1, source_target_pairs={{0,16},{1,17},{2,18},{3,19},{4,20},{5,21},{6,22},{7,23},{8,24},{9,... | collective-permute-start | bytes 393224 | tf_op jit(solution)/shard_map/ppermute | solution.py:267
  5.5 1.2 %collective-permute-done.1 = bf16[128,256]{1,0:T(8,128)(2,1)S(1)} collective-permute-done((bf16[128,256]{1,0:T(8,128)(2,1)S(1)}, bf16[128,256]{1,0:T(8,128)(2,1)S(1)}, u32[]{:S(2)}, u32[]{:S(2)}) %collective-permute-start.1) | collective-permute-done | bytes 65568 | tf_op jit(solution)/shard_map/ppermute | solution.py:272
  6.7 1.6 %collective-permute-start.2 = (bf16[256,256]{1,0:T(8,128)(2,1)S(1)}, bf16[256,256]{1,0:T(8,128)(2,1)S(1)}, u32[]{:S(2)}, u32[]{:S(2)}) collective-permute-start(bf16[256,256]{1,0:T(8,128)(2,1)S(1)} %constant_dynamic-update-slice_fusion.refs_0_), channel_id=1, source_target_pairs={{0,2},{1,5},{2,0},{3,7},{4,6},{5,1},{6,4},{7,3},{8,10},{9,13},{10,... | collective-permute-start | bytes 393224 | tf_op jit(solution)/shard_map/ppermute | solution.py:267
  8.3 2.3 %collective-permute-done.orbitals = bf16[128,2,256]{2,1,0:T(2,128)(2,1)S(1)} collective-permute-done((bf16[128,2,256]{2,1,0:T(2,128)(2,1)}, bf16[128,2,256]{2,1,0:T(2,128)(2,1)S(1)}, u32[]{:S(2)}, u32[]{:S(2)}) %collective-permute-start) | collective-permute-done | bytes 131104 | tf_op jit(solution)/shard_map/ppermute | solution.py:267
  11.8 1.6 %collective-permute-start.3 = (bf16[128,2,256]{2,1,0:T(2,128)(2,1)S(1)}, bf16[128,2,256]{2,1,0:T(2,128)(2,1)S(1)}, u32[]{:S(2)}, u32[]{:S(2)}) collective-permute-start(bf16[128,2,256]{2,1,0:T(2,128)(2,1)S(1)} %collective-permute-done.orbitals), channel_id=1, source_target_pairs={{0,8},{1,9},{2,10},{3,11},{4,12},{5,13},{6,14},{7,15},{8,0},{9,1},... | collective-permute-start | bytes 393224 | tf_op jit(solution)/shard_map/ppermute | solution.py:267
  13.7 1.6 %collective-permute-start.5 = (bf16[512,256]{1,0:T(8,128)(2,1)S(1)}, bf16[512,256]{1,0:T(8,128)(2,1)S(1)}, u32[]{:S(2)}, u32[]{:S(2)}) collective-permute-start(bf16[512,256]{1,0:T(8,128)(2,1)S(1)} %shard_map.39.refs_0_), channel_id=1, source_target_pairs={{0,4},{1,3},{2,6},{3,1},{4,0},{5,7},{6,2},{7,5},{8,12},{9,11},{10,... | collective-permute-start | bytes 786440 | tf_op jit(solution)/shard_map/ppermute | solution.py:267
  15.3 1.5 %collective-permute-done.3.orbitals = bf16[128,2,256]{2,1,0:T(2,128)(2,1)S(1)} collective-permute-done((bf16[128,2,256]{2,1,0:T(2,128)(2,1)S(1)}, bf16[128,2,256]{2,1,0:T(2,128)(2,1)S(1)}, u32[]{:S(2)}, u32[]{:S(2)}) %collective-permute-start.3) | collective-permute-done | bytes 131104 | tf_op jit(solution)/shard_map/ppermute | solution.py:267
  17.3 1.6 %collective-permute-start.9 = (bf16[256,256]{1,0:T(8,128)(2,1)S(1)}, bf16[256,256]{1,0:T(8,128)(2,1)S(1)}, u32[]{:S(2)}, u32[]{:S(2)}) collective-permute-start(bf16[256,256]{1,0:T(8,128)(2,1)S(1)} %shard_map.44.refs_0_), channel_id=1, source_target_pairs={{0,2},{1,5},{2,0},{3,7},{4,6},{5,1},{6,4},{7,3},{8,10},{9,13},{10,... | collective-permute-start | bytes 393224 | tf_op jit(solution)/shard_map/ppermute | solution.py:267
  18.9 1.2 %collective-permute-done.5.refs_1_ = bf16[512,256]{1,0:T(8,128)(2,1)S(1)} collective-permute-done((bf16[512,256]{1,0:T(8,128)(2,1)S(1)}, bf16[512,256]{1,0:T(8,128)(2,1)S(1)}, u32[]{:S(2)}, u32[]{:S(2)}) %collective-permute-start.5) | collective-permute-done | bytes 262176 | tf_op jit(solution)/shard_map/ppermute | solution.py:267
  20.7 1.5 %collective-permute-start.6 = (bf16[256,256]{1,0:T(8,128)(2,1)S(1)}, bf16[256,256]{1,0:T(8,128)(2,1)S(1)}, u32[]{:S(2)}, u32[]{:S(2)}) collective-permute-start(bf16[256,256]{1,0:T(8,128)(2,1)S(1)} %shard_map.41.refs_0_), channel_id=1, source_target_pairs={{0,2},{1,5},{2,0},{3,7},{4,6},{5,1},{6,4},{7,3},{8,10},{9,13},{10,... | collective-permute-start | bytes 393224 | tf_op jit(solution)/shard_map/ppermute | solution.py:267
  22.4 1.6 %collective-permute-start.10 = (bf16[512,256]{1,0:T(8,128)(2,1)S(1)}, bf16[512,256]{1,0:T(8,128)(2,1)S(1)}, u32[]{:S(2)}, u32[]{:S(2)}) collective-permute-start(bf16[512,256]{1,0:T(8,128)(2,1)S(1)} %shard_map.45.refs_2_), channel_id=1, source_target_pairs={{0,4},{1,3},{2,6},{3,1},{4,0},{5,7},{6,2},{7,5},{8,12},{9,11},{10,... | collective-permute-start | bytes 786440 | tf_op jit(solution)/shard_map/ppermute | solution.py:267
  24.0 2.8 %collective-permute-done.6.refs_1_ = bf16[256,256]{1,0:T(8,128)(2,1)S(1)} collective-permute-done((bf16[256,256]{1,0:T(8,128)(2,1)S(1)}, bf16[256,256]{1,0:T(8,128)(2,1)S(1)}, u32[]{:S(2)}, u32[]{:S(2)}) %collective-permute-start.6) | collective-permute-done | bytes 131104 | tf_op jit(solution)/shard_map/ppermute | solution.py:267
  26.7 1.6 %collective-permute-start.11 = (bf16[512,256]{1,0:T(8,128)(2,1)S(1)}, bf16[512,256]{1,0:T(8,128)(2,1)S(1)}, u32[]{:S(2)}, u32[]{:S(2)}) collective-permute-start(bf16[512,256]{1,0:T(8,128)(2,1)S(1)} %shard_map.46.refs_4_), channel_id=1, source_target_pairs={{0,4},{1,3},{2,6},{3,1},{4,0},{5,7},{6,2},{7,5},{8,12},{9,11},{10,... | collective-permute-start | bytes 786440 | tf_op jit(solution)/shard_map/ppermute | solution.py:267
  29.4 2.4 %shard_map.47 = (f32[256,256]{1,0:T(8,128)S(1)}, bf16[256,1536]{1,0:T(8,128)(2,1)S(1)}) custom-call(s32[8]{0:T(128)S(1)} %stack.107.ids, bf16[256,256]{1,0:T(8,128)(2,1)S(1)} %maximum_select_fusion.rows, bf16[256,2048]{1,0:T(8,128)(2,1)S(1)} %copy-done.2, bf16[256,2048]{1,0:T(8,128)(2,1)S(1)} %collective-permute-done.7.kernel_other, ...), custom_call_target="tpu_custom_call" | custom-call | flops 60000002048 | bytes 1000000 | tf_op jit(solution)/shard_map/pallas_call | solution.py:160
  31.8 1.4 %collective-permute-done.11.refs_0_ = bf16[512,256]{1,0:T(8,128)(2,1)S(1)} collective-permute-done((bf16[512,256]{1,0:T(8,128)(2,1)S(1)}, bf16[512,256]{1,0:T(8,128)(2,1)S(1)}, u32[]{:S(2)}, u32[]{:S(2)}) %collective-permute-start.11) | collective-permute-done | bytes 262176 | tf_op jit(solution)/shard_map/ppermute | solution.py:267
  34.7 1.6 %collective-permute-start.14 = (bf16[512,256]{1,0:T(8,128)(2,1)S(1)}, bf16[512,256]{1,0:T(8,128)(2,1)S(1)}, u32[]{:S(2)}, u32[]{:S(2)}) collective-permute-start(bf16[512,256]{1,0:T(8,128)(2,1)S(1)} %get-tuple-element.50), channel_id=1, source_target_pairs={{0,2},{1,5},{2,0},{3,7},{4,6},{5,1},{6,4},{7,3},{8,10},{9,13},{10,... | collective-permute-start | bytes 786440 | tf_op jit(solution)/shard_map/ppermute | solution.py:267
  37.3 3.8 %collective-permute-done.14.got = bf16[512,256]{1,0:T(8,128)(2,1)S(1)} collective-permute-done((bf16[512,256]{1,0:T(8,128)(2,1)S(1)}, bf16[512,256]{1,0:T(8,128)(2,1)S(1)}, u32[]{:S(2)}, u32[]{:S(2)}) %collective-permute-start.14) | collective-permute-done | bytes 262176 | tf_op jit(solution)/shard_map/ppermute | solution.py:267
  41.2 1.6 %collective-permute-start.15 = (bf16[256,256]{1,0:T(8,128)(2,1)S(1)}, bf16[256,256]{1,0:T(8,128)(2,1)S(1)}, u32[]{:S(2)}, u32[]{:S(2)}) collective-permute-start(bf16[256,256]{1,0:T(8,128)(2,1)S(1)} %get-tuple-element.51), channel_id=1, source_target_pairs={{0,4},{1,3},{2,6},{3,1},{4,0},{5,7},{6,2},{7,5},{8,12},{9,11},{10,... | collective-permute-start | bytes 393224 | tf_op jit(solution)/shard_map/ppermute | solution.py:267
  43.3 2.4 %collective-permute-done.13.got = bf16[512,256]{1,0:T(8,128)(2,1)S(1)} collective-permute-done((bf16[512,256]{1,0:T(8,128)(2,1)S(1)}, bf16[512,256]{1,0:T(8,128)(2,1)S(1)}, u32[]{:S(2)}, u32[]{:S(2)}) %collective-permute-start.13) | collective-permute-done | bytes 262176 | tf_op jit(solution)/shard_map/ppermute | solution.py:267
  46.2 2.7 %collective-permute-start.16 = (bf16[128,256]{1,0:T(8,128)(2,1)S(1)}, bf16[128,256]{1,0:T(8,128)(2,1)S(1)}, u32[]{:S(2)}, u32[]{:S(2)}) collective-permute-start(bf16[128,256]{1,0:T(8,128)(2,1)S(1)} %get-tuple-element.53), channel_id=1, source_target_pairs={{0,24},{1,25},{2,26},{3,27},{4,28},{5,29},{6,30},{7,31},{8,16},{9,... | collective-permute-start | bytes 196616 | tf_op jit(solution)/shard_map/ppermute | solution.py:267
  49.0 1.8 %collective-permute-start.19 = (bf16[128,256]{1,0:T(8,128)(2,1)S(1)}, bf16[128,256]{1,0:T(8,128)(2,1)S(1)}, u32[]{:S(2)}, u32[]{:S(2)}) collective-permute-start(bf16[128,256]{1,0:T(8,128)(2,1)S(1)} %get-tuple-element.56), channel_id=1, source_target_pairs={{0,16},{1,17},{2,18},{3,19},{4,20},{5,21},{6,22},{7,23},{8,24},{9,... | collective-permute-start | bytes 196616 | tf_op jit(solution)/shard_map/ppermute | solution.py:267
  50.9 1.6 %collective-permute-done.16 = bf16[128,256]{1,0:T(8,128)(2,1)S(1)} collective-permute-done((bf16[128,256]{1,0:T(8,128)(2,1)S(1)}, bf16[128,256]{1,0:T(8,128)(2,1)S(1)}, u32[]{:S(2)}, u32[]{:S(2)}) %collective-permute-start.16) | collective-permute-done | bytes 65568 | tf_op jit(solution)/shard_map/ppermute | solution.py:267
  52.5 1.3 %collective-permute-done.18 = bf16[128,256]{1,0:T(8,128)(2,1)S(1)} collective-permute-done((bf16[128,256]{1,0:T(8,128)(2,1)S(1)}, bf16[128,256]{1,0:T(8,128)(2,1)S(1)}, u32[]{:S(2)}, u32[]{:S(2)}) %collective-permute-start.18) | collective-permute-done | bytes 65568 | tf_op jit(solution)/shard_map/ppermute | solution.py:267
  54.6 1.3 %collective-permute-done.20.partner = f32[128,256]{1,0:T(8,128)S(1)} collective-permute-done((f32[128,256]{1,0:T(8,128)S(1)}, f32[128,256]{1,0:T(8,128)S(1)}, u32[]{:S(2)}, u32[]{:S(2)}) %collective-permute-start.20) | collective-permute-done | bytes 131104 | tf_op jit(solution)/shard_map/ppermute | solution.py:272
  (48 shorter events, 10.7 us)
Async XLA Ops:
  0.0 10.5 %collective-permute-start = (bf16[128,2,256]{2,1,0:T(2,128)(2,1)}, bf16[128,2,256]{2,1,0:T(2,128)(2,1)S(1)}, u32[]{:S(2)}, u32[]{:S(2)}) collective-permute-start(bf16[128,2,256]{2,1,0:T(2,128)(2,1)} %orbitals.1), channel_id=1, source_target_pairs={{0,16},{1,17},{2,18},{3,19},{4,20},{5,21},{6,22},{7,23},{8,24},{9,... | collective-permute-start | bytes 393224 | tf_op jit(solution)/shard_map/ppermute | solution.py:267
  4.0 0.9 %copy-start.1 = (bf16[128,2,256]{2,1,0:T(2,128)(2,1)S(1)}, bf16[128,2,256]{2,1,0:T(2,128)(2,1)}, u32[]{:S(2)}) copy-start(bf16[128,2,256]{2,1,0:T(2,128)(2,1)} %orbitals.1) | copy-start | bytes 393220
  5.4 1.3 %collective-permute-start.1 = (bf16[128,256]{1,0:T(8,128)(2,1)S(1)}, bf16[128,256]{1,0:T(8,128)(2,1)S(1)}, u32[]{:S(2)}, u32[]{:S(2)}) collective-permute-start(bf16[128,256]{1,0:T(8,128)(2,1)S(1)} %get-tuple-element.32), channel_id=1, source_target_pairs={{0,1},{1,0},{2,3},{3,2},{4,5},{5,4},{6,7},{7,6},{8,9},{9,8},{10,11... | collective-permute-start | bytes 196616 | tf_op jit(solution)/shard_map/ppermute | solution.py:272
  6.7 5.0 %collective-permute-start.2 = (bf16[256,256]{1,0:T(8,128)(2,1)S(1)}, bf16[256,256]{1,0:T(8,128)(2,1)S(1)}, u32[]{:S(2)}, u32[]{:S(2)}) collective-permute-start(bf16[256,256]{1,0:T(8,128)(2,1)S(1)} %constant_dynamic-update-slice_fusion.refs_0_), channel_id=1, source_target_pairs={{0,2},{1,5},{2,0},{3,7},{4,6},{5,1},{6,4},{7,3},{8,10},{9,13},{10,... | collective-permute-start | bytes 393224 | tf_op jit(solution)/shard_map/ppermute | solution.py:267
  11.8 5.0 %collective-permute-start.3 = (bf16[128,2,256]{2,1,0:T(2,128)(2,1)S(1)}, bf16[128,2,256]{2,1,0:T(2,128)(2,1)S(1)}, u32[]{:S(2)}, u32[]{:S(2)}) collective-permute-start(bf16[128,2,256]{2,1,0:T(2,128)(2,1)S(1)} %collective-permute-done.orbitals), channel_id=1, source_target_pairs={{0,8},{1,9},{2,10},{3,11},{4,12},{5,13},{6,14},{7,15},{8,0},{9,1},... | collective-permute-start | bytes 393224 | tf_op jit(solution)/shard_map/ppermute | solution.py:267
  13.6 3.7 %collective-permute-start.8 = (bf16[128,256]{1,0:T(8,128)(2,1)S(1)}, bf16[128,256]{1,0:T(8,128)(2,1)S(1)}, u32[]{:S(2)}, u32[]{:S(2)}) collective-permute-start(bf16[128,256]{1,0:T(8,128)(2,1)S(1)} %get-tuple-element.43), channel_id=1, source_target_pairs={{0,1},{1,0},{2,3},{3,2},{4,5},{5,4},{6,7},{7,6},{8,9},{9,8},{10,11... | collective-permute-start | bytes 196616 | tf_op jit(solution)/shard_map/ppermute | solution.py:272
  13.7 6.4 %collective-permute-start.5 = (bf16[512,256]{1,0:T(8,128)(2,1)S(1)}, bf16[512,256]{1,0:T(8,128)(2,1)S(1)}, u32[]{:S(2)}, u32[]{:S(2)}) collective-permute-start(bf16[512,256]{1,0:T(8,128)(2,1)S(1)} %shard_map.39.refs_0_), channel_id=1, source_target_pairs={{0,4},{1,3},{2,6},{3,1},{4,0},{5,7},{6,2},{7,5},{8,12},{9,11},{10,... | collective-permute-start | bytes 786440 | tf_op jit(solution)/shard_map/ppermute | solution.py:267
  17.2 1.7 %collective-permute-start.4 = (bf16[128,256]{1,0:T(8,128)(2,1)S(1)}, bf16[128,256]{1,0:T(8,128)(2,1)S(1)}, u32[]{:S(2)}, u32[]{:S(2)}) collective-permute-start(bf16[128,256]{1,0:T(8,128)(2,1)S(1)} %get-tuple-element.38), channel_id=1, source_target_pairs={{0,1},{1,0},{2,3},{3,2},{4,5},{5,4},{6,7},{7,6},{8,9},{9,8},{10,11... | collective-permute-start | bytes 196616 | tf_op jit(solution)/shard_map/ppermute | solution.py:272
  17.3 5.0 %collective-permute-start.9 = (bf16[256,256]{1,0:T(8,128)(2,1)S(1)}, bf16[256,256]{1,0:T(8,128)(2,1)S(1)}, u32[]{:S(2)}, u32[]{:S(2)}) collective-permute-start(bf16[256,256]{1,0:T(8,128)(2,1)S(1)} %shard_map.44.refs_0_), channel_id=1, source_target_pairs={{0,2},{1,5},{2,0},{3,7},{4,6},{5,1},{6,4},{7,3},{8,10},{9,13},{10,... | collective-permute-start | bytes 393224 | tf_op jit(solution)/shard_map/ppermute | solution.py:267
  20.2 6.6 %copy-start.2 = (bf16[256,2048]{1,0:T(8,128)(2,1)S(1)}, bf16[256,2048]{1,0:T(8,128)(2,1)}, u32[]{:S(2)}) copy-start(bf16[256,2048]{1,0:T(8,128)(2,1)} %kernel.1) | copy-start | bytes 3145732
  20.2 13.5 %collective-permute-start.12 = (bf16[1024,256]{1,0:T(8,128)(2,1)S(1)}, bf16[1024,256]{1,0:T(8,128)(2,1)S(1)}, u32[]{:S(2)}, u32[]{:S(2)}) collective-permute-start(bf16[1024,256]{1,0:T(8,128)(2,1)S(1)} %shard_map.42), channel_id=1, source_target_pairs={{0,8},{1,9},{2,10},{3,11},{4,12},{5,13},{6,14},{7,15},{8,0},{9,1},... | collective-permute-start | bytes 1572872 | tf_op jit(solution)/shard_map/ppermute | solution.py:267
  20.7 6.0 %collective-permute-start.6 = (bf16[256,256]{1,0:T(8,128)(2,1)S(1)}, bf16[256,256]{1,0:T(8,128)(2,1)S(1)}, u32[]{:S(2)}, u32[]{:S(2)}) collective-permute-start(bf16[256,256]{1,0:T(8,128)(2,1)S(1)} %shard_map.41.refs_0_), channel_id=1, source_target_pairs={{0,2},{1,5},{2,0},{3,7},{4,6},{5,1},{6,4},{7,3},{8,10},{9,13},{10,... | collective-permute-start | bytes 393224 | tf_op jit(solution)/shard_map/ppermute | solution.py:267
  22.4 6.0 %copy-start = (bf16[256,2048]{1,0:T(8,128)(2,1)S(1)}, bf16[256,2048]{1,0:T(8,128)(2,1)}, u32[]{:S(2)}) copy-start(bf16[256,2048]{1,0:T(8,128)(2,1)} %basis) | copy-start | bytes 3145732
  22.4 6.8 %collective-permute-start.10 = (bf16[512,256]{1,0:T(8,128)(2,1)S(1)}, bf16[512,256]{1,0:T(8,128)(2,1)S(1)}, u32[]{:S(2)}, u32[]{:S(2)}) collective-permute-start(bf16[512,256]{1,0:T(8,128)(2,1)S(1)} %shard_map.45.refs_2_), channel_id=1, source_target_pairs={{0,4},{1,3},{2,6},{3,1},{4,0},{5,7},{6,2},{7,5},{8,12},{9,11},{10,... | collective-permute-start | bytes 786440 | tf_op jit(solution)/shard_map/ppermute | solution.py:267
  26.7 2.7 %collective-permute-start.7 = (bf16[256,2048]{1,0:T(8,128)(2,1)S(1)}, bf16[256,2048]{1,0:T(8,128)(2,1)S(1)}, u32[]{:S(2)}, u32[]{:S(2)}) collective-permute-start(bf16[256,2048]{1,0:T(8,128)(2,1)S(1)} %copy-done.2), channel_id=1, source_target_pairs={{0,1},{1,0},{2,3},{3,2},{4,5},{5,4},{6,7},{7,6},{8,9},{9,8},{10,11... | collective-permute-start | bytes 3145736 | tf_op jit(solution)/shard_map/ppermute | solution.py:272
  26.7 6.4 %collective-permute-start.11 = (bf16[512,256]{1,0:T(8,128)(2,1)S(1)}, bf16[512,256]{1,0:T(8,128)(2,1)S(1)}, u32[]{:S(2)}, u32[]{:S(2)}) collective-permute-start(bf16[512,256]{1,0:T(8,128)(2,1)S(1)} %shard_map.46.refs_4_), channel_id=1, source_target_pairs={{0,4},{1,3},{2,6},{3,1},{4,0},{5,7},{6,2},{7,5},{8,12},{9,11},{10,... | collective-permute-start | bytes 786440 | tf_op jit(solution)/shard_map/ppermute | solution.py:267
  34.7 6.4 %collective-permute-start.14 = (bf16[512,256]{1,0:T(8,128)(2,1)S(1)}, bf16[512,256]{1,0:T(8,128)(2,1)S(1)}, u32[]{:S(2)}, u32[]{:S(2)}) collective-permute-start(bf16[512,256]{1,0:T(8,128)(2,1)S(1)} %get-tuple-element.50), channel_id=1, source_target_pairs={{0,2},{1,5},{2,0},{3,7},{4,6},{5,1},{6,4},{7,3},{8,10},{9,13},{10,... | collective-permute-start | bytes 786440 | tf_op jit(solution)/shard_map/ppermute | solution.py:267
  36.5 9.2 %collective-permute-start.13 = (bf16[512,256]{1,0:T(8,128)(2,1)S(1)}, bf16[512,256]{1,0:T(8,128)(2,1)S(1)}, u32[]{:S(2)}, u32[]{:S(2)}) collective-permute-start(bf16[512,256]{1,0:T(8,128)(2,1)S(1)} %shard_map.50), channel_id=1, source_target_pairs={{0,2},{1,5},{2,0},{3,7},{4,6},{5,1},{6,4},{7,3},{8,10},{9,13},{10,... | collective-permute-start | bytes 786440 | tf_op jit(solution)/shard_map/ppermute | solution.py:267
  41.2 5.0 %collective-permute-start.15 = (bf16[256,256]{1,0:T(8,128)(2,1)S(1)}, bf16[256,256]{1,0:T(8,128)(2,1)S(1)}, u32[]{:S(2)}, u32[]{:S(2)}) collective-permute-start(bf16[256,256]{1,0:T(8,128)(2,1)S(1)} %get-tuple-element.51), channel_id=1, source_target_pairs={{0,4},{1,3},{2,6},{3,1},{4,0},{5,7},{6,2},{7,5},{8,12},{9,11},{10,... | collective-permute-start | bytes 393224 | tf_op jit(solution)/shard_map/ppermute | solution.py:267
  42.7 6.2 %collective-permute-start.17 = (bf16[256,256]{1,0:T(8,128)(2,1)S(1)}, bf16[256,256]{1,0:T(8,128)(2,1)S(1)}, u32[]{:S(2)}, u32[]{:S(2)}) collective-permute-start(bf16[256,256]{1,0:T(8,128)(2,1)S(1)} %get-tuple-element.54), channel_id=1, source_target_pairs={{0,4},{1,3},{2,6},{3,1},{4,0},{5,7},{6,2},{7,5},{8,12},{9,11},{10,... | collective-permute-start | bytes 393224 | tf_op jit(solution)/shard_map/ppermute | solution.py:267
  46.2 6.2 %collective-permute-start.16 = (bf16[128,256]{1,0:T(8,128)(2,1)S(1)}, bf16[128,256]{1,0:T(8,128)(2,1)S(1)}, u32[]{:S(2)}, u32[]{:S(2)}) collective-permute-start(bf16[128,256]{1,0:T(8,128)(2,1)S(1)} %get-tuple-element.53), channel_id=1, source_target_pairs={{0,24},{1,25},{2,26},{3,27},{4,28},{5,29},{6,30},{7,31},{8,16},{9,... | collective-permute-start | bytes 196616 | tf_op jit(solution)/shard_map/ppermute | solution.py:267
  49.0 4.8 %collective-permute-start.18 = (bf16[128,256]{1,0:T(8,128)(2,1)S(1)}, bf16[128,256]{1,0:T(8,128)(2,1)S(1)}, u32[]{:S(2)}, u32[]{:S(2)}) collective-permute-start(bf16[128,256]{1,0:T(8,128)(2,1)S(1)} %get-tuple-element.55), channel_id=1, source_target_pairs={{0,8},{1,9},{2,10},{3,11},{4,12},{5,13},{6,14},{7,15},{8,0},{9,1},... | collective-permute-start | bytes 196616 | tf_op jit(solution)/shard_map/ppermute | solution.py:267
  49.0 5.5 %collective-permute-start.19 = (bf16[128,256]{1,0:T(8,128)(2,1)S(1)}, bf16[128,256]{1,0:T(8,128)(2,1)S(1)}, u32[]{:S(2)}, u32[]{:S(2)}) collective-permute-start(bf16[128,256]{1,0:T(8,128)(2,1)S(1)} %get-tuple-element.56), channel_id=1, source_target_pairs={{0,16},{1,17},{2,18},{3,19},{4,20},{5,21},{6,22},{7,23},{8,24},{9,... | collective-permute-start | bytes 196616 | tf_op jit(solution)/shard_map/ppermute | solution.py:267
  54.6 1.4 %collective-permute-start.20 = (f32[128,256]{1,0:T(8,128)S(1)}, f32[128,256]{1,0:T(8,128)S(1)}, u32[]{:S(2)}, u32[]{:S(2)}) collective-permute-start(f32[128,256]{1,0:T(8,128)S(1)} %convert_add_fusion.result), channel_id=1, source_target_pairs={{0,1},{1,0},{2,3},{3,2},{4,5},{5,4},{6,7},{7,6},{8,9},{9,8},{10,11... | collective-permute-start | bytes 393224 | tf_op jit(solution)/shard_map/ppermute | solution.py:272

commit v5 on v4

--- a/solution.py
+++ b/solution.py
@@ -298,7 +298,7 @@
     x8 = first(z8)
     z4 = plane(whole, 1)
     x12 = first(after(z12, whole))
-    p8 = join_blocks(after(z8, whole), x8, weight=6)
+    p8 = join_blocks(after(z8, whole), x8)
     p12 = join_blocks(z12, x12)
     y8 = second(p8)
     y12 = second(p12)

time: 56.9 us -> 56.9 us (level)
  no operation moved by 1% of the time
where the time goes in v5:
time: 56.9 us; the launch traced here: 56.8 us
  starting transfers between devices  24.7 us (43%)
  waiting for transfers between devices  23.7 us (42%)
  Pallas kernels  7.03 us (12%)
  local copies, waits for them, and re-layouts  1.14 us (2%)
    ppermute x16, starting transfers between devices, send(): return lax.ppermute(a, ('row', 'col'), pairs)  24.4 us
    ppermute x16, waiting for transfers between devices, send(): return lax.ppermute(a, ('row', 'col'), pairs)  20.9 us
    ppermute x5, waiting for transfers between devices, box_body(): swap = lambda a: lax.ppermute(a, 'col', [(0, 1), (1, 0)])  2.72 us
    pallas_call x1, Pallas kernels, apply_early(): pl.pallas_call(functools.partial(early_kernel, slots, tuple(later), n //...  2.44 us
    pallas_call x3, Pallas kernels, split_spins(): pl.pallas_call(split_kernel, out_shape=[jax.ShapeDtypeStruct((p, i), orbi...  1.15 us
  transfers between devices with their start and end apart: 21, of which 17 were waited for; matrix products, arithmetic and copies ran while one was open for 0% of the time, Pallas kernels for 9%

profile of v5, /device:TPU:0, one launch (start us, length us, event | category | flops | bytes accessed | tf_op | source)
XLA Modules:
  0.0 56.8 jit_solution(17914114930018402116)
XLA Ops:
  0.0 4.0 %collective-permute-start = (bf16[128,2,256]{2,1,0:T(2,128)(2,1)}, bf16[128,2,256]{2,1,0:T(2,128)(2,1)S(1)}, u32[]{:S(2)}, u32[]{:S(2)}) collective-permute-start(bf16[128,2,256]{2,1,0:T(2,128)(2,1)} %orbitals.1), channel_id=1, source_target_pairs={{0,16},{1,17},{2,18},{3,19},{4,20},{5,21},{6,22},{7,23},{8,24},{9,... | collective-permute-start | bytes 393224 | tf_op jit(solution)/shard_map/ppermute | solution.py:267
  5.5 1.2 %collective-permute-done.1 = bf16[128,256]{1,0:T(8,128)(2,1)S(1)} collective-permute-done((bf16[128,256]{1,0:T(8,128)(2,1)S(1)}, bf16[128,256]{1,0:T(8,128)(2,1)S(1)}, u32[]{:S(2)}, u32[]{:S(2)}) %collective-permute-start.1) | collective-permute-done | bytes 65568 | tf_op jit(solution)/shard_map/ppermute | solution.py:272
  6.7 1.6 %collective-permute-start.2 = (bf16[256,256]{1,0:T(8,128)(2,1)S(1)}, bf16[256,256]{1,0:T(8,128)(2,1)S(1)}, u32[]{:S(2)}, u32[]{:S(2)}) collective-permute-start(bf16[256,256]{1,0:T(8,128)(2,1)S(1)} %constant_dynamic-update-slice_fusion.refs_0_), channel_id=1, source_target_pairs={{0,2},{1,5},{2,0},{3,7},{4,6},{5,1},{6,4},{7,3},{8,10},{9,13},{10,... | collective-permute-start | bytes 393224 | tf_op jit(solution)/shard_map/ppermute | solution.py:267
  8.3 2.3 %collective-permute-done.orbitals = bf16[128,2,256]{2,1,0:T(2,128)(2,1)S(1)} collective-permute-done((bf16[128,2,256]{2,1,0:T(2,128)(2,1)}, bf16[128,2,256]{2,1,0:T(2,128)(2,1)S(1)}, u32[]{:S(2)}, u32[]{:S(2)}) %collective-permute-start) | collective-permute-done | bytes 131104 | tf_op jit(solution)/shard_map/ppermute | solution.py:267
  11.8 1.6 %collective-permute-start.3 = (bf16[128,2,256]{2,1,0:T(2,128)(2,1)S(1)}, bf16[128,2,256]{2,1,0:T(2,128)(2,1)S(1)}, u32[]{:S(2)}, u32[]{:S(2)}) collective-permute-start(bf16[128,2,256]{2,1,0:T(2,128)(2,1)S(1)} %collective-permute-done.orbitals), channel_id=1, source_target_pairs={{0,8},{1,9},{2,10},{3,11},{4,12},{5,13},{6,14},{7,15},{8,0},{9,1},... | collective-permute-start | bytes 393224 | tf_op jit(solution)/shard_map/ppermute | solution.py:267
  13.7 1.6 %collective-permute-start.5 = (bf16[512,256]{1,0:T(8,128)(2,1)S(1)}, bf16[512,256]{1,0:T(8,128)(2,1)S(1)}, u32[]{:S(2)}, u32[]{:S(2)}) collective-permute-start(bf16[512,256]{1,0:T(8,128)(2,1)S(1)} %shard_map.39.refs_0_), channel_id=1, source_target_pairs={{0,4},{1,3},{2,6},{3,1},{4,0},{5,7},{6,2},{7,5},{8,12},{9,11},{10,... | collective-permute-start | bytes 786440 | tf_op jit(solution)/shard_map/ppermute | solution.py:267
  15.3 1.5 %collective-permute-done.3.orbitals = bf16[128,2,256]{2,1,0:T(2,128)(2,1)S(1)} collective-permute-done((bf16[128,2,256]{2,1,0:T(2,128)(2,1)S(1)}, bf16[128,2,256]{2,1,0:T(2,128)(2,1)S(1)}, u32[]{:S(2)}, u32[]{:S(2)}) %collective-permute-start.3) | collective-permute-done | bytes 131104 | tf_op jit(solution)/shard_map/ppermute | solution.py:267
  17.3 1.6 %collective-permute-start.9 = (bf16[256,256]{1,0:T(8,128)(2,1)S(1)}, bf16[256,256]{1,0:T(8,128)(2,1)S(1)}, u32[]{:S(2)}, u32[]{:S(2)}) collective-permute-start(bf16[256,256]{1,0:T(8,128)(2,1)S(1)} %shard_map.44.refs_0_), channel_id=1, source_target_pairs={{0,2},{1,5},{2,0},{3,7},{4,6},{5,1},{6,4},{7,3},{8,10},{9,13},{10,... | collective-permute-start | bytes 393224 | tf_op jit(solution)/shard_map/ppermute | solution.py:267
  18.9 1.2 %collective-permute-done.5.refs_1_ = bf16[512,256]{1,0:T(8,128)(2,1)S(1)} collective-permute-done((bf16[512,256]{1,0:T(8,128)(2,1)S(1)}, bf16[512,256]{1,0:T(8,128)(2,1)S(1)}, u32[]{:S(2)}, u32[]{:S(2)}) %collective-permute-start.5) | collective-permute-done | bytes 262176 | tf_op jit(solution)/shard_map/ppermute | solution.py:267
  20.7 1.5 %collective-permute-start.6 = (bf16[256,256]{1,0:T(8,128)(2,1)S(1)}, bf16[256,256]{1,0:T(8,128)(2,1)S(1)}, u32[]{:S(2)}, u32[]{:S(2)}) collective-permute-start(bf16[256,256]{1,0:T(8,128)(2,1)S(1)} %shard_map.41.refs_0_), channel_id=1, source_target_pairs={{0,2},{1,5},{2,0},{3,7},{4,6},{5,1},{6,4},{7,3},{8,10},{9,13},{10,... | collective-permute-start | bytes 393224 | tf_op jit(solution)/shard_map/ppermute | solution.py:267
  22.4 1.6 %collective-permute-start.10 = (bf16[512,256]{1,0:T(8,128)(2,1)S(1)}, bf16[512,256]{1,0:T(8,128)(2,1)S(1)}, u32[]{:S(2)}, u32[]{:S(2)}) collective-permute-start(bf16[512,256]{1,0:T(8,128)(2,1)S(1)} %shard_map.45.refs_2_), channel_id=1, source_target_pairs={{0,4},{1,3},{2,6},{3,1},{4,0},{5,7},{6,2},{7,5},{8,12},{9,11},{10,... | collective-permute-start | bytes 786440 | tf_op jit(solution)/shard_map/ppermute | solution.py:267
  24.0 2.8 %collective-permute-done.6.refs_1_ = bf16[256,256]{1,0:T(8,128)(2,1)S(1)} collective-permute-done((bf16[256,256]{1,0:T(8,128)(2,1)S(1)}, bf16[256,256]{1,0:T(8,128)(2,1)S(1)}, u32[]{:S(2)}, u32[]{:S(2)}) %collective-permute-start.6) | collective-permute-done | bytes 131104 | tf_op jit(solution)/shard_map/ppermute | solution.py:267
  26.7 1.6 %collective-permute-start.11 = (bf16[512,256]{1,0:T(8,128)(2,1)S(1)}, bf16[512,256]{1,0:T(8,128)(2,1)S(1)}, u32[]{:S(2)}, u32[]{:S(2)}) collective-permute-start(bf16[512,256]{1,0:T(8,128)(2,1)S(1)} %shard_map.46.refs_4_), channel_id=1, source_target_pairs={{0,4},{1,3},{2,6},{3,1},{4,0},{5,7},{6,2},{7,5},{8,12},{9,11},{10,... | collective-permute-start | bytes 786440 | tf_op jit(solution)/shard_map/ppermute | solution.py:267
  29.4 2.4 %shard_map.47 = (f32[256,256]{1,0:T(8,128)S(1)}, bf16[256,1536]{1,0:T(8,128)(2,1)S(1)}) custom-call(s32[8]{0:T(128)S(1)} %stack.107.ids, bf16[256,256]{1,0:T(8,128)(2,1)S(1)} %maximum_select_fusion.rows, bf16[256,2048]{1,0:T(8,128)(2,1)S(1)} %copy-done.2, bf16[256,2048]{1,0:T(8,128)(2,1)S(1)} %collective-permute-done.7.kernel_other, ...), custom_call_target="tpu_custom_call" | custom-call | flops 60000002048 | bytes 1000000 | tf_op jit(solution)/shard_map/pallas_call | solution.py:160
  31.8 1.4 %collective-permute-done.11.refs_0_ = bf16[512,256]{1,0:T(8,128)(2,1)S(1)} collective-permute-done((bf16[512,256]{1,0:T(8,128)(2,1)S(1)}, bf16[512,256]{1,0:T(8,128)(2,1)S(1)}, u32[]{:S(2)}, u32[]{:S(2)}) %collective-permute-start.11) | collective-permute-done | bytes 262176 | tf_op jit(solution)/shard_map/ppermute | solution.py:267
  34.7 1.6 %collective-permute-start.14 = (bf16[512,256]{1,0:T(8,128)(2,1)S(1)}, bf16[512,256]{1,0:T(8,128)(2,1)S(1)}, u32[]{:S(2)}, u32[]{:S(2)}) collective-permute-start(bf16[512,256]{1,0:T(8,128)(2,1)S(1)} %get-tuple-element.50), channel_id=1, source_target_pairs={{0,2},{1,5},{2,0},{3,7},{4,6},{5,1},{6,4},{7,3},{8,10},{9,13},{10,... | collective-permute-start | bytes 786440 | tf_op jit(solution)/shard_map/ppermute | solution.py:267
  37.3 3.8 %collective-permute-done.14.got = bf16[512,256]{1,0:T(8,128)(2,1)S(1)} collective-permute-done((bf16[512,256]{1,0:T(8,128)(2,1)S(1)}, bf16[512,256]{1,0:T(8,128)(2,1)S(1)}, u32[]{:S(2)}, u32[]{:S(2)}) %collective-permute-start.14) | collective-permute-done | bytes 262176 | tf_op jit(solution)/shard_map/ppermute | solution.py:267
  41.2 1.6 %collective-permute-start.15 = (bf16[256,256]{1,0:T(8,128)(2,1)S(1)}, bf16[256,256]{1,0:T(8,128)(2,1)S(1)}, u32[]{:S(2)}, u32[]{:S(2)}) collective-permute-start(bf16[256,256]{1,0:T(8,128)(2,1)S(1)} %get-tuple-element.51), channel_id=1, source_target_pairs={{0,4},{1,3},{2,6},{3,1},{4,0},{5,7},{6,2},{7,5},{8,12},{9,11},{10,... | collective-permute-start | bytes 393224 | tf_op jit(solution)/shard_map/ppermute | solution.py:267
  43.3 2.4 %collective-permute-done.13.got = bf16[512,256]{1,0:T(8,128)(2,1)S(1)} collective-permute-done((bf16[512,256]{1,0:T(8,128)(2,1)S(1)}, bf16[512,256]{1,0:T(8,128)(2,1)S(1)}, u32[]{:S(2)}, u32[]{:S(2)}) %collective-permute-start.13) | collective-permute-done | bytes 262176 | tf_op jit(solution)/shard_map/ppermute | solution.py:267
  46.2 2.7 %collective-permute-start.16 = (bf16[128,256]{1,0:T(8,128)(2,1)S(1)}, bf16[128,256]{1,0:T(8,128)(2,1)S(1)}, u32[]{:S(2)}, u32[]{:S(2)}) collective-permute-start(bf16[128,256]{1,0:T(8,128)(2,1)S(1)} %get-tuple-element.53), channel_id=1, source_target_pairs={{0,24},{1,25},{2,26},{3,27},{4,28},{5,29},{6,30},{7,31},{8,16},{9,... | collective-permute-start | bytes 196616 | tf_op jit(solution)/shard_map/ppermute | solution.py:267
  49.0 1.8 %collective-permute-start.19 = (bf16[128,256]{1,0:T(8,128)(2,1)S(1)}, bf16[128,256]{1,0:T(8,128)(2,1)S(1)}, u32[]{:S(2)}, u32[]{:S(2)}) collective-permute-start(bf16[128,256]{1,0:T(8,128)(2,1)S(1)} %get-tuple-element.56), channel_id=1, source_target_pairs={{0,16},{1,17},{2,18},{3,19},{4,20},{5,21},{6,22},{7,23},{8,24},{9,... | collective-permute-start | bytes 196616 | tf_op jit(solution)/shard_map/ppermute | solution.py:267
  50.9 1.6 %collective-permute-done.16 = bf16[128,256]{1,0:T(8,128)(2,1)S(1)} collective-permute-done((bf16[128,256]{1,0:T(8,128)(2,1)S(1)}, bf16[128,256]{1,0:T(8,128)(2,1)S(1)}, u32[]{:S(2)}, u32[]{:S(2)}) %collective-permute-start.16) | collective-permute-done | bytes 65568 | tf_op jit(solution)/shard_map/ppermute | solution.py:267
  52.5 1.3 %collective-permute-done.18 = bf16[128,256]{1,0:T(8,128)(2,1)S(1)} collective-permute-done((bf16[128,256]{1,0:T(8,128)(2,1)S(1)}, bf16[128,256]{1,0:T(8,128)(2,1)S(1)}, u32[]{:S(2)}, u32[]{:S(2)}) %collective-permute-start.18) | collective-permute-done | bytes 65568 | tf_op jit(solution)/shard_map/ppermute | solution.py:267
  54.6 1.3 %collective-permute-done.20.partner = f32[128,256]{1,0:T(8,128)S(1)} collective-permute-done((f32[128,256]{1,0:T(8,128)S(1)}, f32[128,256]{1,0:T(8,128)S(1)}, u32[]{:S(2)}, u32[]{:S(2)}) %collective-permute-start.20) | collective-permute-done | bytes 131104 | tf_op jit(solution)/shard_map/ppermute | solution.py:272
  (48 shorter events, 10.7 us)
Async XLA Ops:
  0.0 10.5 %collective-permute-start = (bf16[128,2,256]{2,1,0:T(2,128)(2,1)}, bf16[128,2,256]{2,1,0:T(2,128)(2,1)S(1)}, u32[]{:S(2)}, u32[]{:S(2)}) collective-permute-start(bf16[128,2,256]{2,1,0:T(2,128)(2,1)} %orbitals.1), channel_id=1, source_target_pairs={{0,16},{1,17},{2,18},{3,19},{4,20},{5,21},{6,22},{7,23},{8,24},{9,... | collective-permute-start | bytes 393224 | tf_op jit(solution)/shard_map/ppermute | solution.py:267
  4.0 0.9 %copy-start.1 = (bf16[128,2,256]{2,1,0:T(2,128)(2,1)S(1)}, bf16[128,2,256]{2,1,0:T(2,128)(2,1)}, u32[]{:S(2)}) copy-start(bf16[128,2,256]{2,1,0:T(2,128)(2,1)} %orbitals.1) | copy-start | bytes 393220
  5.4 1.3 %collective-permute-start.1 = (bf16[128,256]{1,0:T(8,128)(2,1)S(1)}, bf16[128,256]{1,0:T(8,128)(2,1)S(1)}, u32[]{:S(2)}, u32[]{:S(2)}) collective-permute-start(bf16[128,256]{1,0:T(8,128)(2,1)S(1)} %get-tuple-element.32), channel_id=1, source_target_pairs={{0,1},{1,0},{2,3},{3,2},{4,5},{5,4},{6,7},{7,6},{8,9},{9,8},{10,11... | collective-permute-start | bytes 196616 | tf_op jit(solution)/shard_map/ppermute | solution.py:272
  6.7 5.0 %collective-permute-start.2 = (bf16[256,256]{1,0:T(8,128)(2,1)S(1)}, bf16[256,256]{1,0:T(8,128)(2,1)S(1)}, u32[]{:S(2)}, u32[]{:S(2)}) collective-permute-start(bf16[256,256]{1,0:T(8,128)(2,1)S(1)} %constant_dynamic-update-slice_fusion.refs_0_), channel_id=1, source_target_pairs={{0,2},{1,5},{2,0},{3,7},{4,6},{5,1},{6,4},{7,3},{8,10},{9,13},{10,... | collective-permute-start | bytes 393224 | tf_op jit(solution)/shard_map/ppermute | solution.py:267
  11.8 5.0 %collective-permute-start.3 = (bf16[128,2,256]{2,1,0:T(2,128)(2,1)S(1)}, bf16[128,2,256]{2,1,0:T(2,128)(2,1)S(1)}, u32[]{:S(2)}, u32[]{:S(2)}) collective-permute-start(bf16[128,2,256]{2,1,0:T(2,128)(2,1)S(1)} %collective-permute-done.orbitals), channel_id=1, source_target_pairs={{0,8},{1,9},{2,10},{3,11},{4,12},{5,13},{6,14},{7,15},{8,0},{9,1},... | collective-permute-start | bytes 393224 | tf_op jit(solution)/shard_map/ppermute | solution.py:267
  13.6 3.7 %collective-permute-start.8 = (bf16[128,256]{1,0:T(8,128)(2,1)S(1)}, bf16[128,256]{1,0:T(8,128)(2,1)S(1)}, u32[]{:S(2)}, u32[]{:S(2)}) collective-permute-start(bf16[128,256]{1,0:T(8,128)(2,1)S(1)} %get-tuple-element.43), channel_id=1, source_target_pairs={{0,1},{1,0},{2,3},{3,2},{4,5},{5,4},{6,7},{7,6},{8,9},{9,8},{10,11... | collective-permute-start | bytes 196616 | tf_op jit(solution)/shard_map/ppermute | solution.py:272
  13.7 6.4 %collective-permute-start.5 = (bf16[512,256]{1,0:T(8,128)(2,1)S(1)}, bf16[512,256]{1,0:T(8,128)(2,1)S(1)}, u32[]{:S(2)}, u32[]{:S(2)}) collective-permute-start(bf16[512,256]{1,0:T(8,128)(2,1)S(1)} %shard_map.39.refs_0_), channel_id=1, source_target_pairs={{0,4},{1,3},{2,6},{3,1},{4,0},{5,7},{6,2},{7,5},{8,12},{9,11},{10,... | collective-permute-start | bytes 786440 | tf_op jit(solution)/shard_map/ppermute | solution.py:267
  17.2 1.7 %collective-permute-start.4 = (bf16[128,256]{1,0:T(8,128)(2,1)S(1)}, bf16[128,256]{1,0:T(8,128)(2,1)S(1)}, u32[]{:S(2)}, u32[]{:S(2)}) collective-permute-start(bf16[128,256]{1,0:T(8,128)(2,1)S(1)} %get-tuple-element.38), channel_id=1, source_target_pairs={{0,1},{1,0},{2,3},{3,2},{4,5},{5,4},{6,7},{7,6},{8,9},{9,8},{10,11... | collective-permute-start | bytes 196616 | tf_op jit(solution)/shard_map/ppermute | solution.py:272
  17.3 5.0 %collective-permute-start.9 = (bf16[256,256]{1,0:T(8,128)(2,1)S(1)}, bf16[256,256]{1,0:T(8,128)(2,1)S(1)}, u32[]{:S(2)}, u32[]{:S(2)}) collective-permute-start(bf16[256,256]{1,0:T(8,128)(2,1)S(1)} %shard_map.44.refs_0_), channel_id=1, source_target_pairs={{0,2},{1,5},{2,0},{3,7},{4,6},{5,1},{6,4},{7,3},{8,10},{9,13},{10,... | collective-permute-start | bytes 393224 | tf_op jit(solution)/shard_map/ppermute | solution.py:267
  20.2 6.6 %copy-start.2 = (bf16[256,2048]{1,0:T(8,128)(2,1)S(1)}, bf16[256,2048]{1,0:T(8,128)(2,1)}, u32[]{:S(2)}) copy-start(bf16[256,2048]{1,0:T(8,128)(2,1)} %kernel.1) | copy-start | bytes 3145732
  20.2 13.5 %collective-permute-start.12 = (bf16[1024,256]{1,0:T(8,128)(2,1)S(1)}, bf16[1024,256]{1,0:T(8,128)(2,1)S(1)}, u32[]{:S(2)}, u32[]{:S(2)}) collective-permute-start(bf16[1024,256]{1,0:T(8,128)(2,1)S(1)} %shard_map.42), channel_id=1, source_target_pairs={{0,8},{1,9},{2,10},{3,11},{4,12},{5,13},{6,14},{7,15},{8,0},{9,1},... | collective-permute-start | bytes 1572872 | tf_op jit(solution)/shard_map/ppermute | solution.py:267
  20.7 6.0 %collective-permute-start.6 = (bf16[256,256]{1,0:T(8,128)(2,1)S(1)}, bf16[256,256]{1,0:T(8,128)(2,1)S(1)}, u32[]{:S(2)}, u32[]{:S(2)}) collective-permute-start(bf16[256,256]{1,0:T(8,128)(2,1)S(1)} %shard_map.41.refs_0_), channel_id=1, source_target_pairs={{0,2},{1,5},{2,0},{3,7},{4,6},{5,1},{6,4},{7,3},{8,10},{9,13},{10,... | collective-permute-start | bytes 393224 | tf_op jit(solution)/shard_map/ppermute | solution.py:267
  22.4 6.0 %copy-start = (bf16[256,2048]{1,0:T(8,128)(2,1)S(1)}, bf16[256,2048]{1,0:T(8,128)(2,1)}, u32[]{:S(2)}) copy-start(bf16[256,2048]{1,0:T(8,128)(2,1)} %basis) | copy-start | bytes 3145732
  22.4 6.8 %collective-permute-start.10 = (bf16[512,256]{1,0:T(8,128)(2,1)S(1)}, bf16[512,256]{1,0:T(8,128)(2,1)S(1)}, u32[]{:S(2)}, u32[]{:S(2)}) collective-permute-start(bf16[512,256]{1,0:T(8,128)(2,1)S(1)} %shard_map.45.refs_2_), channel_id=1, source_target_pairs={{0,4},{1,3},{2,6},{3,1},{4,0},{5,7},{6,2},{7,5},{8,12},{9,11},{10,... | collective-permute-start | bytes 786440 | tf_op jit(solution)/shard_map/ppermute | solution.py:267
  26.7 2.7 %collective-permute-start.7 = (bf16[256,2048]{1,0:T(8,128)(2,1)S(1)}, bf16[256,2048]{1,0:T(8,128)(2,1)S(1)}, u32[]{:S(2)}, u32[]{:S(2)}) collective-permute-start(bf16[256,2048]{1,0:T(8,128)(2,1)S(1)} %copy-done.2), channel_id=1, source_target_pairs={{0,1},{1,0},{2,3},{3,2},{4,5},{5,4},{6,7},{7,6},{8,9},{9,8},{10,11... | collective-permute-start | bytes 3145736 | tf_op jit(solution)/shard_map/ppermute | solution.py:272
  26.7 6.4 %collective-permute-start.11 = (bf16[512,256]{1,0:T(8,128)(2,1)S(1)}, bf16[512,256]{1,0:T(8,128)(2,1)S(1)}, u32[]{:S(2)}, u32[]{:S(2)}) collective-permute-start(bf16[512,256]{1,0:T(8,128)(2,1)S(1)} %shard_map.46.refs_4_), channel_id=1, source_target_pairs={{0,4},{1,3},{2,6},{3,1},{4,0},{5,7},{6,2},{7,5},{8,12},{9,11},{10,... | collective-permute-start | bytes 786440 | tf_op jit(solution)/shard_map/ppermute | solution.py:267
  34.7 6.4 %collective-permute-start.14 = (bf16[512,256]{1,0:T(8,128)(2,1)S(1)}, bf16[512,256]{1,0:T(8,128)(2,1)S(1)}, u32[]{:S(2)}, u32[]{:S(2)}) collective-permute-start(bf16[512,256]{1,0:T(8,128)(2,1)S(1)} %get-tuple-element.50), channel_id=1, source_target_pairs={{0,2},{1,5},{2,0},{3,7},{4,6},{5,1},{6,4},{7,3},{8,10},{9,13},{10,... | collective-permute-start | bytes 786440 | tf_op jit(solution)/shard_map/ppermute | solution.py:267
  36.5 9.2 %collective-permute-start.13 = (bf16[512,256]{1,0:T(8,128)(2,1)S(1)}, bf16[512,256]{1,0:T(8,128)(2,1)S(1)}, u32[]{:S(2)}, u32[]{:S(2)}) collective-permute-start(bf16[512,256]{1,0:T(8,128)(2,1)S(1)} %shard_map.50), channel_id=1, source_target_pairs={{0,2},{1,5},{2,0},{3,7},{4,6},{5,1},{6,4},{7,3},{8,10},{9,13},{10,... | collective-permute-start | bytes 786440 | tf_op jit(solution)/shard_map/ppermute | solution.py:267
  41.2 5.0 %collective-permute-start.15 = (bf16[256,256]{1,0:T(8,128)(2,1)S(1)}, bf16[256,256]{1,0:T(8,128)(2,1)S(1)}, u32[]{:S(2)}, u32[]{:S(2)}) collective-permute-start(bf16[256,256]{1,0:T(8,128)(2,1)S(1)} %get-tuple-element.51), channel_id=1, source_target_pairs={{0,4},{1,3},{2,6},{3,1},{4,0},{5,7},{6,2},{7,5},{8,12},{9,11},{10,... | collective-permute-start | bytes 393224 | tf_op jit(solution)/shard_map/ppermute | solution.py:267
  42.7 6.2 %collective-permute-start.17 = (bf16[256,256]{1,0:T(8,128)(2,1)S(1)}, bf16[256,256]{1,0:T(8,128)(2,1)S(1)}, u32[]{:S(2)}, u32[]{:S(2)}) collective-permute-start(bf16[256,256]{1,0:T(8,128)(2,1)S(1)} %get-tuple-element.54), channel_id=1, source_target_pairs={{0,4},{1,3},{2,6},{3,1},{4,0},{5,7},{6,2},{7,5},{8,12},{9,11},{10,... | collective-permute-start | bytes 393224 | tf_op jit(solution)/shard_map/ppermute | solution.py:267
  46.2 6.2 %collective-permute-start.16 = (bf16[128,256]{1,0:T(8,128)(2,1)S(1)}, bf16[128,256]{1,0:T(8,128)(2,1)S(1)}, u32[]{:S(2)}, u32[]{:S(2)}) collective-permute-start(bf16[128,256]{1,0:T(8,128)(2,1)S(1)} %get-tuple-element.53), channel_id=1, source_target_pairs={{0,24},{1,25},{2,26},{3,27},{4,28},{5,29},{6,30},{7,31},{8,16},{9,... | collective-permute-start | bytes 196616 | tf_op jit(solution)/shard_map/ppermute | solution.py:267
  49.0 4.8 %collective-permute-start.18 = (bf16[128,256]{1,0:T(8,128)(2,1)S(1)}, bf16[128,256]{1,0:T(8,128)(2,1)S(1)}, u32[]{:S(2)}, u32[]{:S(2)}) collective-permute-start(bf16[128,256]{1,0:T(8,128)(2,1)S(1)} %get-tuple-element.55), channel_id=1, source_target_pairs={{0,8},{1,9},{2,10},{3,11},{4,12},{5,13},{6,14},{7,15},{8,0},{9,1},... | collective-permute-start | bytes 196616 | tf_op jit(solution)/shard_map/ppermute | solution.py:267
  49.0 5.5 %collective-permute-start.19 = (bf16[128,256]{1,0:T(8,128)(2,1)S(1)}, bf16[128,256]{1,0:T(8,128)(2,1)S(1)}, u32[]{:S(2)}, u32[]{:S(2)}) collective-permute-start(bf16[128,256]{1,0:T(8,128)(2,1)S(1)} %get-tuple-element.56), channel_id=1, source_target_pairs={{0,16},{1,17},{2,18},{3,19},{4,20},{5,21},{6,22},{7,23},{8,24},{9,... | collective-permute-start | bytes 196616 | tf_op jit(solution)/shard_map/ppermute | solution.py:267
  54.6 1.4 %collective-permute-start.20 = (f32[128,256]{1,0:T(8,128)S(1)}, f32[128,256]{1,0:T(8,128)S(1)}, u32[]{:S(2)}, u32[]{:S(2)}) collective-permute-start(f32[128,256]{1,0:T(8,128)S(1)} %convert_add_fusion.result), channel_id=1, source_target_pairs={{0,1},{1,0},{2,3},{3,2},{4,5},{5,4},{6,7},{7,6},{8,9},{9,8},{10,11... | collective-permute-start | bytes 393224 | tf_op jit(solution)/shard_map/ppermute | solution.py:272

commit v6 on v4

--- a/solution.py
+++ b/solution.py
@@ -303,7 +303,7 @@
     y8 = second(p8)
     y12 = second(p12)
 
-    kernel_other = swap(after(kernel, x12))
+    kernel_other = swap(after(kernel, x0))
     order = (1, 2, 0, 3)
     tiles = turn_tiles(
         ids(*[r ^ (near * a) ^ (far * b) ^ (4 * k) for a in (1, 0) for b in (1, 0) for k in order]),

time: 56.9 us -> 57.1 us (level)
  starting transfers between devices: 24.7 us -> 25.3 us
  transfers between devices with their start and end apart: 21 -> 21, of which waited for: 17 -> 15; matrix products, arithmetic and copies ran while one was open for 0% -> 0% of each run, Pallas kernels for 9% -> 9%
where the time goes in v6:
time: 57.1 us; the launch traced here: 57 us
  starting transfers between devices  25.3 us (44%)
  waiting for transfers between devices  23.3 us (41%)
  Pallas kernels  7.03 us (12%)
  local copies, waits for them, and re-layouts  1.14 us (2%)
    ppermute x16, starting transfers between devices, send(): return lax.ppermute(a, ('row', 'col'), pairs)  24.7 us
    ppermute x16, waiting for transfers between devices, send(): return lax.ppermute(a, ('row', 'col'), pairs)  20.7 us
    ppermute x5, waiting for transfers between devices, box_body(): swap = lambda a: lax.ppermute(a, 'col', [(0, 1), (1, 0)])  2.56 us
    pallas_call x1, Pallas kernels, apply_early(): pl.pallas_call(functools.partial(early_kernel, slots, tuple(later), n //...  2.44 us
    pallas_call x3, Pallas kernels, split_spins(): pl.pallas_call(split_kernel, out_shape=[jax.ShapeDtypeStruct((p, i), orbi...  1.15 us
  transfers between devices with their start and end apart: 21, of which 15 were waited for; matrix products, arithmetic and copies ran while one was open for 0% of the time, Pallas kernels for 9%

profile of v6, /device:TPU:0, one launch (start us, length us, event | category | flops | bytes accessed | tf_op | source)
XLA Modules:
  0.0 57.0 jit_solution(7568818103839190762)
XLA Ops:
  0.0 4.0 %collective-permute-start = (bf16[128,2,256]{2,1,0:T(2,128)(2,1)}, bf16[128,2,256]{2,1,0:T(2,128)(2,1)S(1)}, u32[]{:S(2)}, u32[]{:S(2)}) collective-permute-start(bf16[128,2,256]{2,1,0:T(2,128)(2,1)} %orbitals.1), channel_id=1, source_target_pairs={{0,16},{1,17},{2,18},{3,19},{4,20},{5,21},{6,22},{7,23},{8,24},{9,... | collective-permute-start | bytes 393224 | tf_op jit(solution)/shard_map/ppermute | solution.py:267
  5.5 1.2 %collective-permute-done.1 = bf16[128,256]{1,0:T(8,128)(2,1)S(1)} collective-permute-done((bf16[128,256]{1,0:T(8,128)(2,1)S(1)}, bf16[128,256]{1,0:T(8,128)(2,1)S(1)}, u32[]{:S(2)}, u32[]{:S(2)}) %collective-permute-start.1) | collective-permute-done | bytes 65568 | tf_op jit(solution)/shard_map/ppermute | solution.py:272
  6.7 1.6 %collective-permute-start.2 = (bf16[256,256]{1,0:T(8,128)(2,1)S(1)}, bf16[256,256]{1,0:T(8,128)(2,1)S(1)}, u32[]{:S(2)}, u32[]{:S(2)}) collective-permute-start(bf16[256,256]{1,0:T(8,128)(2,1)S(1)} %constant_dynamic-update-slice_fusion.refs_0_), channel_id=1, source_target_pairs={{0,2},{1,5},{2,0},{3,7},{4,6},{5,1},{6,4},{7,3},{8,10},{9,13},{10,... | collective-permute-start | bytes 393224 | tf_op jit(solution)/shard_map/ppermute | solution.py:267
  8.3 2.3 %collective-permute-done.orbitals = bf16[128,2,256]{2,1,0:T(2,128)(2,1)S(1)} collective-permute-done((bf16[128,2,256]{2,1,0:T(2,128)(2,1)}, bf16[128,2,256]{2,1,0:T(2,128)(2,1)S(1)}, u32[]{:S(2)}, u32[]{:S(2)}) %collective-permute-start) | collective-permute-done | bytes 131104 | tf_op jit(solution)/shard_map/ppermute | solution.py:267
  11.8 1.6 %collective-permute-start.3 = (bf16[128,2,256]{2,1,0:T(2,128)(2,1)S(1)}, bf16[128,2,256]{2,1,0:T(2,128)(2,1)S(1)}, u32[]{:S(2)}, u32[]{:S(2)}) collective-permute-start(bf16[128,2,256]{2,1,0:T(2,128)(2,1)S(1)} %collective-permute-done.orbitals), channel_id=1, source_target_pairs={{0,8},{1,9},{2,10},{3,11},{4,12},{5,13},{6,14},{7,15},{8,0},{9,1},... | collective-permute-start | bytes 393224 | tf_op jit(solution)/shard_map/ppermute | solution.py:267
  13.7 1.6 %collective-permute-start.5 = (bf16[512,256]{1,0:T(8,128)(2,1)S(1)}, bf16[512,256]{1,0:T(8,128)(2,1)S(1)}, u32[]{:S(2)}, u32[]{:S(2)}) collective-permute-start(bf16[512,256]{1,0:T(8,128)(2,1)S(1)} %shard_map.39.refs_0_), channel_id=1, source_target_pairs={{0,4},{1,3},{2,6},{3,1},{4,0},{5,7},{6,2},{7,5},{8,12},{9,11},{10,... | collective-permute-start | bytes 786440 | tf_op jit(solution)/shard_map/ppermute | solution.py:267
  15.3 1.5 %collective-permute-done.3.orbitals = bf16[128,2,256]{2,1,0:T(2,128)(2,1)S(1)} collective-permute-done((bf16[128,2,256]{2,1,0:T(2,128)(2,1)S(1)}, bf16[128,2,256]{2,1,0:T(2,128)(2,1)S(1)}, u32[]{:S(2)}, u32[]{:S(2)}) %collective-permute-start.3) | collective-permute-done | bytes 131104 | tf_op jit(solution)/shard_map/ppermute | solution.py:267
  17.3 1.6 %collective-permute-start.9 = (bf16[256,256]{1,0:T(8,128)(2,1)S(1)}, bf16[256,256]{1,0:T(8,128)(2,1)S(1)}, u32[]{:S(2)}, u32[]{:S(2)}) collective-permute-start(bf16[256,256]{1,0:T(8,128)(2,1)S(1)} %shard_map.44.refs_0_), channel_id=1, source_target_pairs={{0,2},{1,5},{2,0},{3,7},{4,6},{5,1},{6,4},{7,3},{8,10},{9,13},{10,... | collective-permute-start | bytes 393224 | tf_op jit(solution)/shard_map/ppermute | solution.py:267
  20.8 1.5 %collective-permute-start.6 = (bf16[256,256]{1,0:T(8,128)(2,1)S(1)}, bf16[256,256]{1,0:T(8,128)(2,1)S(1)}, u32[]{:S(2)}, u32[]{:S(2)}) collective-permute-start(bf16[256,256]{1,0:T(8,128)(2,1)S(1)} %shard_map.41.refs_0_), channel_id=1, source_target_pairs={{0,2},{1,5},{2,0},{3,7},{4,6},{5,1},{6,4},{7,3},{8,10},{9,13},{10,... | collective-permute-start | bytes 393224 | tf_op jit(solution)/shard_map/ppermute | solution.py:267
  22.4 1.6 %collective-permute-start.10 = (bf16[512,256]{1,0:T(8,128)(2,1)S(1)}, bf16[512,256]{1,0:T(8,128)(2,1)S(1)}, u32[]{:S(2)}, u32[]{:S(2)}) collective-permute-start(bf16[512,256]{1,0:T(8,128)(2,1)S(1)} %shard_map.45.refs_2_), channel_id=1, source_target_pairs={{0,4},{1,3},{2,6},{3,1},{4,0},{5,7},{6,2},{7,5},{8,12},{9,11},{10,... | collective-permute-start | bytes 786440 | tf_op jit(solution)/shard_map/ppermute | solution.py:267
  24.0 2.9 %collective-permute-done.6.refs_1_ = bf16[256,256]{1,0:T(8,128)(2,1)S(1)} collective-permute-done((bf16[256,256]{1,0:T(8,128)(2,1)S(1)}, bf16[256,256]{1,0:T(8,128)(2,1)S(1)}, u32[]{:S(2)}, u32[]{:S(2)}) %collective-permute-start.6) | collective-permute-done | bytes 131104 | tf_op jit(solution)/shard_map/ppermute | solution.py:267
  26.9 1.4 %collective-permute-start.11 = (bf16[512,256]{1,0:T(8,128)(2,1)S(1)}, bf16[512,256]{1,0:T(8,128)(2,1)S(1)}, u32[]{:S(2)}, u32[]{:S(2)}) collective-permute-start(bf16[512,256]{1,0:T(8,128)(2,1)S(1)} %shard_map.46.refs_4_), channel_id=1, source_target_pairs={{0,4},{1,3},{2,6},{3,1},{4,0},{5,7},{6,2},{7,5},{8,12},{9,11},{10,... | collective-permute-start | bytes 786440 | tf_op jit(solution)/shard_map/ppermute | solution.py:267
  29.2 2.4 %shard_map.47 = (f32[256,256]{1,0:T(8,128)S(1)}, bf16[256,1536]{1,0:T(8,128)(2,1)S(1)}) custom-call(s32[8]{0:T(128)S(1)} %stack.107.ids, bf16[256,256]{1,0:T(8,128)(2,1)S(1)} %maximum_select_fusion.rows, bf16[256,2048]{1,0:T(8,128)(2,1)S(1)} %copy-done.2, bf16[256,2048]{1,0:T(8,128)(2,1)S(1)} %collective-permute-done.7.kernel_other, ...), custom_call_target="tpu_custom_call" | custom-call | flops 60000002048 | bytes 1000000 | tf_op jit(solution)/shard_map/pallas_call | solution.py:160
  31.6 1.7 %collective-permute-done.11.refs_0_ = bf16[512,256]{1,0:T(8,128)(2,1)S(1)} collective-permute-done((bf16[512,256]{1,0:T(8,128)(2,1)S(1)}, bf16[512,256]{1,0:T(8,128)(2,1)S(1)}, u32[]{:S(2)}, u32[]{:S(2)}) %collective-permute-start.11) | collective-permute-done | bytes 262176 | tf_op jit(solution)/shard_map/ppermute | solution.py:267
  33.6 1.0 %shard_map.48 = (bf16[256,256]{1,0:T(8,128)(2,1)S(1)}, bf16[512,256]{1,0:T(8,128)(2,1)S(1)}) custom-call(bf16[256,256]{1,0:T(8,128)(2,1)S(1)} %maximum_select_fusion.rows, bf16[256,1536]{1,0:T(8,128)(2,1)S(1)} %get-tuple-element.45.packed, f32[256,256]{1,0:T(8,128)S(1)} %get-tuple-element.46.acc, bf16[2048,256]{1,0:T(8,128)(2,1)S(1)} %shard_map.43.tiles, ...), custom_call_target="tpu_custom_call" | custom-call | flops 1000000000 | bytes 1000000 | tf_op jit(solution)/shard_map/pallas_call | solution.py:174
  34.7 1.6 %collective-permute-start.14 = (bf16[512,256]{1,0:T(8,128)(2,1)S(1)}, bf16[512,256]{1,0:T(8,128)(2,1)S(1)}, u32[]{:S(2)}, u32[]{:S(2)}) collective-permute-start(bf16[512,256]{1,0:T(8,128)(2,1)S(1)} %get-tuple-element.50), channel_id=1, source_target_pairs={{0,2},{1,5},{2,0},{3,7},{4,6},{5,1},{6,4},{7,3},{8,10},{9,13},{10,... | collective-permute-start | bytes 786440 | tf_op jit(solution)/shard_map/ppermute | solution.py:267
  37.3 3.8 %collective-permute-done.14.got = bf16[512,256]{1,0:T(8,128)(2,1)S(1)} collective-permute-done((bf16[512,256]{1,0:T(8,128)(2,1)S(1)}, bf16[512,256]{1,0:T(8,128)(2,1)S(1)}, u32[]{:S(2)}, u32[]{:S(2)}) %collective-permute-start.14) | collective-permute-done | bytes 262176 | tf_op jit(solution)/shard_map/ppermute | solution.py:267
  41.1 1.6 %collective-permute-start.15 = (bf16[256,256]{1,0:T(8,128)(2,1)S(1)}, bf16[256,256]{1,0:T(8,128)(2,1)S(1)}, u32[]{:S(2)}, u32[]{:S(2)}) collective-permute-start(bf16[256,256]{1,0:T(8,128)(2,1)S(1)} %get-tuple-element.51), channel_id=1, source_target_pairs={{0,4},{1,3},{2,6},{3,1},{4,0},{5,7},{6,2},{7,5},{8,12},{9,11},{10,... | collective-permute-start | bytes 393224 | tf_op jit(solution)/shard_map/ppermute | solution.py:267
  43.2 2.9 %collective-permute-done.13.got = bf16[512,256]{1,0:T(8,128)(2,1)S(1)} collective-permute-done((bf16[512,256]{1,0:T(8,128)(2,1)S(1)}, bf16[512,256]{1,0:T(8,128)(2,1)S(1)}, u32[]{:S(2)}, u32[]{:S(2)}) %collective-permute-start.13) | collective-permute-done | bytes 262176 | tf_op jit(solution)/shard_map/ppermute | solution.py:267
  46.2 3.0 %collective-permute-start.16 = (bf16[128,256]{1,0:T(8,128)(2,1)S(1)}, bf16[128,256]{1,0:T(8,128)(2,1)S(1)}, u32[]{:S(2)}, u32[]{:S(2)}) collective-permute-start(bf16[128,256]{1,0:T(8,128)(2,1)S(1)} %get-tuple-element.53), channel_id=1, source_target_pairs={{0,24},{1,25},{2,26},{3,27},{4,28},{5,29},{6,30},{7,31},{8,16},{9,... | collective-permute-start | bytes 196616 | tf_op jit(solution)/shard_map/ppermute | solution.py:267
  49.3 2.0 %collective-permute-start.19 = (bf16[128,256]{1,0:T(8,128)(2,1)S(1)}, bf16[128,256]{1,0:T(8,128)(2,1)S(1)}, u32[]{:S(2)}, u32[]{:S(2)}) collective-permute-start(bf16[128,256]{1,0:T(8,128)(2,1)S(1)} %get-tuple-element.56), channel_id=1, source_target_pairs={{0,16},{1,17},{2,18},{3,19},{4,20},{5,21},{6,22},{7,23},{8,24},{9,... | collective-permute-start | bytes 196616 | tf_op jit(solution)/shard_map/ppermute | solution.py:267
  51.3 1.1 %collective-permute-done.16 = bf16[128,256]{1,0:T(8,128)(2,1)S(1)} collective-permute-done((bf16[128,256]{1,0:T(8,128)(2,1)S(1)}, bf16[128,256]{1,0:T(8,128)(2,1)S(1)}, u32[]{:S(2)}, u32[]{:S(2)}) %collective-permute-start.16) | collective-permute-done | bytes 65568 | tf_op jit(solution)/shard_map/ppermute | solution.py:267
  52.4 1.4 %collective-permute-done.18 = bf16[128,256]{1,0:T(8,128)(2,1)S(1)} collective-permute-done((bf16[128,256]{1,0:T(8,128)(2,1)S(1)}, bf16[128,256]{1,0:T(8,128)(2,1)S(1)}, u32[]{:S(2)}, u32[]{:S(2)}) %collective-permute-start.18) | collective-permute-done | bytes 65568 | tf_op jit(solution)/shard_map/ppermute | solution.py:267
  54.8 1.3 %collective-permute-done.20.partner = f32[128,256]{1,0:T(8,128)S(1)} collective-permute-done((f32[128,256]{1,0:T(8,128)S(1)}, f32[128,256]{1,0:T(8,128)S(1)}, u32[]{:S(2)}, u32[]{:S(2)}) %collective-permute-start.20) | collective-permute-done | bytes 131104 | tf_op jit(solution)/shard_map/ppermute | solution.py:272
  (48 shorter events, 10.3 us)
Async XLA Ops:
  0.0 10.5 %collective-permute-start = (bf16[128,2,256]{2,1,0:T(2,128)(2,1)}, bf16[128,2,256]{2,1,0:T(2,128)(2,1)S(1)}, u32[]{:S(2)}, u32[]{:S(2)}) collective-permute-start(bf16[128,2,256]{2,1,0:T(2,128)(2,1)} %orbitals.1), channel_id=1, source_target_pairs={{0,16},{1,17},{2,18},{3,19},{4,20},{5,21},{6,22},{7,23},{8,24},{9,... | collective-permute-start | bytes 393224 | tf_op jit(solution)/shard_map/ppermute | solution.py:267
  4.0 0.9 %copy-start.1 = (bf16[128,2,256]{2,1,0:T(2,128)(2,1)S(1)}, bf16[128,2,256]{2,1,0:T(2,128)(2,1)}, u32[]{:S(2)}) copy-start(bf16[128,2,256]{2,1,0:T(2,128)(2,1)} %orbitals.1) | copy-start | bytes 393220
  5.4 1.3 %collective-permute-start.1 = (bf16[128,256]{1,0:T(8,128)(2,1)S(1)}, bf16[128,256]{1,0:T(8,128)(2,1)S(1)}, u32[]{:S(2)}, u32[]{:S(2)}) collective-permute-start(bf16[128,256]{1,0:T(8,128)(2,1)S(1)} %get-tuple-element.32), channel_id=1, source_target_pairs={{0,1},{1,0},{2,3},{3,2},{4,5},{5,4},{6,7},{7,6},{8,9},{9,8},{10,11... | collective-permute-start | bytes 196616 | tf_op jit(solution)/shard_map/ppermute | solution.py:272
  6.7 5.0 %collective-permute-start.2 = (bf16[256,256]{1,0:T(8,128)(2,1)S(1)}, bf16[256,256]{1,0:T(8,128)(2,1)S(1)}, u32[]{:S(2)}, u32[]{:S(2)}) collective-permute-start(bf16[256,256]{1,0:T(8,128)(2,1)S(1)} %constant_dynamic-update-slice_fusion.refs_0_), channel_id=1, source_target_pairs={{0,2},{1,5},{2,0},{3,7},{4,6},{5,1},{6,4},{7,3},{8,10},{9,13},{10,... | collective-permute-start | bytes 393224 | tf_op jit(solution)/shard_map/ppermute | solution.py:267
  11.8 5.0 %collective-permute-start.3 = (bf16[128,2,256]{2,1,0:T(2,128)(2,1)S(1)}, bf16[128,2,256]{2,1,0:T(2,128)(2,1)S(1)}, u32[]{:S(2)}, u32[]{:S(2)}) collective-permute-start(bf16[128,2,256]{2,1,0:T(2,128)(2,1)S(1)} %collective-permute-done.orbitals), channel_id=1, source_target_pairs={{0,8},{1,9},{2,10},{3,11},{4,12},{5,13},{6,14},{7,15},{8,0},{9,1},... | collective-permute-start | bytes 393224 | tf_op jit(solution)/shard_map/ppermute | solution.py:267
  13.6 3.7 %collective-permute-start.8 = (bf16[128,256]{1,0:T(8,128)(2,1)S(1)}, bf16[128,256]{1,0:T(8,128)(2,1)S(1)}, u32[]{:S(2)}, u32[]{:S(2)}) collective-permute-start(bf16[128,256]{1,0:T(8,128)(2,1)S(1)} %get-tuple-element.43), channel_id=1, source_target_pairs={{0,1},{1,0},{2,3},{3,2},{4,5},{5,4},{6,7},{7,6},{8,9},{9,8},{10,11... | collective-permute-start | bytes 196616 | tf_op jit(solution)/shard_map/ppermute | solution.py:272
  13.7 6.4 %collective-permute-start.5 = (bf16[512,256]{1,0:T(8,128)(2,1)S(1)}, bf16[512,256]{1,0:T(8,128)(2,1)S(1)}, u32[]{:S(2)}, u32[]{:S(2)}) collective-permute-start(bf16[512,256]{1,0:T(8,128)(2,1)S(1)} %shard_map.39.refs_0_), channel_id=1, source_target_pairs={{0,4},{1,3},{2,6},{3,1},{4,0},{5,7},{6,2},{7,5},{8,12},{9,11},{10,... | collective-permute-start | bytes 786440 | tf_op jit(solution)/shard_map/ppermute | solution.py:267
  17.2 1.7 %copy-start.2 = (bf16[256,2048]{1,0:T(8,128)(2,1)S(1)}, bf16[256,2048]{1,0:T(8,128)(2,1)}, u32[]{:S(2)}) copy-start(bf16[256,2048]{1,0:T(8,128)(2,1)} %kernel.1) | copy-start | bytes 3145732
  17.2 1.9 %collective-permute-start.4 = (bf16[128,256]{1,0:T(8,128)(2,1)S(1)}, bf16[128,256]{1,0:T(8,128)(2,1)S(1)}, u32[]{:S(2)}, u32[]{:S(2)}) collective-permute-start(bf16[128,256]{1,0:T(8,128)(2,1)S(1)} %get-tuple-element.38), channel_id=1, source_target_pairs={{0,1},{1,0},{2,3},{3,2},{4,5},{5,4},{6,7},{7,6},{8,9},{9,8},{10,11... | collective-permute-start | bytes 196616 | tf_op jit(solution)/shard_map/ppermute | solution.py:272
  17.3 5.0 %collective-permute-start.9 = (bf16[256,256]{1,0:T(8,128)(2,1)S(1)}, bf16[256,256]{1,0:T(8,128)(2,1)S(1)}, u32[]{:S(2)}, u32[]{:S(2)}) collective-permute-start(bf16[256,256]{1,0:T(8,128)(2,1)S(1)} %shard_map.44.refs_0_), channel_id=1, source_target_pairs={{0,2},{1,5},{2,0},{3,7},{4,6},{5,1},{6,4},{7,3},{8,10},{9,13},{10,... | collective-permute-start | bytes 393224 | tf_op jit(solution)/shard_map/ppermute | solution.py:267
  18.9 10.3 %collective-permute-start.7 = (bf16[256,2048]{1,0:T(8,128)(2,1)S(1)}, bf16[256,2048]{1,0:T(8,128)(2,1)S(1)}, u32[]{:S(2)}, u32[]{:S(2)}) collective-permute-start(bf16[256,2048]{1,0:T(8,128)(2,1)S(1)} %copy-done.2), channel_id=1, source_target_pairs={{0,1},{1,0},{2,3},{3,2},{4,5},{5,4},{6,7},{7,6},{8,9},{9,8},{10,11... | collective-permute-start | bytes 3145736 | tf_op jit(solution)/shard_map/ppermute | solution.py:272
  20.2 13.5 %collective-permute-start.12 = (bf16[1024,256]{1,0:T(8,128)(2,1)S(1)}, bf16[1024,256]{1,0:T(8,128)(2,1)S(1)}, u32[]{:S(2)}, u32[]{:S(2)}) collective-permute-start(bf16[1024,256]{1,0:T(8,128)(2,1)S(1)} %shard_map.42), channel_id=1, source_target_pairs={{0,8},{1,9},{2,10},{3,11},{4,12},{5,13},{6,14},{7,15},{8,0},{9,1},... | collective-permute-start | bytes 1572872 | tf_op jit(solution)/shard_map/ppermute | solution.py:267
  20.8 6.1 %collective-permute-start.6 = (bf16[256,256]{1,0:T(8,128)(2,1)S(1)}, bf16[256,256]{1,0:T(8,128)(2,1)S(1)}, u32[]{:S(2)}, u32[]{:S(2)}) collective-permute-start(bf16[256,256]{1,0:T(8,128)(2,1)S(1)} %shard_map.41.refs_0_), channel_id=1, source_target_pairs={{0,2},{1,5},{2,0},{3,7},{4,6},{5,1},{6,4},{7,3},{8,10},{9,13},{10,... | collective-permute-start | bytes 393224 | tf_op jit(solution)/shard_map/ppermute | solution.py:267
  22.4 5.9 %copy-start = (bf16[256,2048]{1,0:T(8,128)(2,1)S(1)}, bf16[256,2048]{1,0:T(8,128)(2,1)}, u32[]{:S(2)}) copy-start(bf16[256,2048]{1,0:T(8,128)(2,1)} %basis) | copy-start | bytes 3145732
  22.4 6.8 %collective-permute-start.10 = (bf16[512,256]{1,0:T(8,128)(2,1)S(1)}, bf16[512,256]{1,0:T(8,128)(2,1)S(1)}, u32[]{:S(2)}, u32[]{:S(2)}) collective-permute-start(bf16[512,256]{1,0:T(8,128)(2,1)S(1)} %shard_map.45.refs_2_), channel_id=1, source_target_pairs={{0,4},{1,3},{2,6},{3,1},{4,0},{5,7},{6,2},{7,5},{8,12},{9,11},{10,... | collective-permute-start | bytes 786440 | tf_op jit(solution)/shard_map/ppermute | solution.py:267
  26.9 6.4 %collective-permute-start.11 = (bf16[512,256]{1,0:T(8,128)(2,1)S(1)}, bf16[512,256]{1,0:T(8,128)(2,1)S(1)}, u32[]{:S(2)}, u32[]{:S(2)}) collective-permute-start(bf16[512,256]{1,0:T(8,128)(2,1)S(1)} %shard_map.46.refs_4_), channel_id=1, source_target_pairs={{0,4},{1,3},{2,6},{3,1},{4,0},{5,7},{6,2},{7,5},{8,12},{9,11},{10,... | collective-permute-start | bytes 786440 | tf_op jit(solution)/shard_map/ppermute | solution.py:267
  34.7 6.4 %collective-permute-start.14 = (bf16[512,256]{1,0:T(8,128)(2,1)S(1)}, bf16[512,256]{1,0:T(8,128)(2,1)S(1)}, u32[]{:S(2)}, u32[]{:S(2)}) collective-permute-start(bf16[512,256]{1,0:T(8,128)(2,1)S(1)} %get-tuple-element.50), channel_id=1, source_target_pairs={{0,2},{1,5},{2,0},{3,7},{4,6},{5,1},{6,4},{7,3},{8,10},{9,13},{10,... | collective-permute-start | bytes 786440 | tf_op jit(solution)/shard_map/ppermute | solution.py:267
  36.4 9.7 %collective-permute-start.13 = (bf16[512,256]{1,0:T(8,128)(2,1)S(1)}, bf16[512,256]{1,0:T(8,128)(2,1)S(1)}, u32[]{:S(2)}, u32[]{:S(2)}) collective-permute-start(bf16[512,256]{1,0:T(8,128)(2,1)S(1)} %shard_map.50), channel_id=1, source_target_pairs={{0,2},{1,5},{2,0},{3,7},{4,6},{5,1},{6,4},{7,3},{8,10},{9,13},{10,... | collective-permute-start | bytes 786440 | tf_op jit(solution)/shard_map/ppermute | solution.py:267
  41.1 5.0 %collective-permute-start.15 = (bf16[256,256]{1,0:T(8,128)(2,1)S(1)}, bf16[256,256]{1,0:T(8,128)(2,1)S(1)}, u32[]{:S(2)}, u32[]{:S(2)}) collective-permute-start(bf16[256,256]{1,0:T(8,128)(2,1)S(1)} %get-tuple-element.51), channel_id=1, source_target_pairs={{0,4},{1,3},{2,6},{3,1},{4,0},{5,7},{6,2},{7,5},{8,12},{9,11},{10,... | collective-permute-start | bytes 393224 | tf_op jit(solution)/shard_map/ppermute | solution.py:267
  42.7 6.5 %collective-permute-start.17 = (bf16[256,256]{1,0:T(8,128)(2,1)S(1)}, bf16[256,256]{1,0:T(8,128)(2,1)S(1)}, u32[]{:S(2)}, u32[]{:S(2)}) collective-permute-start(bf16[256,256]{1,0:T(8,128)(2,1)S(1)} %get-tuple-element.54), channel_id=1, source_target_pairs={{0,4},{1,3},{2,6},{3,1},{4,0},{5,7},{6,2},{7,5},{8,12},{9,11},{10,... | collective-permute-start | bytes 393224 | tf_op jit(solution)/shard_map/ppermute | solution.py:267
  46.2 6.2 %collective-permute-start.16 = (bf16[128,256]{1,0:T(8,128)(2,1)S(1)}, bf16[128,256]{1,0:T(8,128)(2,1)S(1)}, u32[]{:S(2)}, u32[]{:S(2)}) collective-permute-start(bf16[128,256]{1,0:T(8,128)(2,1)S(1)} %get-tuple-element.53), channel_id=1, source_target_pairs={{0,24},{1,25},{2,26},{3,27},{4,28},{5,29},{6,30},{7,31},{8,16},{9,... | collective-permute-start | bytes 196616 | tf_op jit(solution)/shard_map/ppermute | solution.py:267
  49.2 4.5 %collective-permute-start.18 = (bf16[128,256]{1,0:T(8,128)(2,1)S(1)}, bf16[128,256]{1,0:T(8,128)(2,1)S(1)}, u32[]{:S(2)}, u32[]{:S(2)}) collective-permute-start(bf16[128,256]{1,0:T(8,128)(2,1)S(1)} %get-tuple-element.55), channel_id=1, source_target_pairs={{0,8},{1,9},{2,10},{3,11},{4,12},{5,13},{6,14},{7,15},{8,0},{9,1},... | collective-permute-start | bytes 196616 | tf_op jit(solution)/shard_map/ppermute | solution.py:267
  49.3 5.4 %collective-permute-start.19 = (bf16[128,256]{1,0:T(8,128)(2,1)S(1)}, bf16[128,256]{1,0:T(8,128)(2,1)S(1)}, u32[]{:S(2)}, u32[]{:S(2)}) collective-permute-start(bf16[128,256]{1,0:T(8,128)(2,1)S(1)} %get-tuple-element.56), channel_id=1, source_target_pairs={{0,16},{1,17},{2,18},{3,19},{4,20},{5,21},{6,22},{7,23},{8,24},{9,... | collective-permute-start | bytes 196616 | tf_op jit(solution)/shard_map/ppermute | solution.py:267
  54.7 1.4 %collective-permute-start.20 = (f32[128,256]{1,0:T(8,128)S(1)}, f32[128,256]{1,0:T(8,128)S(1)}, u32[]{:S(2)}, u32[]{:S(2)}) collective-permute-start(f32[128,256]{1,0:T(8,128)S(1)} %convert_add_fusion.result), channel_id=1, source_target_pairs={{0,1},{1,0},{2,3},{3,2},{4,5},{5,4},{6,7},{7,6},{8,9},{9,8},{10,11... | collective-permute-start | bytes 393224 | tf_op jit(solution)/shard_map/ppermute | solution.py:272
